TPU v7x, 32 devices: a whole 2x2x4 slice. The times are simulated.
32 devices in a mesh: groups: 2 (over y), expert: 4 (over z), tensor: 4 (over x, core).
Axes of the slice: x: 2, y: 2, z: 4, core: 2. Of those that a mesh axis runs over, the one named last changes fastest.
Arguments:
- queries: bfloat16 [512, 36864], P(('groups', 'expert'), 'tensor'), parts along dimension 0, may hold values from -24 to 24
- own_latent: bfloat16 [512, 576], P(('groups', 'expert')), parts along dimension 0, may hold values from -6 to 6
- residual_in: bfloat16 [512, 3584], P(('groups', 'expert'), 'tensor'), parts along dimension 0, may hold values from -3 to 3
- row_dest: int32 [512, 1], P(('groups', 'expert')), parts along dimension 0, may hold values from 0 to 3; in each aligned block of 64 rows (0 to 63, 64 to 127, ...) at most 32 rows name the same one
- prompt_cache: bfloat16 [2048, 576], P(('groups', 'expert')), parts along dimension 0, may hold values from -6 to 6
- value_up: bfloat16 [64, 512, 128], P('tensor'), may hold values from -0.5 to 0.5
- out_proj: bfloat16 [8192, 3584], P('tensor', 'expert'), may hold values from -0.125 to 0.125
- norm_gain: bfloat16 [3584], P('tensor'), may hold values from 0.25 to 1.75
- gate_weight: bfloat16 [4, 3584, 1024], P('expert', 'tensor'), may hold values from -0.09375 to 0.09375
- up_weight: bfloat16 [4, 3584, 1024], P('expert', 'tensor'), may hold values from -0.09375 to 0.09375
- down_weight: bfloat16 [4, 1024, 3584], P('expert', None, 'tensor'), may hold values from -0.375 to 0.375
- expert_ids: int32 [512, 2], P(('groups', 'expert')), parts along dimension 0, may hold values from 0 to 3, all different within a row; in each aligned block of 64 rows (0 to 63, 64 to 127, ...) at most 48 rows name the same one
- route_weight: float32 [512, 2], P(('groups', 'expert')), parts along dimension 0, may hold values from 0.05 to 0.6
Outputs:
- scored: bfloat16 [512, 3584], P(('groups', 'expert'), 'tensor'), parts along dimension 0
There are 2 independent parts, one for each index of `groups`. A program takes and returns all parts, laid end to end along the dimension named above; an argument that names none is the same for every part. Nothing has to cross between parts.
Inputs may be any that keep to these rules, and one draw needn't show every extreme that they name: `row_dest`: in each aligned block of 64 rows no sequence is named by more than 32 rows, and some block reaches 32. `expert_ids`: each row names 2 different experts; in each aligned block of 64 rows no expert is named by more than 48 rows, and some block reaches 48.
All inputs are finite; a program needn't handle non-finite values.
Results may differ from a plain program's by a relative error of at most 0.017.
Values may be sent and summed in bfloat16 or wider, within the bound.
No kernel may reach another device: no remote copies, remote signals or barrier semaphores. Data moves between devices by JAX's collectives and lax.ppermute only.
A program may use at most 128 MiB of HBM per device.

v0:
```python
import jax
import jax.numpy as jnp
from jax import lax
from jax.sharding import PartitionSpec as P


def slot_table(targets, count, capacity):
    onehot = (targets[:, None] == jnp.arange(count, dtype=jnp.int32)[None, :]).astype(jnp.int32)
    before = jnp.cumsum(onehot, axis=0) - onehot
    rank = jnp.sum(before * onehot, axis=1)
    return targets * capacity + rank


def local(
    queries,
    own_latent,
    residual_in,
    row_dest,
    prompt_cache,
    value_up,
    out_proj,
    norm_gain,
    gate_weight,
    up_weight,
    down_weight,
    expert_ids,
    route_weight,
):
    shards = lax.axis_size("expert")
    tok_rows = residual_in.shape[0]
    width_part = residual_in.shape[1]
    heads_here = value_up.shape[0]
    latent = value_up.shape[1]
    vhead = value_up.shape[2]
    key_width = own_latent.shape[1]
    scale = (vhead + key_width - latent) ** (-0.5)
    capacity = max(2, 2 * tok_rows // shards)
    total_slots = shards * capacity
    slot = slot_table(row_dest[:, 0], shards, capacity)
    send_query = jnp.zeros((total_slots, queries.shape[1]), queries.dtype).at[slot].set(queries)
    send_key = jnp.zeros((total_slots, key_width), own_latent.dtype).at[slot].set(own_latent)
    recv_query, recv_key = (
        lax.all_to_all(send_query, "expert", split_axis=0, concat_axis=0, tiled=True),
        lax.all_to_all(send_key, "expert", split_axis=0, concat_axis=0, tiled=True),
    )
    query_heads = recv_query.reshape(total_slots, heads_here, key_width)
    scores = (
        jnp.einsum("shc,pc->shp", query_heads, prompt_cache, preferred_element_type=jnp.float32)
        * scale
    )
    own_score = (
        jnp.einsum("shc,sc->sh", query_heads, recv_key, preferred_element_type=jnp.float32) * scale
    )
    top = jnp.maximum(jnp.max(scores, axis=2), own_score)
    expo = jnp.exp(scores - top[:, :, None])
    own_e = jnp.exp(own_score - top)
    total = jnp.sum(expo, axis=2) + own_e
    probs = (expo / total[:, :, None]).astype(jnp.bfloat16)
    own_p = (own_e / total).astype(jnp.bfloat16)
    latent_out = jnp.einsum(
        "shp,pl->shl", probs, prompt_cache[:, :latent], preferred_element_type=jnp.float32
    )
    latent_out = latent_out + own_p.astype(jnp.float32)[:, :, None] * recv_key[
        :, None, :latent
    ].astype(jnp.float32)
    latent_out = latent_out.astype(jnp.bfloat16)
    head_out = jnp.einsum(
        "shl,hlv->shv", latent_out, value_up, preferred_element_type=jnp.float32
    ).astype(jnp.bfloat16)
    head_out = head_out.reshape(total_slots, heads_here * vhead)
    returned_heads = lax.all_to_all(head_out, "expert", split_axis=0, concat_axis=0, tiled=True)
    attn_rows = returned_heads[slot]
    partial_value = jnp.dot(
        attn_rows,
        lax.all_gather(out_proj, "expert", axis=1, tiled=True),
        preferred_element_type=jnp.float32,
    )
    attn_part = lax.psum_scatter(
        partial_value.astype(jnp.bfloat16), "tensor", scatter_dimension=1, tiled=True
    ).astype(jnp.float32)
    resid = residual_in.astype(jnp.float32) + attn_part
    squares = lax.psum(jnp.sum(resid * resid, axis=1), "tensor")
    full_width = width_part * lax.axis_size("tensor")
    normed = (
        resid * lax.rsqrt(squares / full_width + 1e-06)[:, None] * norm_gain.astype(jnp.float32)
    ).astype(jnp.bfloat16)
    topk = expert_ids.shape[1]
    cap_x = 3 * topk * tok_rows // (2 * shards)
    assign_slot = slot_table(expert_ids.reshape(-1), shards, cap_x)
    assign_row = jnp.arange(tok_rows * topk, dtype=jnp.int32) // topk
    send_rows = (
        jnp.zeros((shards * cap_x, width_part), jnp.bfloat16)
        .at[assign_slot]
        .set(normed[assign_row])
    )
    arrived = lax.all_to_all(send_rows, "expert", split_axis=0, concat_axis=0, tiled=True)
    gate_part = (
        jnp.dot(arrived, gate_weight[0], preferred_element_type=jnp.float32)
        .astype(jnp.bfloat16)
        .astype(jnp.float32)
    )
    up_part = (
        jnp.dot(arrived, up_weight[0], preferred_element_type=jnp.float32)
        .astype(jnp.bfloat16)
        .astype(jnp.float32)
    )
    gate_sum, up_sum = (
        lax.psum(gate_part.astype(jnp.bfloat16), "tensor").astype(jnp.float32),
        lax.psum(up_part.astype(jnp.bfloat16), "tensor").astype(jnp.float32),
    )
    hidden = (jax.nn.silu(gate_sum) * up_sum).astype(jnp.bfloat16)
    expert_out = jnp.dot(hidden, down_weight[0], preferred_element_type=jnp.float32).astype(
        jnp.bfloat16
    )
    came_back = lax.all_to_all(expert_out, "expert", split_axis=0, concat_axis=0, tiled=True)
    picked = came_back[assign_slot].astype(jnp.float32).reshape(tok_rows, topk, width_part)
    moe = jnp.sum(route_weight[:, :, None] * picked, axis=1)
    return (resid + moe).astype(jnp.bfloat16)


def solution(mesh):
    return jax.shard_map(
        local,
        mesh=mesh,
        in_specs=(
            P(("groups", "expert"), "tensor"),
            P(("groups", "expert"), None),
            P(("groups", "expert"), "tensor"),
            P(("groups", "expert"), None),
            P(("groups", "expert"), None),
            P("tensor", None, None),
            P("tensor", "expert"),
            P("tensor"),
            P("expert", "tensor", None),
            P("expert", "tensor", None),
            P("expert", None, "tensor"),
            P(("groups", "expert"), None),
            P(("groups", "expert"), None),
        ),
        out_specs=P(("groups", "expert"), "tensor"),
        check_vma=False,
    )
```

profile of v0, /device:TPU:0, one launch (start us, length us, event | category | flops | bytes accessed | tf_op | source)
XLA Modules:
  0.0 445.2 jit_solution(11598379299307744804)
XLA Ops:
  6.5 0.7 all-gather.2.cloned.1.call-update
  7.4 0.1 reduce_window_sum.22
  7.5 0.2 select_reduce_fusion.1
  7.7 1.8 scatter_custom_fusion.1
  9.6 6.3 %all-to-all-start.1 = ((bf16[4,32,576]{2,1,0:T(8,128)(2,1)}), bf16[4,32,576]{2,1,0:T(8,128)(2,1)S(1)}, u32[]{:S(2)}, u32[]{:S(2)}) async-start(bf16[4,32,576]{2,1,0:T(8,128)(2,1)} %bitcast.5), calls=%async_computation.1 | async-start | bytes 327680 | tf_op jit(solution)/shard_map/all_to_all | solution.py:44
  15.9 4.6 %scatter_custom_fusion = bf16[128,9216]{1,0:T(8,128)(2,1)} fusion(s32[64]{0:T(128)S(1)} %fusion.54, bf16[64,9216]{1,0:T(8,128)(2,1)} %param.13, bf16[]{:T(256)} %constant.18.clone.1), kind=kCustom, calls=%fused_computation.26 | custom fusion | bytes 2359808 | tf_op jit(solution)/shard_map/scatter | solution.py:40
  20.5 1.8 all-to-all-done.1
  22.3 4.6 %all-to-all-start = ((bf16[4,32,9216]{2,1,0:T(8,128)(2,1)}), bf16[4,32,9216]{2,1,0:T(8,128)(2,1)}, u32[]{:S(2)}, u32[]{:S(2)}) async-start(bf16[4,32,9216]{2,1,0:T(8,128)(2,1)} %bitcast.78), calls=%async_computation | async-start | bytes 4718592 | tf_op jit(solution)/shard_map/all_to_all | solution.py:43
  26.9 116.0 %all-to-all-done = bf16[4,32,9216]{2,1,0:T(8,128)(2,1)} async-done(((bf16[4,32,9216]{2,1,0:T(8,128)(2,1)}), bf16[4,32,9216]{2,1,0:T(8,128)(2,1)}, u32[]{:S(2)}, u32[]{:S(2)}) %all-to-all-start) | async-done | bytes 2359328 | tf_op jit(solution)/shard_map/all_to_all | solution.py:43
  142.9 5.0 %reshape.102 = bf16[128,16,576]{2,1,0:T(8,128)(2,1)} reshape(bf16[4,32,9216]{2,1,0:T(8,128)(2,1)} %all-to-all-done) | data formatting | bytes 4718592 | tf_op jit(solution)/shard_map/reshape | solution.py:46
  147.9 2.8 fusion.36
  150.8 2.9 multiply_reduce_fusion
  153.7 1.3 copy-done.1
  155.0 0.8 fusion.8
  155.8 3.2 fusion.17
  159.1 0.3 copy.24
  159.4 1.0 all_to_all.43
  160.5 3.5 all-to-all-start.2
  164.0 0.1 copy.27
  164.1 0.1 eq.34
  164.3 30.6 %all-to-all-done.2 = bf16[4,32,2048]{2,1,0:T(8,128)(2,1)S(1)} async-done(((bf16[4,32,2048]{2,1,0:T(8,128)(2,1)}), bf16[4,32,2048]{2,1,0:T(8,128)(2,1)S(1)}, u32[]{:S(2)}, u32[]{:S(2)}) %all-to-all-start.2) | async-done | bytes 524320 | tf_op jit(solution)/shard_map/all_to_all | solution.py:71
  194.8 0.7 gather_fusion
  195.6 130.2 %all-gather.2.cloned.1.call-done = bf16[2048,3584]{1,0:T(8,128)(2,1)} async-done(((bf16[2048,896]{1,0:T(8,128)(2,1)}), bf16[2048,3584]{1,0:T(8,128)(2,1)}) %all-gather.2.cloned.1.call-update) | async-done | bytes 14680080 | tf_op jit(solution)/shard_map/all_gather | solution.py:75
  325.8 7.8 %convolution_convert_fusion = bf16[64,3584]{1,0:T(8,128)(2,1)S(1)} fusion(bf16[64,2048]{1,0:T(8,128)(2,1)S(1)} %gather_fusion, bf16[2048,3584]{1,0:T(8,128)(2,1)} %all-gather.2.cloned.1.call-done), kind=kOutput, calls=%fused_computation.6 | convolution fusion | flops 939753472 | bytes 15400960 | tf_op jit(solution)/shard_map/dot_general | solution.py:73
  333.6 1.2 copy.30
  334.8 0.2 all-reduce.3.cloned.1.call-start
  335.1 0.2 reduce_window_sum.23
  335.3 0.1 copy.26
  335.4 0.1 mul.101
  335.6 0.2 select_reduce_fusion
  335.8 21.5 %reduce-scatter.4.cloned.1.call-done = bf16[896,64]{1,0:T(8,128)(2,1)} async-done(((bf16[3584,64]{1,0:T(8,128)(2,1)}), bf16[896,64]{1,0:T(8,128)(2,1)}) %reduce-scatter.4.cloned.1.call-update) | async-done | bytes 114704
  357.3 1.1 copy.31
  358.4 0.1 multiply_reduce_fusion.2
  358.5 5.8 %psum.21 = f32[64]{0:T(128)S(1)} all-reduce(f32[64]{0:T(128)S(1)} %multiply_reduce_fusion.2), channel_id=1, replica_groups=mesh['groups'=2,'expert'=4,'tensor'=4] {'tensor'}, use_global_device_ids=true, to_apply=%region_10.11 | all-reduce | flops 64 | bytes 512 | tf_op jit(solution)/shard_map/psum | solution.py:82
  364.3 0.1 multiply_convert_fusion
  364.4 2.0 scatter_custom_fusion.2
  366.4 15.1 %all_to_all.57 = bf16[4,48,896]{2,1,0:T(8,128)(2,1)S(1)} all-to-all(bf16[4,48,896]{2,1,0:T(8,128)(2,1)S(1)} %bitcast.82), channel_id=1, replica_groups=mesh['groups'=2,'expert'=4,'tensor'=4] {'expert'}, dimensions={0} | all-to-all | bytes 688128 | tf_op jit(solution)/shard_map/all_to_all | solution.py:96
  381.5 2.9 fusion.11
  384.4 1.3 fusion.14
  385.7 33.1 %all-reduce.3.cloned.1.call-done = (bf16[192,1024]{1,0:T(8,128)(2,1)}, bf16[192,1024]{1,0:T(8,128)(2,1)}) async-done(((bf16[192,1024]{1,0:T(8,128)(2,1)}, bf16[192,1024]{1,0:T(8,128)(2,1)}), (bf16[192,1024]{1,0:T(8,128)(2,1)}, bf16[192,1024]{1,0:T(8,128)(2,1)})) %all-reduce.3.cloned.1.call-update) | async-done | bytes 786448 | tf_op jit(solution)/shard_map/psum | solution.py:109
  418.8 3.1 fusion.18
  421.9 4.6 %all-to-all-start.4 = ((bf16[4,48,896]{2,1,0:T(8,128)(2,1)}), bf16[4,48,896]{2,1,0:T(8,128)(2,1)S(1)}, u32[]{:S(2)}, u32[]{:S(2)}) async-start(bf16[4,48,896]{2,1,0:T(8,128)(2,1)} %bitcast.20), calls=%async_computation.4 | async-start | bytes 688128 | tf_op jit(solution)/shard_map/all_to_all | solution.py:115
  426.5 0.1 copy.25
  426.6 9.7 %all-to-all-done.4 = bf16[4,48,896]{2,1,0:T(8,128)(2,1)S(1)} async-done(((bf16[4,48,896]{2,1,0:T(8,128)(2,1)}), bf16[4,48,896]{2,1,0:T(8,128)(2,1)S(1)}, u32[]{:S(2)}, u32[]{:S(2)}) %all-to-all-start.4) | async-done | bytes 344096 | tf_op jit(solution)/shard_map/all_to_all | solution.py:115
  436.3 0.9 gather_fusion.1
  437.2 0.2 reshape.103
  437.4 0.6 multiply_reduce_fusion.1
  438.0 0.7 add_convert_fusion.1
  (36 shorter events, 0.5 us)
Async XLA Ops:
  6.5 149.3 %copy-start = (bf16[16,512,128]{2,1,0:T(8,128)(2,1)S(1)}, bf16[16,512,128]{2,1,0:T(8,128)(2,1)}, u32[]{:S(2)}) copy-start(bf16[16,512,128]{2,1,0:T(8,128)(2,1)} %param.18) | copy-start | bytes 6291460
  6.5 0.8 copy-start.5
  6.5 319.2 %all-gather.2.cloned.1.call-start = ((), (), s32[]{:S(2)}) async-start(), calls=%async_computation.6 | async-start | bytes 18350080 | tf_op jit(solution)/shard_map/all_gather | solution.py:75
  9.6 12.7 %all-to-all-start.1 = ((bf16[4,32,576]{2,1,0:T(8,128)(2,1)}), bf16[4,32,576]{2,1,0:T(8,128)(2,1)S(1)}, u32[]{:S(2)}, u32[]{:S(2)}) async-start(bf16[4,32,576]{2,1,0:T(8,128)(2,1)} %bitcast.5), calls=%async_computation.1 | async-start | bytes 327680 | tf_op jit(solution)/shard_map/all_to_all | solution.py:44
  22.3 120.6 %all-to-all-start = ((bf16[4,32,9216]{2,1,0:T(8,128)(2,1)}), bf16[4,32,9216]{2,1,0:T(8,128)(2,1)}, u32[]{:S(2)}, u32[]{:S(2)}) async-start(bf16[4,32,9216]{2,1,0:T(8,128)(2,1)} %bitcast.78), calls=%async_computation | async-start | bytes 4718592 | tf_op jit(solution)/shard_map/all_to_all | solution.py:43
  147.9 2.9 copy-start.8
  153.7 1.3 copy-start.1
  159.1 4.9 %copy-start.6 = (bf16[896]{0:T(1024)(128)(2,1)S(1)}, bf16[896]{0:T(1024)(128)(2,1)}, u32[]{:S(2)}) copy-start(bf16[896]{0:T(1024)(128)(2,1)} %param.20) | copy-start | bytes 5380
  159.1 5.0 %copy-start.4 = (s32[64,2]{0,1:T(2,128)S(1)}, s32[64,2]{0,1:T(2,128)}, u32[]{:S(2)}) copy-start(s32[64,2]{0,1:T(2,128)} %param.24) | copy-start | bytes 1540
  160.5 34.4 %all-to-all-start.2 = ((bf16[4,32,2048]{2,1,0:T(8,128)(2,1)}), bf16[4,32,2048]{2,1,0:T(8,128)(2,1)S(1)}, u32[]{:S(2)}, u32[]{:S(2)}) async-start(bf16[4,32,2048]{2,1,0:T(8,128)(2,1)} %all_to_all.43), calls=%async_computation.2 | async-start | bytes 1048576 | tf_op jit(solution)/shard_map/all_to_all | solution.py:71
  164.0 193.3 %reduce-scatter.4.cloned.1.call-start = ((), (), s32[]{:S(2)}) async-start(), calls=%async_computation.7 | async-start | bytes 1146880
  333.6 24.8 %copy-start.3 = (bf16[64,896]{1,0:T(8,128)(2,1)S(1)}, bf16[64,896]{1,0:T(8,128)(2,1)}, u32[]{:S(2)}) copy-start(bf16[64,896]{1,0:T(8,128)(2,1)} %param.15) | copy-start | bytes 344068
  334.8 84.0 %all-reduce.3.cloned.1.call-start = ((), (), s32[]{:S(2)}) async-start(), calls=%async_computation.8 | async-start | bytes 1572864 | tf_op jit(solution)/shard_map/psum | solution.py:109
  366.4 18.0 %copy-start.2 = (bf16[1,896,1024]{2,1,0:T(8,128)(2,1)S(1)}, bf16[1,896,1024]{2,1,0:T(8,128)(2,1)}, u32[]{:S(2)}) copy-start(bf16[1,896,1024]{2,1,0:T(8,128)(2,1)} %param.22) | copy-start | bytes 5505028
  418.8 7.7 %copy-start.7 = (f32[64,2]{0,1:T(2,128)S(1)}, f32[64,2]{0,1:T(2,128)}, u32[]{:S(2)}) copy-start(f32[64,2]{0,1:T(2,128)} %param.25) | copy-start | bytes 1540
  421.9 14.4 %all-to-all-start.4 = ((bf16[4,48,896]{2,1,0:T(8,128)(2,1)}), bf16[4,48,896]{2,1,0:T(8,128)(2,1)S(1)}, u32[]{:S(2)}, u32[]{:S(2)}) async-start(bf16[4,48,896]{2,1,0:T(8,128)(2,1)} %bitcast.20), calls=%async_computation.4 | async-start | bytes 688128 | tf_op jit(solution)/shard_map/all_to_all | solution.py:115
Sparse Core Ops, SparseCore 0:
  9.0 316.7 all-gather.1
  335.0 22.2 reduce-scatter.3
  385.9 32.8 all-reduce.2
where the time goes:
time: 446 us; the launch traced here: 445 us
  waiting for transfers between devices  343 us (77%)
  matrix products  24 us (5%)
  local copies, waits for them, and re-layouts  21.1 us (5%)
  blocking collectives  20.9 us (5%)
  starting transfers between devices  19.2 us (4%)
  between operations  13.4 us (3%)
    all_gather x1, waiting for transfers between devices, local(): lax.all_gather(out_proj, 'expert', axis=1, tiled=True)  130 us
    all_to_all x1, waiting for transfers between devices, local(): lax.all_to_all(send_query, 'expert', split_axis=0, concat_axis=0, tiled=T...  116 us
    psum x1, waiting for transfers between devices, local(): lax.psum(up_part.astype(jnp.bfloat16), 'tensor').astype(jnp.float32)  33.1 us
    all_to_all x1, waiting for transfers between devices, local(): lax.all_to_all(head_out, 'expert', split_axis=0, concat_axis=0, tiled=True)  30.6 us
    unnamed x4, waiting for transfers between devices  22.2 us
    all_to_all x1, blocking collectives, local(): lax.all_to_all(send_rows, 'expert', split_axis=0, concat_axis=0, tiled=True)  15.1 us
    all_to_all x1, waiting for transfers between devices, local(): lax.all_to_all(expert_out, 'expert', split_axis=0, concat_axis=0, tiled=T...  9.65 us
  transfers between devices with their start and end apart: 7, of which 7 were waited for; matrix products, arithmetic and copies ran while one was open for 5% of the time, Pallas kernels for 0%

commit v1 on v0

--- a/solution.py
+++ b/solution.py
@@ -1,7 +1,310 @@
+import functools
+
 import jax
 import jax.numpy as jnp
 from jax import lax
+from jax.experimental import pallas as pl
+from jax.experimental.pallas import tpu as pltpu
 from jax.sharding import PartitionSpec as P
+
+F32 = jnp.float32
+BF16 = jnp.bfloat16
+VMEM = pl.BlockSpec(memory_space=pltpu.VMEM)
+SMEM = pl.BlockSpec(memory_space=pltpu.SMEM)
+
+
+def dot(a, b):
+    return jnp.dot(a, b, preferred_element_type=F32)
+
+
+def dot_t(a, b):
+    return lax.dot_general(a, b, (((1,), (1,)), ((), ())), preferred_element_type=F32)
+
+
+def call(kernel, outs, specs, args, flops, scratch=()):
+    moved = sum(a.size * a.dtype.itemsize for a in args)
+    moved += sum(o.size * o.dtype.itemsize for o in outs)
+    return pl.pallas_call(
+        kernel,
+        out_shape=outs,
+        in_specs=specs,
+        out_specs=[VMEM] * len(outs),
+        scratch_shapes=list(scratch),
+        compiler_params=pltpu.CompilerParams(vmem_limit_bytes=32 * 1024 * 1024),
+        cost_estimate=pl.CostEstimate(flops=flops, bytes_accessed=moved, transcendentals=0),
+    )(*args)
+
+
+def shape(dims, dtype):
+    return jax.ShapeDtypeStruct(dims, dtype)
+
+
+def attend_kernel(scale, group, rel_ref, q_ref, own_ref, *refs):
+    keys, vup_ref, out_ref = refs[:-2], refs[-2], refs[-1]
+    rows, latent = own_ref.shape[0], vup_ref.shape[1]
+    heads, vhead = vup_ref.shape[0], vup_ref.shape[2]
+    blocks = [keys[0][...]]
+    for k in range(1, len(keys), 2):
+        blocks.append(jnp.concatenate([keys[k][...], keys[k + 1][...]], axis=0))
+    own = own_ref[...]
+    rel = jnp.concatenate([rel_ref[...]] * group, axis=0)
+    lane = lax.broadcasted_iota(jnp.int32, (rows * group, rows), 1)
+    line = lax.broadcasted_iota(jnp.int32, (rows * group, rows), 0) % rows
+    for first in range(0, heads, group):
+        q = q_ref[first * rows : (first + group) * rows, :]
+        score = dot_t(q, blocks[0])
+        for k in range(1, len(blocks)):
+            score = jnp.where(rel == k, dot_t(q, blocks[k]), score)
+        score = score * scale
+        own_score = jnp.where(lane == line, dot_t(q, own) * scale, -1e30)
+        top = jnp.maximum(
+            jnp.max(score, axis=1, keepdims=True), jnp.max(own_score, axis=1, keepdims=True)
+        )
+        expo = jnp.exp(score - top)
+        own_e = jnp.exp(own_score - top)
+        total = jnp.sum(expo, axis=1, keepdims=True) + jnp.sum(own_e, axis=1, keepdims=True)
+        inverse = 1.0 / total
+        probs = expo * inverse
+        acc = dot((own_e * inverse).astype(BF16), own[:, :latent])
+        for k in range(len(blocks)):
+            part = jnp.where(rel == k, probs, 0.0).astype(BF16)
+            acc = acc + dot(part, blocks[k][:, :latent])
+        acc = acc.astype(BF16)
+        for h in range(group):
+            head = dot(acc[h * rows : (h + 1) * rows], vup_ref[first + h])
+            out_ref[:, (first + h) * vhead : (first + h + 1) * vhead] = head.astype(BF16)
+
+
+def split_store(flag, value, keep_ref, send_ref):
+    half = value.shape[0] // 2
+
+    @pl.when(flag == 0)
+    def _():
+        keep_ref[...] = value[:half].astype(keep_ref.dtype)
+        send_ref[...] = value[half:].astype(send_ref.dtype)
+
+    @pl.when(flag != 0)
+    def _():
+        keep_ref[...] = value[half:].astype(keep_ref.dtype)
+        send_ref[...] = value[:half].astype(send_ref.dtype)
+
+
+def project_kernel(bits_ref, h0, h1, h2, h3, w_ref, keep_ref, send_ref):
+    rows = jnp.concatenate([h0[...], h1[...], h2[...], h3[...]], axis=0)
+    split_store(bits_ref[0], dot(rows, w_ref[...]), keep_ref, send_ref)
+
+
+def halve_kernel(bits_ref, kept_ref, got_ref, keep_ref, send_ref):
+    split_store(bits_ref[1], kept_ref[...] + got_ref[...].astype(F32), keep_ref, send_ref)
+
+
+def pieces(value):
+    high = value.astype(BF16).astype(F32)
+    middle = (value - high).astype(BF16).astype(F32)
+    lane = lax.broadcasted_iota(jnp.int32, (value.shape[0], 128), 1)
+    rest = jnp.where(lane == 2, value - high - middle, 0.0)
+    return jnp.where(lane == 0, high, jnp.where(lane == 1, middle, rest))
+
+
+def expand_kernel(bits_ref, pick_ref, a0, a1, a2, a3, gain_ref, gate_ref, up_ref, keep_ref, send_ref):
+    slots = pick_ref.shape[0] // 4
+    taken = [
+        dot(pick_ref[k * slots : (k + 1) * slots, :], a[...]) for k, a in enumerate((a0, a1, a2, a3))
+    ]
+    rows = jnp.concatenate(taken, axis=0)
+    squares = jnp.sum(rows * rows, axis=1, keepdims=True)
+    scaled = (rows * gain_ref[...].astype(F32)).astype(BF16)
+    full = jnp.concatenate(
+        [dot(scaled, gate_ref[...]), dot(scaled, up_ref[...]), pieces(squares)], axis=1
+    ).astype(BF16)
+    split_store(bits_ref[0], full, keep_ref, send_ref)
+
+
+def halve_expand_kernel(bits_ref, kept_ref, got_ref, keep_ref, send_ref):
+    width = kept_ref.shape[1] - 128
+    total = kept_ref[...].astype(F32) + got_ref[...].astype(F32)
+    squares = jnp.sum(total[:, width:], axis=1, keepdims=True)
+    total = jnp.concatenate([total[:, :width], pieces(squares)], axis=1)
+    split_store(bits_ref[1], total, keep_ref, send_ref)
+
+
+def hidden_kernel(features, kept_ref, got_ref, out_ref):
+    ff = (kept_ref.shape[1] - 128) // 2
+    total = kept_ref[...] + got_ref[...].astype(F32)
+    squares = jnp.sum(total[:, 2 * ff :], axis=1, keepdims=True)
+    scale = lax.rsqrt(squares / features + 1e-06)
+    gate = total[:, :ff] * scale
+    up = total[:, ff : 2 * ff] * scale
+    out_ref[...] = (gate / (1.0 + jnp.exp(-gate)) * up).astype(BF16)
+
+
+def contract_kernel(bits_ref, h0, h1, h2, h3, w_ref, o0, o1, o2, o3, held):
+    slots = h0.shape[0]
+    rows = jnp.concatenate([h0[...], h1[...], h2[...], h3[...]], axis=0)
+    held[...] = dot(rows, w_ref[...]).astype(BF16)
+    mine = 2 * bits_ref[0] + bits_ref[1]
+    for k, out in enumerate((o0, o1, o2, o3)):
+        start = pl.multiple_of((mine ^ k) * slots, 16)
+        out[...] = held[pl.ds(start, slots), :]
+
+
+def combine_kernel(put_ref, weight_ref, resid_ref, r0, r1, r2, r3, out_ref):
+    total = resid_ref[...].astype(F32)
+    for k, got in enumerate((r0, r1, r2, r3)):
+        total = total + weight_ref[:, k : k + 1] * dot(put_ref[k], got[...])
+    out_ref[...] = total.astype(BF16)
+
+
+def ranks(chosen):
+    count = chosen.astype(jnp.int32)
+    return jnp.cumsum(count, axis=-1) - count
+
+
+def square(
+    queries,
+    own_latent,
+    residual_in,
+    row_dest,
+    prompt_cache,
+    value_up,
+    out_proj,
+    norm_gain,
+    gate_weight,
+    up_weight,
+    down_weight,
+    expert_ids,
+    route_weight,
+):
+    count = 4
+    rows, width = residual_in.shape
+    heads, latent, vhead = value_up.shape
+    key_width = own_latent.shape[1]
+    prompt = prompt_cache.shape[0]
+    topk = expert_ids.shape[1]
+    ff = gate_weight.shape[2]
+    slots = 3 * topk * rows // (2 * count)
+    scale = (vhead + key_width - latent) ** (-0.5)
+    shard = lax.axis_index("expert")
+    tensor = lax.axis_index("tensor")
+    bits = jnp.stack([tensor % 2, tensor // 2]).astype(jnp.int32)
+
+    def along(value, k):
+        return lax.ppermute(value, "expert", [(i, (i + k) % count) for i in range(count)])
+
+    def swap(value, mask):
+        return lax.ppermute(value, "tensor", [(i, i ^ mask) for i in range(count)])
+
+    def place(t):
+        return 2 * (t % 2) + t // 2
+
+    def target(e, t, k):
+        return ((e - place(t) + k) % count) * count + e
+
+    cells = [(e, t) for e in range(count) for t in range(count)]
+
+    with jax.named_scope("gather_cache"):
+        half = lax.dynamic_slice_in_dim(prompt_cache, (tensor % 2) * (prompt // 2), prompt // 2, 0)
+        keys = [prompt_cache]
+        for k in range(1, count):
+            got = along(half, k)
+            keys += [got, swap(got, 1)]
+    with jax.named_scope("residual_to_columns"):
+        resid_cols = lax.ppermute(
+            residual_in, ("expert", "tensor"), [(target(e, t, 0), e * count + t) for e, t in cells]
+        )
+    with jax.named_scope("routing"):
+        ids = [expert_ids] + [along(expert_ids, k) for k in range(1, count)]
+        chosen = jnp.any(jnp.stack(ids) == shard, axis=2)
+        slot = jnp.arange(slots, dtype=jnp.int32)
+        pick = chosen[:, None, :] & (ranks(chosen)[:, None, :] == slot[None, :, None])
+        pick = pick.astype(BF16).reshape(count * slots, rows)
+        experts = (shard + jnp.arange(count, dtype=jnp.int32)) % count
+        named = expert_ids[None, :, :] == experts[:, None, None]
+        mine = jnp.any(named, axis=2)
+        put = mine[:, :, None] & (ranks(mine)[:, :, None] == slot[None, None, :])
+        put = put.astype(BF16)
+        weights = jnp.sum(jnp.where(named, route_weight[None], 0.0), axis=2).T
+        rel = (shard - row_dest) % count
+    with jax.named_scope("query_layout"):
+        q = queries.reshape(rows, heads, key_width).transpose(1, 0, 2)
+        q = q.reshape(heads * rows, key_width)
+    with jax.named_scope("attend"):
+        group = 4
+        (head_out,) = call(
+            functools.partial(attend_kernel, scale, group),
+            [shape((rows, heads * vhead), BF16)],
+            [VMEM] * (4 + len(keys)),
+            (rel, q, own_latent, *keys, value_up),
+            2 * heads * rows * count * prompt * (key_width + latent),
+        )
+    with jax.named_scope("gather_heads"):
+        gathered = [head_out] + [along(head_out, k) for k in range(1, count)]
+    with jax.named_scope("project"):
+        kept, sent = call(
+            project_kernel,
+            [shape((2 * rows, width), F32), shape((2 * rows, width), BF16)],
+            [SMEM] + [VMEM] * 5,
+            (bits, *gathered, out_proj),
+            2 * count * rows * heads * vhead * width,
+        )
+        kept, sent = call(
+            halve_kernel,
+            [shape((rows, width), F32), shape((rows, width), BF16)],
+            [SMEM, VMEM, VMEM],
+            (bits, kept, swap(sent, 1)),
+            2 * rows * width,
+        )
+        resid = (kept + swap(sent, 2).astype(F32) + resid_cols.astype(F32)).astype(BF16)
+    with jax.named_scope("scatter_resid"):
+        arrived = [
+            lax.ppermute(
+                resid, ("expert", "tensor"), [(e * count + t, target(e, t, k)) for e, t in cells]
+            )
+            for k in range(count)
+        ]
+    with jax.named_scope("expand"):
+        wide = 2 * ff + 128
+        kept, sent = call(
+            expand_kernel,
+            [shape((2 * slots, wide), BF16), shape((2 * slots, wide), BF16)],
+            [SMEM] + [VMEM] * 8,
+            (bits, pick, *arrived, norm_gain[None, :], gate_weight[0], up_weight[0]),
+            4 * count * slots * width * ff,
+        )
+        kept, sent = call(
+            halve_expand_kernel,
+            [shape((slots, wide), F32), shape((slots, wide), BF16)],
+            [SMEM, VMEM, VMEM],
+            (bits, kept, swap(sent, 1)),
+            2 * slots * wide,
+        )
+        (hidden,) = call(
+            functools.partial(hidden_kernel, width * count),
+            [shape((slots, ff), BF16)],
+            [VMEM, VMEM],
+            (kept, swap(sent, 2)),
+            8 * slots * wide,
+        )
+    with jax.named_scope("contract"):
+        across = swap(hidden, 2)
+        outs = call(
+            contract_kernel,
+            [shape((slots, width), BF16)] * count,
+            [SMEM] + [VMEM] * 5,
+            (bits, hidden, across, swap(hidden, 1), swap(across, 1), down_weight[0]),
+            2 * count * slots * width * ff,
+            [pltpu.VMEM((count * slots, width), BF16)],
+        )
+    with jax.named_scope("combine"):
+        back = [outs[0]] + [along(outs[k], -k) for k in range(1, count)]
+        (scored,) = call(
+            combine_kernel,
+            [shape((rows, width), BF16)],
+            [VMEM] * 7,
+            (put, weights, arrived[0], *back),
+            2 * count * rows * slots * width,
+        )
+    return scored
 
 
 def slot_table(targets, count, capacity):
@@ -11,7 +314,7 @@
     return targets * capacity + rank
 
 
-def local(
+def general(
     queries,
     own_latent,
     residual_in,
@@ -118,6 +421,12 @@
     return (resid + moe).astype(jnp.bfloat16)
 
 
+def local(*args):
+    if lax.axis_size("expert") == 4 and lax.axis_size("tensor") == 4:
+        return square(*args)
+    return general(*args)
+
+
 def solution(mesh):
     return jax.shard_map(
         local,

time: 446 us -> 123 us (0.28)
  waiting for transfers between devices: 343 us -> 50.7 us
  starting transfers between devices: 19.2 us -> 46 us
  matrix products: 24 us -> 0 us
  blocking collectives: 20.9 us -> 0 us
  Pallas kernels: 0 us -> 14.8 us
  between operations: 13.4 us -> 0.29 us
  local copies, waits for them, and re-layouts: 21.1 us -> 9.17 us
    all_to_all x4 -> x0, waiting for transfers between devices: 158 us -> none  [the longest x1 116 us: local(): lax.all_to_all(send_query, 'expert', split_axis=0, concat_axis=0, tiled=T...]
    all_gather x1 -> x0, waiting for transfers between devices: 130 us -> none  [local(): lax.all_gather(out_proj, 'expert', axis=1, tiled=True)]
    ppermute x0 -> x27, waiting for transfers between devices: none -> 50.7 us  [the longest x12 35.5 us: along(): lax.ppermute(value, 'expert', [(i, (i + k) % count) for i in range(count)])]
    ppermute x0 -> x27, starting transfers between devices: none -> 46 us  [the longest x12 19.6 us: along(): lax.ppermute(value, 'expert', [(i, (i + k) % count) for i in range(count)])]
    psum x1 -> x0, waiting for transfers between devices: 33.1 us -> none  [local(): lax.psum(up_part.astype(jnp.bfloat16), 'tensor').astype(jnp.float32)]
    dot_general x7 -> x0, matrix products: 24 us -> none  [the longest x1 7.79 us: local(): jnp.dot(attn_rows, lax.all_gather(out_proj, 'expert', axis=1, tiled=True)...]
    unnamed x4 -> x0, waiting for transfers between devices: 22.2 us -> none
    all_to_all x4 -> x0, starting transfers between devices: 18.9 us -> none  [the longest x1 6.32 us: local(): lax.all_to_all(send_key, 'expert', split_axis=0, concat_axis=0, tiled=True)]
  transfers between devices with their start and end apart: 7 -> 27, of which waited for: 7 -> 16; matrix products, arithmetic and copies ran while one was open for 5% -> 4% of each run, Pallas kernels for 0% -> 1%
where the time goes in v1:
time: 123 us
  waiting for transfers between devices  50.7 us (41%)
  starting transfers between devices  46 us (37%)
  Pallas kernels  14.8 us (12%)
  local copies, waits for them, and re-layouts  9.17 us (7%)
  other arithmetic  1.73 us (1%)
    ppermute x12, waiting for transfers between devices, along(): lax.ppermute(value, 'expert', [(i, (i + k) % count) for i in range(count)])  35.5 us
    ppermute x12, starting transfers between devices, along(): lax.ppermute(value, 'expert', [(i, (i + k) % count) for i in range(count)])  19.6 us
    pallas_call x8, Pallas kernels, call(): pl.pallas_call(kernel, out_shape=outs, in_specs=specs, out_specs=[VMEM] *...  14.8 us
    ppermute x4, starting transfers between devices, square(): lax.ppermute(resid, ('expert', 'tensor'), [(e * count + t, target(e, t, k...  13.4 us
    ppermute x10, waiting for transfers between devices, swap(): return lax.ppermute(value, 'tensor', [(i, i ^ mask) for i in range(count)])  13 us
    ppermute x10, starting transfers between devices, swap(): return lax.ppermute(value, 'tensor', [(i, i ^ mask) for i in range(count)])  12.3 us
    unnamed x21, local copies, waits for them, and re-layouts  6.23 us
    reshape x2, local copies, waits for them, and re-layouts, square(): q = queries.reshape(rows, heads, key_width).transpose(1, 0, 2)  2.52 us
  transfers between devices with their start and end apart: 27, of which 16 were waited for; matrix products, arithmetic and copies ran while one was open for 4% of the time, Pallas kernels for 1%

profile of v1, /device:TPU:0, one launch (start us, length us, event | category | flops | bytes accessed | tf_op | source)
XLA Modules:
  0.0 122.6 jit_solution(10022666406021667857)
XLA Ops:
  0.0 1.2 copy.43.refs_0_
  1.2 3.1 %collective-permute-start = (bf16[128,576]{1,0:T(8,128)(2,1)S(1)}, bf16[128,576]{1,0:T(8,128)(2,1)S(1)}, u32[]{:S(2)}, u32[]{:S(2)}) collective-permute-start(bf16[128,576]{1,0:T(8,128)(2,1)S(1)} %constant_dynamic-slice_fusion), channel_id=1, source_target_pairs={{0,4},{4,8},{8,12},{12,0},{1,5},{5,9},{9,13},{13,1},{2,6},{6,10},{... | collective-permute-start | bytes 442376 | tf_op jit(solution)/shard_map/gather_cache/ppermute | solution.py:192
  4.3 2.6 %collective-permute-start.2 = (bf16[128,576]{1,0:T(8,128)(2,1)S(1)}, bf16[128,576]{1,0:T(8,128)(2,1)S(1)}, u32[]{:S(2)}, u32[]{:S(2)}) collective-permute-start(bf16[128,576]{1,0:T(8,128)(2,1)S(1)} %constant_dynamic-slice_fusion), channel_id=1, source_target_pairs={{0,8},{4,12},{8,0},{12,4},{1,9},{5,13},{9,1},{13,5},{2,10},{6,14},... | collective-permute-start | bytes 442376 | tf_op jit(solution)/shard_map/gather_cache/ppermute | solution.py:192
  6.9 1.3 %collective-permute-start.4 = (bf16[128,576]{1,0:T(8,128)(2,1)S(1)}, bf16[128,576]{1,0:T(8,128)(2,1)S(1)}, u32[]{:S(2)}, u32[]{:S(2)}) collective-permute-start(bf16[128,576]{1,0:T(8,128)(2,1)S(1)} %constant_dynamic-slice_fusion), channel_id=1, source_target_pairs={{0,12},{4,0},{8,4},{12,8},{1,13},{5,1},{9,5},{13,9},{2,14},{6,2},{... | collective-permute-start | bytes 442376 | tf_op jit(solution)/shard_map/gather_cache/ppermute | solution.py:192
  8.2 0.7 broadcast_compare_fusion
  9.1 2.2 %reshape.53 = bf16[64,16,576]{2,1,0:T(8,128)(2,1)S(1)} reshape(bf16[64,9216]{1,0:T(8,128)(2,1)} %param.13) | data formatting | bytes 2359296 | tf_op jit(solution)/shard_map/query_layout/reshape | solution.py:229
  11.4 0.3 copy.41
  11.7 5.9 %collective-permute-done.2.refs_3_ = bf16[128,576]{1,0:T(8,128)(2,1)S(1)} collective-permute-done((bf16[128,576]{1,0:T(8,128)(2,1)S(1)}, bf16[128,576]{1,0:T(8,128)(2,1)S(1)}, u32[]{:S(2)}, u32[]{:S(2)}) %collective-permute-start.2) | collective-permute-done | bytes 147488 | tf_op jit(solution)/shard_map/gather_cache/ppermute | solution.py:192
  17.6 0.5 collective-permute-start.5
  18.2 0.8 collective-permute-done.3.refs_4_
  19.3 7.5 %attend.1.h0 = bf16[64,2048]{1,0:T(8,128)(2,1)S(1)} custom-call(s32[64,1]{1,0:T(8,128)S(1)} %add_select_fusion.rel_ref, bf16[1024,576]{1,0:T(8,128)(2,1)S(1)} %bitcast.24, bf16[64,576]{1,0:T(8,128)(2,1)S(1)} %copy-done.5, bf16[256,576]{1,0:T(8,128)(2,1)S(1)} %copy.43.refs_0_, bf16[128,576]{1,0:T(8,128)(2,1)S(1)} %collective-permute-done.refs_1_, ...), custom_call_target="tpu_custom_call" | custom-call | flops 2281701376 | bytes 4792576 | tf_op jit(solution)/shard_map/attend/pallas_call | solution.py:27
  26.8 3.8 %collective-permute-start.6 = (bf16[64,2048]{1,0:T(8,128)(2,1)S(1)}, bf16[64,2048]{1,0:T(8,128)(2,1)S(1)}, u32[]{:S(2)}, u32[]{:S(2)}) collective-permute-start(bf16[64,2048]{1,0:T(8,128)(2,1)S(1)} %attend.1.h0), channel_id=1, source_target_pairs={{0,4},{4,8},{8,12},{12,0},{1,5},{5,9},{9,13},{13,1},{2,6},{6,10},{... | collective-permute-start | bytes 786440 | tf_op jit(solution)/shard_map/gather_heads/ppermute | solution.py:192
  30.6 1.9 %collective-permute-start.7 = (bf16[64,2048]{1,0:T(8,128)(2,1)S(1)}, bf16[64,2048]{1,0:T(8,128)(2,1)S(1)}, u32[]{:S(2)}, u32[]{:S(2)}) collective-permute-start(bf16[64,2048]{1,0:T(8,128)(2,1)S(1)} %attend.1.h0), channel_id=1, source_target_pairs={{0,8},{4,12},{8,0},{12,4},{1,9},{5,13},{9,1},{13,5},{2,10},{6,14},... | collective-permute-start | bytes 786440 | tf_op jit(solution)/shard_map/gather_heads/ppermute | solution.py:192
  32.4 0.6 collective-permute-start.8
  33.1 6.0 %collective-permute-done.6.h1 = bf16[64,2048]{1,0:T(8,128)(2,1)S(1)} collective-permute-done((bf16[64,2048]{1,0:T(8,128)(2,1)S(1)}, bf16[64,2048]{1,0:T(8,128)(2,1)S(1)}, u32[]{:S(2)}, u32[]{:S(2)}) %collective-permute-start.6) | collective-permute-done | bytes 262176 | tf_op jit(solution)/shard_map/gather_heads/ppermute | solution.py:192
  39.1 10.9 %collective-permute-done.7.h2 = bf16[64,2048]{1,0:T(8,128)(2,1)S(1)} collective-permute-done((bf16[64,2048]{1,0:T(8,128)(2,1)S(1)}, bf16[64,2048]{1,0:T(8,128)(2,1)S(1)}, u32[]{:S(2)}, u32[]{:S(2)}) %collective-permute-start.7) | collective-permute-done | bytes 262176 | tf_op jit(solution)/shard_map/gather_heads/ppermute | solution.py:192
  50.0 2.0 %copy-done = bf16[2048,896]{1,0:T(8,128)(2,1)S(1)} copy-done((bf16[2048,896]{1,0:T(8,128)(2,1)S(1)}, bf16[2048,896]{1,0:T(8,128)(2,1)}, u32[]{:S(2)}) %copy-start) | copy-done | bytes 3670040
  52.0 1.8 %project.2 = (f32[128,896]{1,0:T(8,128)S(1)}, bf16[128,896]{1,0:T(8,128)(2,1)S(1)}) custom-call(s32[2]{0:T(128)S(1)} %pad_add_fusion.bits_ref, bf16[64,2048]{1,0:T(8,128)(2,1)S(1)} %attend.1.h0, bf16[64,2048]{1,0:T(8,128)(2,1)S(1)} %collective-permute-done.6.h1, bf16[64,2048]{1,0:T(8,128)(2,1)S(1)} %collective-permute-done.7.h2, ...), custom_call_target="tpu_custom_call" | custom-call | flops 939524096 | bytes 5406728 | tf_op jit(solution)/shard_map/project/pallas_call | solution.py:27
  54.0 0.7 collective-permute-start.11
  54.7 0.8 collective-permute-done.9.got_ref
  55.5 0.6 project.3
  56.1 7.1 %collective-permute-start.10 = (bf16[64,896]{1,0:T(8,128)(2,1)S(1)}, bf16[64,896]{1,0:T(8,128)(2,1)S(1)}, u32[]{:S(2)}, u32[]{:S(2)}) collective-permute-start(bf16[64,896]{1,0:T(8,128)(2,1)S(1)} %get-tuple-element.20), channel_id=1, source_target_pairs={{0,2},{1,3},{2,0},{3,1},{4,6},{5,7},{6,4},{7,5},{8,10},{9,11},{10,... | collective-permute-start | bytes 344072 | tf_op jit(solution)/shard_map/project/ppermute | solution.py:195
  63.2 1.5 %collective-permute-start.15 = (s32[64,2]{0,1:T(2,128)S(1)}, s32[64,2]{0,1:T(2,128)S(1)}, u32[]{:S(2)}, u32[]{:S(2)}) collective-permute-start(s32[64,2]{0,1:T(2,128)S(1)} %copy-done.6), channel_id=1, source_target_pairs={{0,12},{4,0},{8,4},{12,8},{1,13},{5,1},{9,5},{13,9},{2,14},{6,2},{... | collective-permute-start | bytes 1544 | tf_op jit(solution)/shard_map/routing/ppermute | solution.py:192
  64.7 0.9 collective-permute-start.14
  65.8 1.0 collective-permute-done.15
  66.8 2.4 %collective-permute-done.14 = s32[64,2]{0,1:T(2,128)S(1)} collective-permute-done((s32[64,2]{0,1:T(2,128)S(1)}, s32[64,2]{0,1:T(2,128)S(1)}, u32[]{:S(2)}, u32[]{:S(2)}) %collective-permute-start.14) | collective-permute-done | bytes 544 | tf_op jit(solution)/shard_map/routing/ppermute | solution.py:192
  69.2 1.8 %collective-permute-done.13 = s32[64,2]{0,1:T(2,128)S(1)} collective-permute-done((s32[64,2]{0,1:T(2,128)S(1)}, s32[64,2]{0,1:T(2,128)S(1)}, u32[]{:S(2)}, u32[]{:S(2)}) %collective-permute-start.13) | collective-permute-done | bytes 544 | tf_op jit(solution)/shard_map/routing/ppermute | solution.py:192
  71.4 0.7 collective-permute-start.12
  72.0 1.9 %collective-permute-start.16 = (bf16[64,896]{1,0:T(8,128)(2,1)S(1)}, bf16[64,896]{1,0:T(8,128)(2,1)S(1)}, u32[]{:S(2)}, u32[]{:S(2)}) collective-permute-start(bf16[64,896]{1,0:T(8,128)(2,1)S(1)} %add_convert_fusion), channel_id=1, source_target_pairs={{0,4},{1,12},{2,0},{3,8},{4,9},{5,1},{6,5},{7,13},{8,14},{9,6},{10... | collective-permute-start | bytes 344072 | tf_op jit(solution)/shard_map/scatter_resid/ppermute | solution.py:260
  74.0 5.0 %collective-permute-start.17 = (bf16[64,896]{1,0:T(8,128)(2,1)S(1)}, bf16[64,896]{1,0:T(8,128)(2,1)S(1)}, u32[]{:S(2)}, u32[]{:S(2)}) collective-permute-start(bf16[64,896]{1,0:T(8,128)(2,1)S(1)} %add_convert_fusion), channel_id=1, source_target_pairs={{0,8},{1,0},{2,4},{3,12},{4,13},{5,5},{6,9},{7,1},{8,2},{9,10},{10... | collective-permute-start | bytes 344072 | tf_op jit(solution)/shard_map/scatter_resid/ppermute | solution.py:260
  78.9 5.8 %collective-permute-start.18 = (bf16[64,896]{1,0:T(8,128)(2,1)S(1)}, bf16[64,896]{1,0:T(8,128)(2,1)S(1)}, u32[]{:S(2)}, u32[]{:S(2)}) collective-permute-start(bf16[64,896]{1,0:T(8,128)(2,1)S(1)} %add_convert_fusion), channel_id=1, source_target_pairs={{0,12},{1,4},{2,8},{3,0},{4,1},{5,9},{6,13},{7,5},{8,6},{9,14},{10... | collective-permute-start | bytes 344072 | tf_op jit(solution)/shard_map/scatter_resid/ppermute | solution.py:260
  84.9 2.2 %collective-permute-done.18.a3 = bf16[64,896]{1,0:T(8,128)(2,1)S(1)} collective-permute-done((bf16[64,896]{1,0:T(8,128)(2,1)S(1)}, bf16[64,896]{1,0:T(8,128)(2,1)S(1)}, u32[]{:S(2)}, u32[]{:S(2)}) %collective-permute-start.18) | collective-permute-done | bytes 114720 | tf_op jit(solution)/shard_map/scatter_resid/ppermute | solution.py:260
  87.1 1.5 %copy-done.2 = bf16[1,896,1024]{2,1,0:T(8,128)(2,1)S(1)} copy-done((bf16[1,896,1024]{2,1,0:T(8,128)(2,1)S(1)}, bf16[1,896,1024]{2,1,0:T(8,128)(2,1)}, u32[]{:S(2)}) %copy-start.2) | copy-done | bytes 1835032
  88.6 1.8 %expand.3 = (bf16[96,2176]{1,0:T(8,128)(2,1)S(1)}, bf16[96,2176]{1,0:T(8,128)(2,1)S(1)}) custom-call(s32[2]{0:T(128)S(1)} %pad_add_fusion.bits_ref, bf16[192,64]{1,0:T(8,128)(2,1)S(1)} %fusion.3.pick_ref, bf16[64,896]{1,0:T(8,128)(2,1)S(1)} %collective-permute-done.12.a0.resid_ref, bf16[64,896]{1,0:T(8,128)(2,1)S(1)} %collective-permute-done.16.a1, ...), custom_call_target="tpu_custom_call" | custom-call | flops 704643072 | bytes 4990728 | tf_op jit(solution)/shard_map/expand/pallas_call | solution.py:27
  90.5 1.7 %collective-permute-done.19.got_ref = bf16[96,2176]{1,0:T(8,128)(2,1)S(1)} collective-permute-done((bf16[96,2176]{1,0:T(8,128)(2,1)S(1)}, bf16[96,2176]{1,0:T(8,128)(2,1)S(1)}, u32[]{:S(2)}, u32[]{:S(2)}) %collective-permute-start.19) | collective-permute-done | bytes 417824 | tf_op jit(solution)/shard_map/expand/ppermute | solution.py:195
  92.2 0.8 expand.4
  93.0 2.7 %collective-permute-start.20 = (bf16[48,2176]{1,0:T(8,128)(2,1)S(1)}, bf16[48,2176]{1,0:T(8,128)(2,1)S(1)}, u32[]{:S(2)}, u32[]{:S(2)}) collective-permute-start(bf16[48,2176]{1,0:T(8,128)(2,1)S(1)} %get-tuple-element.24), channel_id=1, source_target_pairs={{0,2},{1,3},{2,0},{3,1},{4,6},{5,7},{6,4},{7,5},{8,10},{9,11},{10,... | collective-permute-start | bytes 626696 | tf_op jit(solution)/shard_map/expand/ppermute | solution.py:195
  96.0 5.3 %collective-permute-done.20.got_ref = bf16[48,2176]{1,0:T(8,128)(2,1)S(1)} collective-permute-done((bf16[48,2176]{1,0:T(8,128)(2,1)S(1)}, bf16[48,2176]{1,0:T(8,128)(2,1)S(1)}, u32[]{:S(2)}, u32[]{:S(2)}) %collective-permute-start.20) | collective-permute-done | bytes 208928 | tf_op jit(solution)/shard_map/expand/ppermute | solution.py:195
  101.5 1.8 %collective-permute-start.21 = (bf16[48,1024]{1,0:T(8,128)(2,1)S(1)}, bf16[48,1024]{1,0:T(8,128)(2,1)S(1)}, u32[]{:S(2)}, u32[]{:S(2)}) collective-permute-start(bf16[48,1024]{1,0:T(8,128)(2,1)S(1)} %expand.5.h0), channel_id=1, source_target_pairs={{0,2},{1,3},{2,0},{3,1},{4,6},{5,7},{6,4},{7,5},{8,10},{9,11},{10,... | collective-permute-start | bytes 294920 | tf_op jit(solution)/shard_map/contract/ppermute | solution.py:195
  103.3 2.9 %collective-permute-done.21.h1 = bf16[48,1024]{1,0:T(8,128)(2,1)S(1)} collective-permute-done((bf16[48,1024]{1,0:T(8,128)(2,1)S(1)}, bf16[48,1024]{1,0:T(8,128)(2,1)S(1)}, u32[]{:S(2)}, u32[]{:S(2)}) %collective-permute-start.21) | collective-permute-done | bytes 98336 | tf_op jit(solution)/shard_map/contract/ppermute | solution.py:195
  106.4 1.1 collective-permute-done.23.h3
  107.5 1.5 %copy-done.3 = bf16[1,1024,896]{2,1,0:T(8,128)(2,1)S(1)} copy-done((bf16[1,1024,896]{2,1,0:T(8,128)(2,1)S(1)}, bf16[1,1024,896]{2,1,0:T(8,128)(2,1)}, u32[]{:S(2)}) %copy-start.3) | copy-done | bytes 1835032
  109.0 1.1 contract.1
  110.2 3.2 %collective-permute-start.24 = (bf16[48,896]{1,0:T(8,128)(2,1)S(1)}, bf16[48,896]{1,0:T(8,128)(2,1)S(1)}, u32[]{:S(2)}, u32[]{:S(2)}) collective-permute-start(bf16[48,896]{1,0:T(8,128)(2,1)S(1)} %get-tuple-element.26), channel_id=1, source_target_pairs={{0,12},{4,0},{8,4},{12,8},{1,13},{5,1},{9,5},{13,9},{2,14},{6,2},{... | collective-permute-start | bytes 258056 | tf_op jit(solution)/shard_map/combine/ppermute | solution.py:192
  113.4 0.6 collective-permute-start.26
  114.2 2.1 %collective-permute-done.24.r1 = bf16[48,896]{1,0:T(8,128)(2,1)S(1)} collective-permute-done((bf16[48,896]{1,0:T(8,128)(2,1)S(1)}, bf16[48,896]{1,0:T(8,128)(2,1)S(1)}, u32[]{:S(2)}, u32[]{:S(2)}) %collective-permute-start.24) | collective-permute-done | bytes 86048 | tf_op jit(solution)/shard_map/combine/ppermute | solution.py:192
  116.3 5.4 %collective-permute-done.25.r2 = bf16[48,896]{1,0:T(8,128)(2,1)S(1)} collective-permute-done((bf16[48,896]{1,0:T(8,128)(2,1)S(1)}, bf16[48,896]{1,0:T(8,128)(2,1)S(1)}, u32[]{:S(2)}, u32[]{:S(2)}) %collective-permute-start.25) | collective-permute-done | bytes 86048 | tf_op jit(solution)/shard_map/combine/ppermute | solution.py:192
  121.7 0.9 combine.1
  (60 shorter events, 2.3 us)
Async XLA Ops:
  1.2 10.4 %collective-permute-start = (bf16[128,576]{1,0:T(8,128)(2,1)S(1)}, bf16[128,576]{1,0:T(8,128)(2,1)S(1)}, u32[]{:S(2)}, u32[]{:S(2)}) collective-permute-start(bf16[128,576]{1,0:T(8,128)(2,1)S(1)} %constant_dynamic-slice_fusion), channel_id=1, source_target_pairs={{0,4},{4,8},{8,12},{12,0},{1,5},{5,9},{9,13},{13,1},{2,6},{6,10},{... | collective-permute-start | bytes 442376 | tf_op jit(solution)/shard_map/gather_cache/ppermute | solution.py:192
  4.3 13.3 %collective-permute-start.2 = (bf16[128,576]{1,0:T(8,128)(2,1)S(1)}, bf16[128,576]{1,0:T(8,128)(2,1)S(1)}, u32[]{:S(2)}, u32[]{:S(2)}) collective-permute-start(bf16[128,576]{1,0:T(8,128)(2,1)S(1)} %constant_dynamic-slice_fusion), channel_id=1, source_target_pairs={{0,8},{4,12},{8,0},{12,4},{1,9},{5,13},{9,1},{13,5},{2,10},{6,14},... | collective-permute-start | bytes 442376 | tf_op jit(solution)/shard_map/gather_cache/ppermute | solution.py:192
  6.9 10.8 %collective-permute-start.4 = (bf16[128,576]{1,0:T(8,128)(2,1)S(1)}, bf16[128,576]{1,0:T(8,128)(2,1)S(1)}, u32[]{:S(2)}, u32[]{:S(2)}) collective-permute-start(bf16[128,576]{1,0:T(8,128)(2,1)S(1)} %constant_dynamic-slice_fusion), channel_id=1, source_target_pairs={{0,12},{4,0},{8,4},{12,8},{1,13},{5,1},{9,5},{13,9},{2,14},{6,2},{... | collective-permute-start | bytes 442376 | tf_op jit(solution)/shard_map/gather_cache/ppermute | solution.py:192
  11.3 7.9 %copy-start.4 = (bf16[16,512,128]{2,1,0:T(8,128)(2,1)S(1)}, bf16[16,512,128]{2,1,0:T(8,128)(2,1)}, u32[]{:S(2)}) copy-start(bf16[16,512,128]{2,1,0:T(8,128)(2,1)} %refs_7_.1) | copy-start | bytes 6291460
  11.3 7.9 %copy-start.5 = (bf16[64,576]{1,0:T(8,128)(2,1)S(1)}, bf16[64,576]{1,0:T(8,128)(2,1)}, u32[]{:S(2)}) copy-start(bf16[64,576]{1,0:T(8,128)(2,1)} %own_ref.1) | copy-start | bytes 221188
  11.7 6.5 %collective-permute-start.1 = (bf16[128,576]{1,0:T(8,128)(2,1)S(1)}, bf16[128,576]{1,0:T(8,128)(2,1)S(1)}, u32[]{:S(2)}, u32[]{:S(2)}) collective-permute-start(bf16[128,576]{1,0:T(8,128)(2,1)S(1)} %collective-permute-done.refs_1_), channel_id=1, source_target_pairs={{0,1},{1,0},{2,3},{3,2},{4,5},{5,4},{6,7},{7,6},{8,9},{9,8},{10,11... | collective-permute-start | bytes 442376 | tf_op jit(solution)/shard_map/gather_cache/ppermute | solution.py:195
  17.6 1.4 %collective-permute-start.3 = (bf16[128,576]{1,0:T(8,128)(2,1)S(1)}, bf16[128,576]{1,0:T(8,128)(2,1)S(1)}, u32[]{:S(2)}, u32[]{:S(2)}) collective-permute-start(bf16[128,576]{1,0:T(8,128)(2,1)S(1)} %collective-permute-done.2.refs_3_), channel_id=1, source_target_pairs={{0,1},{1,0},{2,3},{3,2},{4,5},{5,4},{6,7},{7,6},{8,9},{9,8},{10,11... | collective-permute-start | bytes 442376 | tf_op jit(solution)/shard_map/gather_cache/ppermute | solution.py:195
  17.6 1.6 %collective-permute-start.5 = (bf16[128,576]{1,0:T(8,128)(2,1)S(1)}, bf16[128,576]{1,0:T(8,128)(2,1)S(1)}, u32[]{:S(2)}, u32[]{:S(2)}) collective-permute-start(bf16[128,576]{1,0:T(8,128)(2,1)S(1)} %collective-permute-done.4.refs_5_), channel_id=1, source_target_pairs={{0,1},{1,0},{2,3},{3,2},{4,5},{5,4},{6,7},{7,6},{8,9},{9,8},{10,11... | collective-permute-start | bytes 442376 | tf_op jit(solution)/shard_map/gather_cache/ppermute | solution.py:195
  26.8 12.3 %collective-permute-start.6 = (bf16[64,2048]{1,0:T(8,128)(2,1)S(1)}, bf16[64,2048]{1,0:T(8,128)(2,1)S(1)}, u32[]{:S(2)}, u32[]{:S(2)}) collective-permute-start(bf16[64,2048]{1,0:T(8,128)(2,1)S(1)} %attend.1.h0), channel_id=1, source_target_pairs={{0,4},{4,8},{8,12},{12,0},{1,5},{5,9},{9,13},{13,1},{2,6},{6,10},{... | collective-permute-start | bytes 786440 | tf_op jit(solution)/shard_map/gather_heads/ppermute | solution.py:192
  30.6 19.4 %collective-permute-start.7 = (bf16[64,2048]{1,0:T(8,128)(2,1)S(1)}, bf16[64,2048]{1,0:T(8,128)(2,1)S(1)}, u32[]{:S(2)}, u32[]{:S(2)}) collective-permute-start(bf16[64,2048]{1,0:T(8,128)(2,1)S(1)} %attend.1.h0), channel_id=1, source_target_pairs={{0,8},{4,12},{8,0},{12,4},{1,9},{5,13},{9,1},{13,5},{2,10},{6,14},... | collective-permute-start | bytes 786440 | tf_op jit(solution)/shard_map/gather_heads/ppermute | solution.py:192
  32.4 17.6 %collective-permute-start.8 = (bf16[64,2048]{1,0:T(8,128)(2,1)S(1)}, bf16[64,2048]{1,0:T(8,128)(2,1)S(1)}, u32[]{:S(2)}, u32[]{:S(2)}) collective-permute-start(bf16[64,2048]{1,0:T(8,128)(2,1)S(1)} %attend.1.h0), channel_id=1, source_target_pairs={{0,12},{4,0},{8,4},{12,8},{1,13},{5,1},{9,5},{13,9},{2,14},{6,2},{... | collective-permute-start | bytes 786440 | tf_op jit(solution)/shard_map/gather_heads/ppermute | solution.py:192
  33.0 32.8 %copy-start.7 = (bf16[896]{0:T(1024)(128)(2,1)S(1)}, bf16[896]{0:T(1024)(128)(2,1)}, u32[]{:S(2)}) copy-start(bf16[896]{0:T(1024)(128)(2,1)} %param.20) | copy-start | bytes 5380
  33.0 30.2 %copy-start.6 = (s32[64,2]{0,1:T(2,128)S(1)}, s32[64,2]{0,1:T(2,128)}, u32[]{:S(2)}) copy-start(s32[64,2]{0,1:T(2,128)} %param.24) | copy-start | bytes 1540
  50.0 2.0 %copy-start = (bf16[2048,896]{1,0:T(8,128)(2,1)S(1)}, bf16[2048,896]{1,0:T(8,128)(2,1)}, u32[]{:S(2)}) copy-start(bf16[2048,896]{1,0:T(8,128)(2,1)} %w_ref.1) | copy-start | bytes 11010052
  52.0 1.9 %copy-start.9 = (bf16[64,896]{1,0:T(8,128)(2,1)S(1)}, bf16[64,896]{1,0:T(8,128)(2,1)}, u32[]{:S(2)}) copy-start(bf16[64,896]{1,0:T(8,128)(2,1)} %param.15) | copy-start | bytes 344068
  52.0 35.1 %copy-start.1 = (bf16[1,896,1024]{2,1,0:T(8,128)(2,1)S(1)}, bf16[1,896,1024]{2,1,0:T(8,128)(2,1)}, u32[]{:S(2)}) copy-start(bf16[1,896,1024]{2,1,0:T(8,128)(2,1)} %param.21) | copy-start | bytes 5505028
  53.9 1.6 %collective-permute-start.9 = (bf16[128,896]{1,0:T(8,128)(2,1)S(1)}, bf16[128,896]{1,0:T(8,128)(2,1)S(1)}, u32[]{:S(2)}, u32[]{:S(2)}) collective-permute-start(bf16[128,896]{1,0:T(8,128)(2,1)S(1)} %get-tuple-element.18), channel_id=1, source_target_pairs={{0,1},{1,0},{2,3},{3,2},{4,5},{5,4},{6,7},{7,6},{8,9},{9,8},{10,11... | collective-permute-start | bytes 688136 | tf_op jit(solution)/shard_map/project/ppermute | solution.py:195
  54.0 17.3 %collective-permute-start.11 = (bf16[64,896]{1,0:T(8,128)(2,1)S(1)}, bf16[64,896]{1,0:T(8,128)(2,1)S(1)}, u32[]{:S(2)}, u32[]{:S(2)}) collective-permute-start(bf16[64,896]{1,0:T(8,128)(2,1)S(1)} %copy-done.9), channel_id=1, source_target_pairs={{0,0},{8,1},{12,2},{4,3},{5,4},{13,5},{1,6},{9,7},{10,8},{2,9},{6,... | collective-permute-start | bytes 344072 | tf_op jit(solution)/shard_map/residual_to_columns/ppermute | solution.py:212
  56.1 15.2 %collective-permute-start.10 = (bf16[64,896]{1,0:T(8,128)(2,1)S(1)}, bf16[64,896]{1,0:T(8,128)(2,1)S(1)}, u32[]{:S(2)}, u32[]{:S(2)}) collective-permute-start(bf16[64,896]{1,0:T(8,128)(2,1)S(1)} %get-tuple-element.20), channel_id=1, source_target_pairs={{0,2},{1,3},{2,0},{3,1},{4,6},{5,7},{6,4},{7,5},{8,10},{9,11},{10,... | collective-permute-start | bytes 344072 | tf_op jit(solution)/shard_map/project/ppermute | solution.py:195
  63.2 3.6 %collective-permute-start.15 = (s32[64,2]{0,1:T(2,128)S(1)}, s32[64,2]{0,1:T(2,128)S(1)}, u32[]{:S(2)}, u32[]{:S(2)}) collective-permute-start(s32[64,2]{0,1:T(2,128)S(1)} %copy-done.6), channel_id=1, source_target_pairs={{0,12},{4,0},{8,4},{12,8},{1,13},{5,1},{9,5},{13,9},{2,14},{6,2},{... | collective-permute-start | bytes 1544 | tf_op jit(solution)/shard_map/routing/ppermute | solution.py:192
  64.7 4.5 %collective-permute-start.14 = (s32[64,2]{0,1:T(2,128)S(1)}, s32[64,2]{0,1:T(2,128)S(1)}, u32[]{:S(2)}, u32[]{:S(2)}) collective-permute-start(s32[64,2]{0,1:T(2,128)S(1)} %copy-done.6), channel_id=1, source_target_pairs={{0,8},{4,12},{8,0},{12,4},{1,9},{5,13},{9,1},{13,5},{2,10},{6,14},... | collective-permute-start | bytes 1544 | tf_op jit(solution)/shard_map/routing/ppermute | solution.py:192
  65.7 5.4 %collective-permute-start.13 = (s32[64,2]{0,1:T(2,128)S(1)}, s32[64,2]{0,1:T(2,128)S(1)}, u32[]{:S(2)}, u32[]{:S(2)}) collective-permute-start(s32[64,2]{0,1:T(2,128)S(1)} %copy-done.6), channel_id=1, source_target_pairs={{0,4},{4,8},{8,12},{12,0},{1,5},{5,9},{9,13},{13,1},{2,6},{6,10},{... | collective-permute-start | bytes 1544 | tf_op jit(solution)/shard_map/routing/ppermute | solution.py:192
  71.4 13.5 %collective-permute-start.12 = (bf16[64,896]{1,0:T(8,128)(2,1)S(1)}, bf16[64,896]{1,0:T(8,128)(2,1)S(1)}, u32[]{:S(2)}, u32[]{:S(2)}) collective-permute-start(bf16[64,896]{1,0:T(8,128)(2,1)S(1)} %add_convert_fusion), channel_id=1, source_target_pairs={{0,0},{1,8},{2,12},{3,4},{4,5},{5,13},{6,1},{7,9},{8,10},{9,2},{10... | collective-permute-start | bytes 344072 | tf_op jit(solution)/shard_map/scatter_resid/ppermute | solution.py:260
  72.0 12.8 %collective-permute-start.16 = (bf16[64,896]{1,0:T(8,128)(2,1)S(1)}, bf16[64,896]{1,0:T(8,128)(2,1)S(1)}, u32[]{:S(2)}, u32[]{:S(2)}) collective-permute-start(bf16[64,896]{1,0:T(8,128)(2,1)S(1)} %add_convert_fusion), channel_id=1, source_target_pairs={{0,4},{1,12},{2,0},{3,8},{4,9},{5,1},{6,5},{7,13},{8,14},{9,6},{10... | collective-permute-start | bytes 344072 | tf_op jit(solution)/shard_map/scatter_resid/ppermute | solution.py:260
  74.0 10.9 %collective-permute-start.17 = (bf16[64,896]{1,0:T(8,128)(2,1)S(1)}, bf16[64,896]{1,0:T(8,128)(2,1)S(1)}, u32[]{:S(2)}, u32[]{:S(2)}) collective-permute-start(bf16[64,896]{1,0:T(8,128)(2,1)S(1)} %add_convert_fusion), channel_id=1, source_target_pairs={{0,8},{1,0},{2,4},{3,12},{4,13},{5,5},{6,9},{7,1},{8,2},{9,10},{10... | collective-permute-start | bytes 344072 | tf_op jit(solution)/shard_map/scatter_resid/ppermute | solution.py:260
  78.9 8.2 %collective-permute-start.18 = (bf16[64,896]{1,0:T(8,128)(2,1)S(1)}, bf16[64,896]{1,0:T(8,128)(2,1)S(1)}, u32[]{:S(2)}, u32[]{:S(2)}) collective-permute-start(bf16[64,896]{1,0:T(8,128)(2,1)S(1)} %add_convert_fusion), channel_id=1, source_target_pairs={{0,12},{1,4},{2,8},{3,0},{4,1},{5,9},{6,13},{7,5},{8,6},{9,14},{10... | collective-permute-start | bytes 344072 | tf_op jit(solution)/shard_map/scatter_resid/ppermute | solution.py:260
  87.1 1.5 %copy-start.2 = (bf16[1,896,1024]{2,1,0:T(8,128)(2,1)S(1)}, bf16[1,896,1024]{2,1,0:T(8,128)(2,1)}, u32[]{:S(2)}) copy-start(bf16[1,896,1024]{2,1,0:T(8,128)(2,1)} %param.22) | copy-start | bytes 5505028
  90.4 1.8 %collective-permute-start.19 = (bf16[96,2176]{1,0:T(8,128)(2,1)S(1)}, bf16[96,2176]{1,0:T(8,128)(2,1)S(1)}, u32[]{:S(2)}, u32[]{:S(2)}) collective-permute-start(bf16[96,2176]{1,0:T(8,128)(2,1)S(1)} %get-tuple-element.22), channel_id=1, source_target_pairs={{0,1},{1,0},{2,3},{3,2},{4,5},{5,4},{6,7},{7,6},{8,9},{9,8},{10,11... | collective-permute-start | bytes 1253384 | tf_op jit(solution)/shard_map/expand/ppermute | solution.py:195
  92.2 21.8 %copy-start.8 = (f32[64,2]{0,1:T(2,128)S(1)}, f32[64,2]{0,1:T(2,128)}, u32[]{:S(2)}) copy-start(f32[64,2]{0,1:T(2,128)} %param.25) | copy-start | bytes 1540
  93.0 8.4 %collective-permute-start.20 = (bf16[48,2176]{1,0:T(8,128)(2,1)S(1)}, bf16[48,2176]{1,0:T(8,128)(2,1)S(1)}, u32[]{:S(2)}, u32[]{:S(2)}) collective-permute-start(bf16[48,2176]{1,0:T(8,128)(2,1)S(1)} %get-tuple-element.24), channel_id=1, source_target_pairs={{0,2},{1,3},{2,0},{3,1},{4,6},{5,7},{6,4},{7,5},{8,10},{9,11},{10,... | collective-permute-start | bytes 626696 | tf_op jit(solution)/shard_map/expand/ppermute | solution.py:195
  101.5 4.7 %collective-permute-start.21 = (bf16[48,1024]{1,0:T(8,128)(2,1)S(1)}, bf16[48,1024]{1,0:T(8,128)(2,1)S(1)}, u32[]{:S(2)}, u32[]{:S(2)}) collective-permute-start(bf16[48,1024]{1,0:T(8,128)(2,1)S(1)} %expand.5.h0), channel_id=1, source_target_pairs={{0,2},{1,3},{2,0},{3,1},{4,6},{5,7},{6,4},{7,5},{8,10},{9,11},{10,... | collective-permute-start | bytes 294920 | tf_op jit(solution)/shard_map/contract/ppermute | solution.py:195
  103.3 3.0 %collective-permute-start.22 = (bf16[48,1024]{1,0:T(8,128)(2,1)S(1)}, bf16[48,1024]{1,0:T(8,128)(2,1)S(1)}, u32[]{:S(2)}, u32[]{:S(2)}) collective-permute-start(bf16[48,1024]{1,0:T(8,128)(2,1)S(1)} %expand.5.h0), channel_id=1, source_target_pairs={{0,1},{1,0},{2,3},{3,2},{4,5},{5,4},{6,7},{7,6},{8,9},{9,8},{10,11... | collective-permute-start | bytes 294920 | tf_op jit(solution)/shard_map/contract/ppermute | solution.py:195
  106.2 1.3 %collective-permute-start.23 = (bf16[48,1024]{1,0:T(8,128)(2,1)S(1)}, bf16[48,1024]{1,0:T(8,128)(2,1)S(1)}, u32[]{:S(2)}, u32[]{:S(2)}) collective-permute-start(bf16[48,1024]{1,0:T(8,128)(2,1)S(1)} %collective-permute-done.21.h1), channel_id=1, source_target_pairs={{0,1},{1,0},{2,3},{3,2},{4,5},{5,4},{6,7},{7,6},{8,9},{9,8},{10,11... | collective-permute-start | bytes 294920 | tf_op jit(solution)/shard_map/contract/ppermute | solution.py:195
  107.5 1.5 %copy-start.3 = (bf16[1,1024,896]{2,1,0:T(8,128)(2,1)S(1)}, bf16[1,1024,896]{2,1,0:T(8,128)(2,1)}, u32[]{:S(2)}) copy-start(bf16[1,1024,896]{2,1,0:T(8,128)(2,1)} %param.23) | copy-start | bytes 5505028
  110.2 6.1 %collective-permute-start.24 = (bf16[48,896]{1,0:T(8,128)(2,1)S(1)}, bf16[48,896]{1,0:T(8,128)(2,1)S(1)}, u32[]{:S(2)}, u32[]{:S(2)}) collective-permute-start(bf16[48,896]{1,0:T(8,128)(2,1)S(1)} %get-tuple-element.26), channel_id=1, source_target_pairs={{0,12},{4,0},{8,4},{12,8},{1,13},{5,1},{9,5},{13,9},{2,14},{6,2},{... | collective-permute-start | bytes 258056 | tf_op jit(solution)/shard_map/combine/ppermute | solution.py:192
  113.4 8.4 %collective-permute-start.25 = (bf16[48,896]{1,0:T(8,128)(2,1)S(1)}, bf16[48,896]{1,0:T(8,128)(2,1)S(1)}, u32[]{:S(2)}, u32[]{:S(2)}) collective-permute-start(bf16[48,896]{1,0:T(8,128)(2,1)S(1)} %get-tuple-element.27), channel_id=1, source_target_pairs={{0,8},{4,12},{8,0},{12,4},{1,9},{5,13},{9,1},{13,5},{2,10},{6,14},... | collective-permute-start | bytes 258056 | tf_op jit(solution)/shard_map/combine/ppermute | solution.py:192
  113.4 8.4 %collective-permute-start.26 = (bf16[48,896]{1,0:T(8,128)(2,1)S(1)}, bf16[48,896]{1,0:T(8,128)(2,1)S(1)}, u32[]{:S(2)}, u32[]{:S(2)}) collective-permute-start(bf16[48,896]{1,0:T(8,128)(2,1)S(1)} %get-tuple-element.28), channel_id=1, source_target_pairs={{0,4},{4,8},{8,12},{12,0},{1,5},{5,9},{9,13},{13,1},{2,6},{6,10},{... | collective-permute-start | bytes 258056 | tf_op jit(solution)/shard_map/combine/ppermute | solution.py:192

commit v2 on v1

--- a/solution.py
+++ b/solution.py
@@ -39,40 +39,51 @@
     return jax.ShapeDtypeStruct(dims, dtype)
 
 
-def attend_kernel(scale, group, rel_ref, q_ref, own_ref, *refs):
-    keys, vup_ref, out_ref = refs[:-2], refs[-2], refs[-1]
-    rows, latent = own_ref.shape[0], vup_ref.shape[1]
-    heads, vhead = vup_ref.shape[0], vup_ref.shape[2]
-    blocks = [keys[0][...]]
-    for k in range(1, len(keys), 2):
-        blocks.append(jnp.concatenate([keys[k][...], keys[k + 1][...]], axis=0))
+def attend_rows(scale, q, own, caches, wanted, rel, latent):
+    rows, many = own.shape[0], q.shape[0]
+    lane = lax.broadcasted_iota(jnp.int32, (many, rows), 1)
+    line = lax.broadcasted_iota(jnp.int32, (many, rows), 0) % rows
+    score = dot(q, caches[0])
+    for cache, k in zip(caches[1:], wanted[1:]):
+        score = jnp.where(rel == k, dot(q, cache), score)
+    score = score * scale
+    own_score = jnp.where(lane == line, dot_t(q, own) * scale, -1e30)
+    top = jnp.maximum(
+        jnp.max(score, axis=1, keepdims=True), jnp.max(own_score, axis=1, keepdims=True)
+    )
+    expo = jnp.exp(score - top)
+    own_e = jnp.exp(own_score - top)
+    total = jnp.sum(expo, axis=1, keepdims=True) + jnp.sum(own_e, axis=1, keepdims=True)
+    inverse = 1.0 / total
+    probs = expo * inverse
+    acc = dot((own_e * inverse).astype(BF16), own[:, :latent])
+    for cache, k in zip(caches, wanted):
+        part = jnp.where(rel == k, probs, 0.0).astype(BF16)
+        acc = acc + dot_t(part, cache[:latent])
+    return acc
+
+
+def attend_kernel(scale, group, bits_ref, rel_ref, q_ref, own_ref, *refs):
+    near_ref, far, (vup_ref, out_ref, held) = refs[0], refs[1:-3], refs[-3:]
+    rows = own_ref.shape[0]
+    latent, vhead = vup_ref.shape[1:]
+    half = far[0].shape[0]
+    start = pl.multiple_of(bits_ref[0] * half, 16)
+    other = pl.multiple_of((1 - bits_ref[0]) * half, 16)
+    caches = [near_ref[...]]
+    for k in range(len(far) // 2):
+        held[k, pl.ds(start, half), :] = far[2 * k][...]
+        held[k, pl.ds(other, half), :] = far[2 * k + 1][...]
+        caches.append(held[k])
+    rel = jnp.concatenate([rel_ref[...]] * group, axis=0)
     own = own_ref[...]
-    rel = jnp.concatenate([rel_ref[...]] * group, axis=0)
-    lane = lax.broadcasted_iota(jnp.int32, (rows * group, rows), 1)
-    line = lax.broadcasted_iota(jnp.int32, (rows * group, rows), 0) % rows
-    for first in range(0, heads, group):
+    for first in range(0, vup_ref.shape[0], group):
         q = q_ref[first * rows : (first + group) * rows, :]
-        score = dot_t(q, blocks[0])
-        for k in range(1, len(blocks)):
-            score = jnp.where(rel == k, dot_t(q, blocks[k]), score)
-        score = score * scale
-        own_score = jnp.where(lane == line, dot_t(q, own) * scale, -1e30)
-        top = jnp.maximum(
-            jnp.max(score, axis=1, keepdims=True), jnp.max(own_score, axis=1, keepdims=True)
-        )
-        expo = jnp.exp(score - top)
-        own_e = jnp.exp(own_score - top)
-        total = jnp.sum(expo, axis=1, keepdims=True) + jnp.sum(own_e, axis=1, keepdims=True)
-        inverse = 1.0 / total
-        probs = expo * inverse
-        acc = dot((own_e * inverse).astype(BF16), own[:, :latent])
-        for k in range(len(blocks)):
-            part = jnp.where(rel == k, probs, 0.0).astype(BF16)
-            acc = acc + dot(part, blocks[k][:, :latent])
-        acc = acc.astype(BF16)
+        acc = attend_rows(scale, q, own, caches, range(len(caches)), rel, latent).astype(BF16)
         for h in range(group):
             head = dot(acc[h * rows : (h + 1) * rows], vup_ref[first + h])
-            out_ref[:, (first + h) * vhead : (first + h + 1) * vhead] = head.astype(BF16)
+            at = (first + h) * vhead
+            out_ref[:, at : at + vhead] = head.astype(BF16)
 
 
 def split_store(flag, value, keep_ref, send_ref):
@@ -89,13 +100,25 @@
         send_ref[...] = value[:half].astype(send_ref.dtype)
 
 
-def project_kernel(bits_ref, h0, h1, h2, h3, w_ref, keep_ref, send_ref):
-    rows = jnp.concatenate([h0[...], h1[...], h2[...], h3[...]], axis=0)
-    split_store(bits_ref[0], dot(rows, w_ref[...]), keep_ref, send_ref)
+def project_kernel(bits_ref, h0, h1, h2, h3, w_ref, keep_ref, send_ref, held):
+    rows = h0.shape[0]
+    for i, head in enumerate((h0, h1, h2, h3)):
+        shard = bits_ref[2] ^ i
+        position = 2 * (shard % 2) + shard // 2
+        held[pl.ds(pl.multiple_of(position * rows, 16), rows), :] = head[...]
+    split_store(bits_ref[0], dot(held[...], w_ref[...]), keep_ref, send_ref)
 
 
 def halve_kernel(bits_ref, kept_ref, got_ref, keep_ref, send_ref):
     split_store(bits_ref[1], kept_ref[...] + got_ref[...].astype(F32), keep_ref, send_ref)
+
+
+def resid_kernel(kept_ref, got_ref, given_ref, pick_ref, resid_ref, *outs):
+    resid = kept_ref[...] + got_ref[...].astype(F32) + given_ref[...].astype(F32)
+    resid = resid.astype(BF16)
+    resid_ref[...] = resid
+    for k, out in enumerate(outs):
+        out[...] = dot(pick_ref[k], resid).astype(BF16)
 
 
 def pieces(value):
@@ -106,12 +129,8 @@
     return jnp.where(lane == 0, high, jnp.where(lane == 1, middle, rest))
 
 
-def expand_kernel(bits_ref, pick_ref, a0, a1, a2, a3, gain_ref, gate_ref, up_ref, keep_ref, send_ref):
-    slots = pick_ref.shape[0] // 4
-    taken = [
-        dot(pick_ref[k * slots : (k + 1) * slots, :], a[...]) for k, a in enumerate((a0, a1, a2, a3))
-    ]
-    rows = jnp.concatenate(taken, axis=0)
+def expand_kernel(bits_ref, a0, a1, gain_ref, gate_ref, up_ref, keep_ref, send_ref):
+    rows = jnp.concatenate([a0[...], a1[...]], axis=0).astype(F32)
     squares = jnp.sum(rows * rows, axis=1, keepdims=True)
     scaled = (rows * gain_ref[...].astype(F32)).astype(BF16)
     full = jnp.concatenate(
@@ -120,12 +139,13 @@
     split_store(bits_ref[0], full, keep_ref, send_ref)
 
 
-def halve_expand_kernel(bits_ref, kept_ref, got_ref, keep_ref, send_ref):
+def add_expand_kernel(kept_ref, got_ref, total_ref, send_ref):
     width = kept_ref.shape[1] - 128
     total = kept_ref[...].astype(F32) + got_ref[...].astype(F32)
     squares = jnp.sum(total[:, width:], axis=1, keepdims=True)
     total = jnp.concatenate([total[:, :width], pieces(squares)], axis=1)
-    split_store(bits_ref[1], total, keep_ref, send_ref)
+    total_ref[...] = total
+    send_ref[...] = total.astype(BF16)
 
 
 def hidden_kernel(features, kept_ref, got_ref, out_ref):
@@ -138,14 +158,13 @@
     out_ref[...] = (gate / (1.0 + jnp.exp(-gate)) * up).astype(BF16)
 
 
-def contract_kernel(bits_ref, h0, h1, h2, h3, w_ref, o0, o1, o2, o3, held):
-    slots = h0.shape[0]
-    rows = jnp.concatenate([h0[...], h1[...], h2[...], h3[...]], axis=0)
-    held[...] = dot(rows, w_ref[...]).astype(BF16)
-    mine = 2 * bits_ref[0] + bits_ref[1]
-    for k, out in enumerate((o0, o1, o2, o3)):
-        start = pl.multiple_of((mine ^ k) * slots, 16)
-        out[...] = held[pl.ds(start, slots), :]
+def contract_kernel(bits_ref, mine_ref, other_ref, w_ref, first_ref, second_ref, held):
+    slots = mine_ref.shape[0]
+    held[pl.ds(pl.multiple_of(bits_ref[0] * slots, 16), slots), :] = mine_ref[...]
+    held[pl.ds(pl.multiple_of((1 - bits_ref[0]) * slots, 16), slots), :] = other_ref[...]
+    result = dot(held[...], w_ref[...]).astype(BF16)
+    first_ref[...] = result[:slots]
+    second_ref[...] = result[slots:]
 
 
 def combine_kernel(put_ref, weight_ref, resid_ref, r0, r1, r2, r3, out_ref):
@@ -186,59 +205,67 @@
     scale = (vhead + key_width - latent) ** (-0.5)
     shard = lax.axis_index("expert")
     tensor = lax.axis_index("tensor")
-    bits = jnp.stack([tensor % 2, tensor // 2]).astype(jnp.int32)
+    bits = jnp.stack([tensor % 2, tensor // 2, shard]).astype(jnp.int32)
+
+    def across(value, mask):
+        return lax.ppermute(value, "expert", [(i, i ^ mask) for i in range(count)])
+
+    def swap(value, mask):
+        return lax.ppermute(value, "tensor", [(i, i ^ mask) for i in range(count)])
+
+    def both(value, target):
+        pairs = [(e * count + t, target(e, t)) for e in range(count) for t in range(count)]
+        return lax.ppermute(value, ("expert", "tensor"), pairs)
 
     def along(value, k):
         return lax.ppermute(value, "expert", [(i, (i + k) % count) for i in range(count)])
 
-    def swap(value, mask):
-        return lax.ppermute(value, "tensor", [(i, i ^ mask) for i in range(count)])
-
-    def place(t):
-        return 2 * (t % 2) + t // 2
-
-    def target(e, t, k):
-        return ((e - place(t) + k) % count) * count + e
-
-    cells = [(e, t) for e in range(count) for t in range(count)]
+    def transposed(value):
+        return both(value, lambda e, t: t * count + e)
+
+    def gather(value):
+        second = across(value, 2)
+        return [value, across(value, 1), second, across(second, 1)]
 
     with jax.named_scope("gather_cache"):
-        half = lax.dynamic_slice_in_dim(prompt_cache, (tensor % 2) * (prompt // 2), prompt // 2, 0)
-        keys = [prompt_cache]
+        cache = prompt_cache.T
+        size = key_width // 2
+        half = lax.dynamic_slice_in_dim(cache, (tensor % 2) * size, size, 0)
+        keys = [cache]
         for k in range(1, count):
             got = along(half, k)
             keys += [got, swap(got, 1)]
-    with jax.named_scope("residual_to_columns"):
-        resid_cols = lax.ppermute(
-            residual_in, ("expert", "tensor"), [(target(e, t, 0), e * count + t) for e, t in cells]
-        )
+    with jax.named_scope("query_layout"):
+        q = queries.reshape(rows, heads, key_width).transpose(1, 0, 2)
+        q = q.reshape(heads * rows, key_width)
+    with jax.named_scope("early"):
+        ids, q = lax.optimization_barrier((expert_ids, q))
+        ids = transposed(ids)
     with jax.named_scope("routing"):
-        ids = [expert_ids] + [along(expert_ids, k) for k in range(1, count)]
-        chosen = jnp.any(jnp.stack(ids) == shard, axis=2)
+        step = jnp.arange(count, dtype=jnp.int32)
         slot = jnp.arange(slots, dtype=jnp.int32)
+        chosen = jnp.any(ids[None] == ((tensor + step) % count)[:, None, None], axis=2)
         pick = chosen[:, None, :] & (ranks(chosen)[:, None, :] == slot[None, :, None])
-        pick = pick.astype(BF16).reshape(count * slots, rows)
-        experts = (shard + jnp.arange(count, dtype=jnp.int32)) % count
-        named = expert_ids[None, :, :] == experts[:, None, None]
+        pick = pick.astype(BF16)
+        named = expert_ids[None] == ((shard + step) % count)[:, None, None]
         mine = jnp.any(named, axis=2)
         put = mine[:, :, None] & (ranks(mine)[:, :, None] == slot[None, None, :])
         put = put.astype(BF16)
         weights = jnp.sum(jnp.where(named, route_weight[None], 0.0), axis=2).T
         rel = (shard - row_dest) % count
-    with jax.named_scope("query_layout"):
-        q = queries.reshape(rows, heads, key_width).transpose(1, 0, 2)
-        q = q.reshape(heads * rows, key_width)
     with jax.named_scope("attend"):
         group = 4
+        q, pick, put, weights = lax.optimization_barrier((q, pick, put, weights))
         (head_out,) = call(
             functools.partial(attend_kernel, scale, group),
             [shape((rows, heads * vhead), BF16)],
-            [VMEM] * (4 + len(keys)),
-            (rel, q, own_latent, *keys, value_up),
+            [SMEM] + [VMEM] * (4 + len(keys)),
+            (bits, rel, q, own_latent, *keys, value_up),
             2 * heads * rows * count * prompt * (key_width + latent),
+            [pltpu.VMEM((count - 1, key_width, prompt), BF16)],
         )
     with jax.named_scope("gather_heads"):
-        gathered = [head_out] + [along(head_out, k) for k in range(1, count)]
+        gathered = gather(head_out)
     with jax.named_scope("project"):
         kept, sent = call(
             project_kernel,
@@ -246,7 +273,10 @@
             [SMEM] + [VMEM] * 5,
             (bits, *gathered, out_proj),
             2 * count * rows * heads * vhead * width,
+            [pltpu.VMEM((count * rows, heads * vhead), BF16)],
         )
+        given, sent = lax.optimization_barrier((residual_in, sent))
+        given = transposed(given)
         kept, sent = call(
             halve_kernel,
             [shape((rows, width), F32), shape((rows, width), BF16)],
@@ -254,54 +284,63 @@
             (bits, kept, swap(sent, 1)),
             2 * rows * width,
         )
-        resid = (kept + swap(sent, 2).astype(F32) + resid_cols.astype(F32)).astype(BF16)
+        resid, *picked = call(
+            resid_kernel,
+            [shape((rows, width), BF16)] + [shape((slots, width), BF16)] * count,
+            [VMEM] * 4,
+            (kept, swap(sent, 2), given, pick),
+            2 * count * rows * slots * width,
+        )
     with jax.named_scope("scatter_resid"):
         arrived = [
-            lax.ppermute(
-                resid, ("expert", "tensor"), [(e * count + t, target(e, t, k)) for e, t in cells]
+            both(picked[k], lambda e, t, k=k: (t + k) % count * count + e) for k in range(count)
+        ]
+    wide = 2 * ff + 128
+    outs = []
+    for first in range(0, count, 2):
+        with jax.named_scope("expand"):
+            kept, sent = call(
+                expand_kernel,
+                [shape((slots, wide), BF16), shape((slots, wide), BF16)],
+                [SMEM] + [VMEM] * 5,
+                (bits, *arrived[first : first + 2], norm_gain[None, :], gate_weight[0], up_weight[0]),
+                8 * slots * width * ff,
             )
-            for k in range(count)
-        ]
-    with jax.named_scope("expand"):
-        wide = 2 * ff + 128
-        kept, sent = call(
-            expand_kernel,
-            [shape((2 * slots, wide), BF16), shape((2 * slots, wide), BF16)],
-            [SMEM] + [VMEM] * 8,
-            (bits, pick, *arrived, norm_gain[None, :], gate_weight[0], up_weight[0]),
-            4 * count * slots * width * ff,
-        )
-        kept, sent = call(
-            halve_expand_kernel,
-            [shape((slots, wide), F32), shape((slots, wide), BF16)],
-            [SMEM, VMEM, VMEM],
-            (bits, kept, swap(sent, 1)),
-            2 * slots * wide,
-        )
-        (hidden,) = call(
-            functools.partial(hidden_kernel, width * count),
-            [shape((slots, ff), BF16)],
-            [VMEM, VMEM],
-            (kept, swap(sent, 2)),
-            8 * slots * wide,
-        )
-    with jax.named_scope("contract"):
-        across = swap(hidden, 2)
-        outs = call(
-            contract_kernel,
-            [shape((slots, width), BF16)] * count,
-            [SMEM] + [VMEM] * 5,
-            (bits, hidden, across, swap(hidden, 1), swap(across, 1), down_weight[0]),
-            2 * count * slots * width * ff,
-            [pltpu.VMEM((count * slots, width), BF16)],
-        )
+            kept, sent = call(
+                add_expand_kernel,
+                [shape((slots, wide), F32), shape((slots, wide), BF16)],
+                [VMEM, VMEM],
+                (kept, swap(sent, 1)),
+                2 * slots * wide,
+            )
+            got = swap(sent, 2)
+            if first == 0:
+                resid, _ = lax.optimization_barrier((resid, sent))
+                resid = transposed(resid)
+                resid, got = lax.optimization_barrier((resid, got))
+            (hidden,) = call(
+                functools.partial(hidden_kernel, width * count),
+                [shape((slots, ff), BF16)],
+                [VMEM, VMEM],
+                (kept, got),
+                8 * slots * wide,
+            )
+        with jax.named_scope("contract"):
+            outs += call(
+                contract_kernel,
+                [shape((slots, width), BF16)] * 2,
+                [SMEM] + [VMEM] * 3,
+                (bits, hidden, swap(hidden, 1), down_weight[0]),
+                4 * slots * width * ff,
+                [pltpu.VMEM((2 * slots, ff), BF16)],
+            )
     with jax.named_scope("combine"):
         back = [outs[0]] + [along(outs[k], -k) for k in range(1, count)]
         (scored,) = call(
             combine_kernel,
             [shape((rows, width), BF16)],
             [VMEM] * 7,
-            (put, weights, arrived[0], *back),
+            (put, weights, resid, *back),
             2 * count * rows * slots * width,
         )
     return scored

time: 123 us -> 110 us (0.89)
  waiting for transfers between devices: 50.7 us -> 44 us
  starting transfers between devices: 46 us -> 42.6 us
  local copies, waits for them, and re-layouts: 9.17 us -> 6.39 us
    ppermute x12 -> x6, waiting for transfers between devices: 35.5 us -> 7.78 us  [along(): lax.ppermute(value, 'expert', [(i, (i + k) % count) for i in range(count)])]
    ppermute x5 -> x10, waiting for transfers between devices: 2.21 us -> 20.8 us  [the longest x3 20.1 us: across(): return lax.ppermute(value, 'expert', [(i, i ^ mask) for i in range(count)])]
    ppermute x12 -> x6, starting transfers between devices: 19.6 us -> 11.4 us  [along(): lax.ppermute(value, 'expert', [(i, (i + k) % count) for i in range(count)])]
    unnamed x21 -> x24, local copies, waits for them, and re-layouts: 6.23 us -> 1.99 us
    ppermute x10 -> x11, starting transfers between devices: 12.3 us -> 14.9 us  [swap(): return lax.ppermute(value, 'tensor', [(i, i ^ mask) for i in range(count)])]
    ppermute x10 -> x11, waiting for transfers between devices: 13 us -> 15.5 us  [swap(): return lax.ppermute(value, 'tensor', [(i, i ^ mask) for i in range(count)])]
    ppermute x5 -> x10, starting transfers between devices: 14 us -> 16.3 us  [the longest x7 11 us: both(): return lax.ppermute(value, ('expert', 'tensor'), pairs)]
    dynamic_slice x1, local copies, waits for them, and re-layouts: 0.02 us -> 1.57 us  [square(): half = lax.dynamic_slice_in_dim(cache, tensor % 2 * size, size, 0)]
  transfers between devices with their start and end apart: 27 -> 27, of which waited for: 16 -> 13; matrix products, arithmetic and copies ran while one was open for 4% -> 4% of each run, Pallas kernels for 1% -> 5%
where the time goes in v2:
time: 110 us; the launch traced here: 109 us
  waiting for transfers between devices  44 us (40%)
  starting transfers between devices  42.6 us (39%)
  Pallas kernels  15 us (14%)
  local copies, waits for them, and re-layouts  6.39 us (6%)
    ppermute x3, waiting for transfers between devices, across(): return lax.ppermute(value, 'expert', [(i, i ^ mask) for i in range(count)])  20.1 us
    ppermute x11, waiting for transfers between devices, swap(): return lax.ppermute(value, 'tensor', [(i, i ^ mask) for i in range(count)])  15.5 us
    pallas_call x13, Pallas kernels, call(): pl.pallas_call(kernel, out_shape=outs, in_specs=specs, out_specs=[VMEM] *...  15 us
    ppermute x11, starting transfers between devices, swap(): return lax.ppermute(value, 'tensor', [(i, i ^ mask) for i in range(count)])  14.9 us
    ppermute x6, starting transfers between devices, along(): lax.ppermute(value, 'expert', [(i, (i + k) % count) for i in range(count)])  11.4 us
    ppermute x7, starting transfers between devices, both(): return lax.ppermute(value, ('expert', 'tensor'), pairs)  11 us
    ppermute x6, waiting for transfers between devices, along(): lax.ppermute(value, 'expert', [(i, (i + k) % count) for i in range(count)])  7.78 us
    ppermute x3, starting transfers between devices, across(): return lax.ppermute(value, 'expert', [(i, i ^ mask) for i in range(count)])  5.35 us
  transfers between devices with their start and end apart: 27, of which 13 were waited for; matrix products, arithmetic and copies ran while one was open for 4% of the time, Pallas kernels for 5%

profile of v2, /device:TPU:0, one launch (start us, length us, event | category | flops | bytes accessed | tf_op | source)
XLA Modules:
  0.0 109.4 jit_solution(12229647760864074249)
XLA Ops:
  0.0 1.6 %dynamic-slice_bitcast_fusion = bf16[288,256]{1,0:T(8,128)(2,1)} fusion(bf16[256,576]{0,1:T(8,128)(2,1)} %param.17, s32[]{:T(128)S(6)} %select_n.50), kind=kLoop, calls=%fused_computation | loop fusion | bytes 294916 | tf_op jit(solution)/shard_map/gather_cache/dynamic_slice | solution.py:233
  1.6 3.0 %collective-permute-start.1 = (bf16[288,256]{1,0:T(8,128)(2,1)}, bf16[288,256]{1,0:T(8,128)(2,1)S(1)}, u32[]{:S(2)}, u32[]{:S(2)}) collective-permute-start(bf16[288,256]{1,0:T(8,128)(2,1)} %dynamic-slice_bitcast_fusion), channel_id=1, source_target_pairs={{0,4},{4,8},{8,12},{12,0},{1,5},{5,9},{9,13},{13,1},{2,6},{6,10},{... | collective-permute-start | bytes 442376 | tf_op jit(solution)/shard_map/gather_cache/ppermute | solution.py:221
  4.6 2.6 %collective-permute-start.3 = (bf16[288,256]{1,0:T(8,128)(2,1)}, bf16[288,256]{1,0:T(8,128)(2,1)S(1)}, u32[]{:S(2)}, u32[]{:S(2)}) collective-permute-start(bf16[288,256]{1,0:T(8,128)(2,1)} %dynamic-slice_bitcast_fusion), channel_id=1, source_target_pairs={{0,8},{4,12},{8,0},{12,4},{1,9},{5,13},{9,1},{13,5},{2,10},{6,14},... | collective-permute-start | bytes 442376 | tf_op jit(solution)/shard_map/gather_cache/ppermute | solution.py:221
  7.2 1.3 %collective-permute-start.5 = (bf16[288,256]{1,0:T(8,128)(2,1)}, bf16[288,256]{1,0:T(8,128)(2,1)S(1)}, u32[]{:S(2)}, u32[]{:S(2)}) collective-permute-start(bf16[288,256]{1,0:T(8,128)(2,1)} %dynamic-slice_bitcast_fusion), channel_id=1, source_target_pairs={{0,12},{4,0},{8,4},{12,8},{1,13},{5,1},{9,5},{13,9},{2,14},{6,2},{... | collective-permute-start | bytes 442376 | tf_op jit(solution)/shard_map/gather_cache/ppermute | solution.py:221
  8.5 2.2 %reshape.65 = bf16[64,16,576]{2,1,0:T(8,128)(2,1)S(1)} reshape(bf16[64,9216]{1,0:T(8,128)(2,1)} %param.13) | data formatting | bytes 2359296 | tf_op jit(solution)/shard_map/query_layout/reshape | solution.py:239
  10.8 0.3 copy.32
  11.1 0.3 copy-done.7
  11.5 0.6 collective-permute-start
  12.2 0.2 reduce_window_sum.18
  13.5 2.7 %collective-permute-start.2 = (bf16[288,256]{1,0:T(8,128)(2,1)S(1)}, bf16[288,256]{1,0:T(8,128)(2,1)S(1)}, u32[]{:S(2)}, u32[]{:S(2)}) collective-permute-start(bf16[288,256]{1,0:T(8,128)(2,1)S(1)} %collective-permute-done.1.refs_1_), channel_id=1, source_target_pairs={{0,1},{1,0},{2,3},{3,2},{4,5},{5,4},{6,7},{7,6},{8,9},{9,8},{10,11... | collective-permute-start | bytes 442376 | tf_op jit(solution)/shard_map/gather_cache/ppermute | solution.py:214
  16.2 0.9 collective-permute-done.3.refs_3_
  17.1 0.5 collective-permute-start.6
  17.7 0.8 collective-permute-done.4.refs_4_
  18.7 1.6 %copy-done.5 = bf16[16,512,128]{2,1,0:T(8,128)(2,1)S(1)} copy-done((bf16[16,512,128]{2,1,0:T(8,128)(2,1)S(1)}, bf16[16,512,128]{2,1,0:T(8,128)(2,1)}, u32[]{:S(2)}) %copy-start.5) | copy-done | bytes 2097176
  20.3 6.0 %attend.1.h0 = bf16[64,2048]{1,0:T(8,128)(2,1)S(1)} custom-call(s32[3]{0:T(128)S(1)} %pad_add_fusion.bits_ref, s32[64,1]{1,0:T(8,128)S(1)} %add_select_fusion.rel_ref, bf16[1024,576]{1,0:T(8,128)(2,1)S(1)} %bitcast.19, bf16[64,576]{1,0:T(8,128)(2,1)S(1)} %copy-done.6, bf16[576,256]{1,0:T(8,128)(2,1)S(1)} %bitcast.21, ...), custom_call_target="tpu_custom_call" | custom-call | flops 2281701376 | bytes 4792588 | tf_op jit(solution)/shard_map/attend/pallas_call | solution.py:27
  26.3 5.0 %collective-permute-start.8 = (bf16[64,2048]{1,0:T(8,128)(2,1)S(1)}, bf16[64,2048]{1,0:T(8,128)(2,1)S(1)}, u32[]{:S(2)}, u32[]{:S(2)}) collective-permute-start(bf16[64,2048]{1,0:T(8,128)(2,1)S(1)} %attend.1.h0), channel_id=1, source_target_pairs={{0,8},{4,12},{8,0},{12,4},{1,9},{5,13},{9,1},{13,5},{2,10},{6,14},... | collective-permute-start | bytes 786440 | tf_op jit(solution)/shard_map/gather_heads/ppermute | solution.py:211
  31.3 0.3 collective-permute-start.7
  31.6 12.2 %collective-permute-done.8.h2 = bf16[64,2048]{1,0:T(8,128)(2,1)S(1)} collective-permute-done((bf16[64,2048]{1,0:T(8,128)(2,1)S(1)}, bf16[64,2048]{1,0:T(8,128)(2,1)S(1)}, u32[]{:S(2)}, u32[]{:S(2)}) %collective-permute-start.8) | collective-permute-done | bytes 262176 | tf_op jit(solution)/shard_map/gather_heads/ppermute | solution.py:211
  43.9 0.8 collective-permute-done.7.h1
  44.7 7.1 %collective-permute-done.9.h3 = bf16[64,2048]{1,0:T(8,128)(2,1)S(1)} collective-permute-done((bf16[64,2048]{1,0:T(8,128)(2,1)S(1)}, bf16[64,2048]{1,0:T(8,128)(2,1)S(1)}, u32[]{:S(2)}, u32[]{:S(2)}) %collective-permute-start.9) | collective-permute-done | bytes 262176 | tf_op jit(solution)/shard_map/gather_heads/ppermute | solution.py:211
  51.8 1.9 %project.3 = (f32[128,896]{1,0:T(8,128)S(1)}, bf16[128,896]{1,0:T(8,128)(2,1)S(1)}) custom-call(s32[3]{0:T(128)S(1)} %pad_add_fusion.bits_ref, bf16[64,2048]{1,0:T(8,128)(2,1)S(1)} %attend.1.h0, bf16[64,2048]{1,0:T(8,128)(2,1)S(1)} %collective-permute-done.7.h1, bf16[64,2048]{1,0:T(8,128)(2,1)S(1)} %collective-permute-done.8.h2, ...), custom_call_target="tpu_custom_call" | custom-call | flops 939524096 | bytes 5406732 | tf_op jit(solution)/shard_map/project/pallas_call | solution.py:27
  53.8 0.7 collective-permute-start.12
  54.5 0.8 collective-permute-done.10.got_ref
  55.2 0.6 project.4
  55.9 3.5 %collective-permute-start.11 = (bf16[64,896]{1,0:T(8,128)(2,1)S(1)}, bf16[64,896]{1,0:T(8,128)(2,1)S(1)}, u32[]{:S(2)}, u32[]{:S(2)}) collective-permute-start(bf16[64,896]{1,0:T(8,128)(2,1)S(1)} %get-tuple-element.46), channel_id=1, source_target_pairs={{0,2},{1,3},{2,0},{3,1},{4,6},{5,7},{6,4},{7,5},{8,10},{9,11},{10,... | collective-permute-start | bytes 344072 | tf_op jit(solution)/shard_map/project/ppermute | solution.py:214
  59.4 5.7 %collective-permute-done.11.got_ref = bf16[64,896]{1,0:T(8,128)(2,1)S(1)} collective-permute-done((bf16[64,896]{1,0:T(8,128)(2,1)S(1)}, bf16[64,896]{1,0:T(8,128)(2,1)S(1)}, u32[]{:S(2)}, u32[]{:S(2)}) %collective-permute-start.11) | collective-permute-done | bytes 114720 | tf_op jit(solution)/shard_map/project/ppermute | solution.py:214
  65.1 0.3 project.5
  65.4 0.7 collective-permute-start.13
  66.0 1.5 %collective-permute-start.14 = (bf16[48,896]{1,0:T(8,128)(2,1)S(1)}, bf16[48,896]{1,0:T(8,128)(2,1)S(1)}, u32[]{:S(2)}, u32[]{:S(2)}) collective-permute-start(bf16[48,896]{1,0:T(8,128)(2,1)S(1)} %get-tuple-element.51), channel_id=1, source_target_pairs={{0,4},{1,8},{2,12},{3,0},{4,5},{5,9},{6,13},{7,1},{8,6},{9,10},{10... | collective-permute-start | bytes 258056 | tf_op jit(solution)/shard_map/scatter_resid/ppermute | solution.py:218
  67.5 4.7 %collective-permute-start.20 = (bf16[48,896]{1,0:T(8,128)(2,1)S(1)}, bf16[48,896]{1,0:T(8,128)(2,1)S(1)}, u32[]{:S(2)}, u32[]{:S(2)}) collective-permute-start(bf16[48,896]{1,0:T(8,128)(2,1)S(1)} %get-tuple-element.61), channel_id=1, source_target_pairs={{0,8},{1,12},{2,0},{3,4},{4,9},{5,13},{6,1},{7,5},{8,10},{9,14},{1... | collective-permute-start | bytes 258056 | tf_op jit(solution)/shard_map/scatter_resid/ppermute | solution.py:218
  72.2 2.1 %collective-permute-start.21 = (bf16[48,896]{1,0:T(8,128)(2,1)S(1)}, bf16[48,896]{1,0:T(8,128)(2,1)S(1)}, u32[]{:S(2)}, u32[]{:S(2)}) collective-permute-start(bf16[48,896]{1,0:T(8,128)(2,1)S(1)} %get-tuple-element.62), channel_id=1, source_target_pairs={{0,12},{1,0},{2,4},{3,8},{4,13},{5,1},{6,5},{7,9},{8,14},{9,2},{10... | collective-permute-start | bytes 258056 | tf_op jit(solution)/shard_map/scatter_resid/ppermute | solution.py:218
  74.4 1.3 %expand.6 = (bf16[48,2176]{1,0:T(8,128)(2,1)S(1)}, bf16[48,2176]{1,0:T(8,128)(2,1)S(1)}) custom-call(s32[3]{0:T(128)S(1)} %pad_add_fusion.bits_ref, bf16[48,896]{1,0:T(8,128)(2,1)S(1)} %collective-permute-done.13.a0, bf16[48,896]{1,0:T(8,128)(2,1)S(1)} %collective-permute-done.14.a1, bf16[1,896]{1,0:T(2,128)(2,1)S(1)} %broadcast_in_dim.12.gain_ref, ...), custom_call_target="tpu_custom_call" | custom-call | flops 352321536 | bytes 4261644 | tf_op jit(solution)/shard_map/expand/pallas_call | solution.py:27
  75.8 0.6 collective-permute-done.21.a1
  76.5 1.3 %expand.9 = (bf16[48,2176]{1,0:T(8,128)(2,1)S(1)}, bf16[48,2176]{1,0:T(8,128)(2,1)S(1)}) custom-call(s32[3]{0:T(128)S(1)} %pad_add_fusion.bits_ref, bf16[48,896]{1,0:T(8,128)(2,1)S(1)} %collective-permute-done.20.a0, bf16[48,896]{1,0:T(8,128)(2,1)S(1)} %collective-permute-done.21.a1, bf16[1,896]{1,0:T(2,128)(2,1)S(1)} %broadcast_in_dim.12.gain_ref, ...), custom_call_target="tpu_custom_call" | custom-call | flops 352321536 | bytes 4261644 | tf_op jit(solution)/shard_map/expand/pallas_call | solution.py:27
  77.8 2.3 %collective-permute-start.22 = (bf16[48,2176]{1,0:T(8,128)(2,1)S(1)}, bf16[48,2176]{1,0:T(8,128)(2,1)S(1)}, u32[]{:S(2)}, u32[]{:S(2)}) collective-permute-start(bf16[48,2176]{1,0:T(8,128)(2,1)S(1)} %get-tuple-element.64), channel_id=1, source_target_pairs={{0,1},{1,0},{2,3},{3,2},{4,5},{5,4},{6,7},{7,6},{8,9},{9,8},{10,11... | collective-permute-start | bytes 626696 | tf_op jit(solution)/shard_map/expand/ppermute | solution.py:214
  80.2 2.6 %collective-permute-start.17 = (bf16[48,2176]{1,0:T(8,128)(2,1)S(1)}, bf16[48,2176]{1,0:T(8,128)(2,1)S(1)}, u32[]{:S(2)}, u32[]{:S(2)}) collective-permute-start(bf16[48,2176]{1,0:T(8,128)(2,1)S(1)} %get-tuple-element.54), channel_id=1, source_target_pairs={{0,2},{1,3},{2,0},{3,1},{4,6},{5,7},{6,4},{7,5},{8,10},{9,11},{10,... | collective-permute-start | bytes 626696 | tf_op jit(solution)/shard_map/expand/ppermute | solution.py:214
  83.0 1.3 %collective-permute-start.23 = (bf16[48,2176]{1,0:T(8,128)(2,1)S(1)}, bf16[48,2176]{1,0:T(8,128)(2,1)S(1)}, u32[]{:S(2)}, u32[]{:S(2)}) collective-permute-start(bf16[48,2176]{1,0:T(8,128)(2,1)S(1)} %get-tuple-element.66), channel_id=1, source_target_pairs={{0,2},{1,3},{2,0},{3,1},{4,6},{5,7},{6,4},{7,5},{8,10},{9,11},{10,... | collective-permute-start | bytes 626696 | tf_op jit(solution)/shard_map/expand/ppermute | solution.py:214
  84.3 0.7 collective-permute-start.16
  85.0 3.9 %collective-permute-done.17.got_ref = bf16[48,2176]{1,0:T(8,128)(2,1)S(1)} collective-permute-done((bf16[48,2176]{1,0:T(8,128)(2,1)S(1)}, bf16[48,2176]{1,0:T(8,128)(2,1)S(1)}, u32[]{:S(2)}, u32[]{:S(2)}) %collective-permute-start.17) | collective-permute-done | bytes 208928 | tf_op jit(solution)/shard_map/expand/ppermute | solution.py:214
  89.1 1.8 %collective-permute-start.18 = (bf16[48,1024]{1,0:T(8,128)(2,1)S(1)}, bf16[48,1024]{1,0:T(8,128)(2,1)S(1)}, u32[]{:S(2)}, u32[]{:S(2)}) collective-permute-start(bf16[48,1024]{1,0:T(8,128)(2,1)S(1)} %expand.8.mine_ref), channel_id=1, source_target_pairs={{0,1},{1,0},{2,3},{3,2},{4,5},{5,4},{6,7},{7,6},{8,9},{9,8},{10,11... | collective-permute-start | bytes 294920 | tf_op jit(solution)/shard_map/contract/ppermute | solution.py:214
  90.9 4.1 %collective-permute-done.23.got_ref = bf16[48,2176]{1,0:T(8,128)(2,1)S(1)} collective-permute-done((bf16[48,2176]{1,0:T(8,128)(2,1)S(1)}, bf16[48,2176]{1,0:T(8,128)(2,1)S(1)}, u32[]{:S(2)}, u32[]{:S(2)}) %collective-permute-start.23) | collective-permute-done | bytes 208928 | tf_op jit(solution)/shard_map/expand/ppermute | solution.py:214
  95.2 1.0 contract.2
  96.2 3.6 %collective-permute-start.19 = (bf16[48,896]{1,0:T(8,128)(2,1)S(1)}, bf16[48,896]{1,0:T(8,128)(2,1)S(1)}, u32[]{:S(2)}, u32[]{:S(2)}) collective-permute-start(bf16[48,896]{1,0:T(8,128)(2,1)S(1)} %get-tuple-element.60), channel_id=1, source_target_pairs={{0,12},{4,0},{8,4},{12,8},{1,13},{5,1},{9,5},{13,9},{2,14},{6,2},{... | collective-permute-start | bytes 258056 | tf_op jit(solution)/shard_map/combine/ppermute | solution.py:221
  99.8 1.0 contract.3
  100.9 0.8 collective-permute-start.26
  101.6 1.1 collective-permute-done.19.r1
  102.7 5.8 %collective-permute-done.25.r2 = bf16[48,896]{1,0:T(8,128)(2,1)S(1)} collective-permute-done((bf16[48,896]{1,0:T(8,128)(2,1)S(1)}, bf16[48,896]{1,0:T(8,128)(2,1)S(1)}, u32[]{:S(2)}, u32[]{:S(2)}) %collective-permute-start.25) | collective-permute-done | bytes 86048 | tf_op jit(solution)/shard_map/combine/ppermute | solution.py:221
  108.5 0.9 combine.1
  (66 shorter events, 2.3 us)
Async XLA Ops:
  1.6 11.9 %collective-permute-start.1 = (bf16[288,256]{1,0:T(8,128)(2,1)}, bf16[288,256]{1,0:T(8,128)(2,1)S(1)}, u32[]{:S(2)}, u32[]{:S(2)}) collective-permute-start(bf16[288,256]{1,0:T(8,128)(2,1)} %dynamic-slice_bitcast_fusion), channel_id=1, source_target_pairs={{0,4},{4,8},{8,12},{12,0},{1,5},{5,9},{9,13},{13,1},{2,6},{6,10},{... | collective-permute-start | bytes 442376 | tf_op jit(solution)/shard_map/gather_cache/ppermute | solution.py:221
  4.6 12.5 %collective-permute-start.3 = (bf16[288,256]{1,0:T(8,128)(2,1)}, bf16[288,256]{1,0:T(8,128)(2,1)S(1)}, u32[]{:S(2)}, u32[]{:S(2)}) collective-permute-start(bf16[288,256]{1,0:T(8,128)(2,1)} %dynamic-slice_bitcast_fusion), channel_id=1, source_target_pairs={{0,8},{4,12},{8,0},{12,4},{1,9},{5,13},{9,1},{13,5},{2,10},{6,14},... | collective-permute-start | bytes 442376 | tf_op jit(solution)/shard_map/gather_cache/ppermute | solution.py:221
  7.2 9.9 %collective-permute-start.5 = (bf16[288,256]{1,0:T(8,128)(2,1)}, bf16[288,256]{1,0:T(8,128)(2,1)S(1)}, u32[]{:S(2)}, u32[]{:S(2)}) collective-permute-start(bf16[288,256]{1,0:T(8,128)(2,1)} %dynamic-slice_bitcast_fusion), channel_id=1, source_target_pairs={{0,12},{4,0},{8,4},{12,8},{1,13},{5,1},{9,5},{13,9},{2,14},{6,2},{... | collective-permute-start | bytes 442376 | tf_op jit(solution)/shard_map/gather_cache/ppermute | solution.py:221
  10.8 0.7 copy-start.7
  10.8 1.9 %copy-start.9 = (f32[64,2]{0,1:T(2,128)S(1)}, f32[64,2]{0,1:T(2,128)}, u32[]{:S(2)}) copy-start(f32[64,2]{0,1:T(2,128)} %param.25) | copy-start | bytes 1540
  10.8 1.9 %copy-start.10 = (s32[64,1]{0,1:T(1,128)S(1)}, s32[64,1]{0,1:T(1,128)}, u32[]{:S(2)}) copy-start(s32[64,1]{0,1:T(1,128)} %param.16) | copy-start | bytes 772
  10.8 7.9 %copy-start.4 = (bf16[256,576]{0,1:T(8,128)(2,1)S(1)}, bf16[256,576]{0,1:T(8,128)(2,1)}, u32[]{:S(2)}) copy-start(bf16[256,576]{0,1:T(8,128)(2,1)} %param.17) | copy-start | bytes 884740
  10.8 7.9 %copy-start.6 = (bf16[64,576]{1,0:T(8,128)(2,1)S(1)}, bf16[64,576]{1,0:T(8,128)(2,1)}, u32[]{:S(2)}) copy-start(bf16[64,576]{1,0:T(8,128)(2,1)} %own_ref.1) | copy-start | bytes 221188
  11.5 1.7 %collective-permute-start = (s32[64,2]{0,1:T(2,128)S(1)}, s32[64,2]{0,1:T(2,128)S(1)}, u32[]{:S(2)}, u32[]{:S(2)}) collective-permute-start(s32[64,2]{0,1:T(2,128)S(1)} %copy-done.7), channel_id=1, source_target_pairs={{0,0},{1,4},{2,8},{3,12},{4,1},{5,5},{6,9},{7,13},{8,2},{9,6},{10,... | collective-permute-start | bytes 1544 | tf_op jit(solution)/shard_map/early/ppermute | solution.py:218
  13.5 4.1 %collective-permute-start.2 = (bf16[288,256]{1,0:T(8,128)(2,1)S(1)}, bf16[288,256]{1,0:T(8,128)(2,1)S(1)}, u32[]{:S(2)}, u32[]{:S(2)}) collective-permute-start(bf16[288,256]{1,0:T(8,128)(2,1)S(1)} %collective-permute-done.1.refs_1_), channel_id=1, source_target_pairs={{0,1},{1,0},{2,3},{3,2},{4,5},{5,4},{6,7},{7,6},{8,9},{9,8},{10,11... | collective-permute-start | bytes 442376 | tf_op jit(solution)/shard_map/gather_cache/ppermute | solution.py:214
  17.1 1.4 %collective-permute-start.4 = (bf16[288,256]{1,0:T(8,128)(2,1)S(1)}, bf16[288,256]{1,0:T(8,128)(2,1)S(1)}, u32[]{:S(2)}, u32[]{:S(2)}) collective-permute-start(bf16[288,256]{1,0:T(8,128)(2,1)S(1)} %collective-permute-done.3.refs_3_), channel_id=1, source_target_pairs={{0,1},{1,0},{2,3},{3,2},{4,5},{5,4},{6,7},{7,6},{8,9},{9,8},{10,11... | collective-permute-start | bytes 442376 | tf_op jit(solution)/shard_map/gather_cache/ppermute | solution.py:214
  17.1 1.6 %collective-permute-start.6 = (bf16[288,256]{1,0:T(8,128)(2,1)S(1)}, bf16[288,256]{1,0:T(8,128)(2,1)S(1)}, u32[]{:S(2)}, u32[]{:S(2)}) collective-permute-start(bf16[288,256]{1,0:T(8,128)(2,1)S(1)} %collective-permute-done.5.refs_5_), channel_id=1, source_target_pairs={{0,1},{1,0},{2,3},{3,2},{4,5},{5,4},{6,7},{7,6},{8,9},{9,8},{10,11... | collective-permute-start | bytes 442376 | tf_op jit(solution)/shard_map/gather_cache/ppermute | solution.py:214
  18.7 1.6 %copy-start.5 = (bf16[16,512,128]{2,1,0:T(8,128)(2,1)S(1)}, bf16[16,512,128]{2,1,0:T(8,128)(2,1)}, u32[]{:S(2)}) copy-start(bf16[16,512,128]{2,1,0:T(8,128)(2,1)} %refs_7_.1) | copy-start | bytes 6291460
  20.3 31.5 %copy-start.3 = (bf16[2048,896]{1,0:T(8,128)(2,1)S(1)}, bf16[2048,896]{1,0:T(8,128)(2,1)}, u32[]{:S(2)}) copy-start(bf16[2048,896]{1,0:T(8,128)(2,1)} %w_ref.1) | copy-start | bytes 11010052
  26.3 27.5 %copy-start.11 = (bf16[64,896]{1,0:T(8,128)(2,1)S(1)}, bf16[64,896]{1,0:T(8,128)(2,1)}, u32[]{:S(2)}) copy-start(bf16[64,896]{1,0:T(8,128)(2,1)} %param.15) | copy-start | bytes 344068
  26.3 48.1 %copy-start.8 = (bf16[896]{0:T(1024)(128)(2,1)S(1)}, bf16[896]{0:T(1024)(128)(2,1)}, u32[]{:S(2)}) copy-start(bf16[896]{0:T(1024)(128)(2,1)} %param.20) | copy-start | bytes 5380
  26.3 48.1 %copy-start = (bf16[1,896,1024]{2,1,0:T(8,128)(2,1)S(1)}, bf16[1,896,1024]{2,1,0:T(8,128)(2,1)}, u32[]{:S(2)}) copy-start(bf16[1,896,1024]{2,1,0:T(8,128)(2,1)} %param.21) | copy-start | bytes 5505028
  26.3 48.1 %copy-start.1 = (bf16[1,896,1024]{2,1,0:T(8,128)(2,1)S(1)}, bf16[1,896,1024]{2,1,0:T(8,128)(2,1)}, u32[]{:S(2)}) copy-start(bf16[1,896,1024]{2,1,0:T(8,128)(2,1)} %param.22) | copy-start | bytes 5505028
  26.3 17.6 %collective-permute-start.8 = (bf16[64,2048]{1,0:T(8,128)(2,1)S(1)}, bf16[64,2048]{1,0:T(8,128)(2,1)S(1)}, u32[]{:S(2)}, u32[]{:S(2)}) collective-permute-start(bf16[64,2048]{1,0:T(8,128)(2,1)S(1)} %attend.1.h0), channel_id=1, source_target_pairs={{0,8},{4,12},{8,0},{12,4},{1,9},{5,13},{9,1},{13,5},{2,10},{6,14},... | collective-permute-start | bytes 786440 | tf_op jit(solution)/shard_map/gather_heads/ppermute | solution.py:211
  31.3 13.4 %collective-permute-start.7 = (bf16[64,2048]{1,0:T(8,128)(2,1)S(1)}, bf16[64,2048]{1,0:T(8,128)(2,1)S(1)}, u32[]{:S(2)}, u32[]{:S(2)}) collective-permute-start(bf16[64,2048]{1,0:T(8,128)(2,1)S(1)} %attend.1.h0), channel_id=1, source_target_pairs={{0,4},{4,0},{8,12},{12,8},{1,5},{5,1},{9,13},{13,9},{2,6},{6,2},{1... | collective-permute-start | bytes 786440 | tf_op jit(solution)/shard_map/gather_heads/ppermute | solution.py:211
  43.9 7.9 %collective-permute-start.9 = (bf16[64,2048]{1,0:T(8,128)(2,1)S(1)}, bf16[64,2048]{1,0:T(8,128)(2,1)S(1)}, u32[]{:S(2)}, u32[]{:S(2)}) collective-permute-start(bf16[64,2048]{1,0:T(8,128)(2,1)S(1)} %collective-permute-done.8.h2), channel_id=1, source_target_pairs={{0,4},{4,0},{8,12},{12,8},{1,5},{5,1},{9,13},{13,9},{2,6},{6,2},{1... | collective-permute-start | bytes 786440 | tf_op jit(solution)/shard_map/gather_heads/ppermute | solution.py:211
  53.7 1.6 %collective-permute-start.10 = (bf16[128,896]{1,0:T(8,128)(2,1)S(1)}, bf16[128,896]{1,0:T(8,128)(2,1)S(1)}, u32[]{:S(2)}, u32[]{:S(2)}) collective-permute-start(bf16[128,896]{1,0:T(8,128)(2,1)S(1)} %get-tuple-element.44), channel_id=1, source_target_pairs={{0,1},{1,0},{2,3},{3,2},{4,5},{5,4},{6,7},{7,6},{8,9},{9,8},{10,11... | collective-permute-start | bytes 688136 | tf_op jit(solution)/shard_map/project/ppermute | solution.py:214
  53.8 5.6 %collective-permute-start.12 = (bf16[64,896]{1,0:T(8,128)(2,1)S(1)}, bf16[64,896]{1,0:T(8,128)(2,1)S(1)}, u32[]{:S(2)}, u32[]{:S(2)}) collective-permute-start(bf16[64,896]{1,0:T(8,128)(2,1)S(1)} %copy-done.11), channel_id=1, source_target_pairs={{0,0},{1,4},{2,8},{3,12},{4,1},{5,5},{6,9},{7,13},{8,2},{9,6},{10,... | collective-permute-start | bytes 344072 | tf_op jit(solution)/shard_map/project/ppermute | solution.py:218
  55.9 9.2 %collective-permute-start.11 = (bf16[64,896]{1,0:T(8,128)(2,1)S(1)}, bf16[64,896]{1,0:T(8,128)(2,1)S(1)}, u32[]{:S(2)}, u32[]{:S(2)}) collective-permute-start(bf16[64,896]{1,0:T(8,128)(2,1)S(1)} %get-tuple-element.46), channel_id=1, source_target_pairs={{0,2},{1,3},{2,0},{3,1},{4,6},{5,7},{6,4},{7,5},{8,10},{9,11},{10,... | collective-permute-start | bytes 344072 | tf_op jit(solution)/shard_map/project/ppermute | solution.py:214
  65.4 9.0 %collective-permute-start.13 = (bf16[48,896]{1,0:T(8,128)(2,1)S(1)}, bf16[48,896]{1,0:T(8,128)(2,1)S(1)}, u32[]{:S(2)}, u32[]{:S(2)}) collective-permute-start(bf16[48,896]{1,0:T(8,128)(2,1)S(1)} %get-tuple-element.50), channel_id=1, source_target_pairs={{0,0},{1,4},{2,8},{3,12},{4,1},{5,5},{6,9},{7,13},{8,2},{9,6},{10,... | collective-permute-start | bytes 258056 | tf_op jit(solution)/shard_map/scatter_resid/ppermute | solution.py:218
  66.0 8.3 %collective-permute-start.14 = (bf16[48,896]{1,0:T(8,128)(2,1)S(1)}, bf16[48,896]{1,0:T(8,128)(2,1)S(1)}, u32[]{:S(2)}, u32[]{:S(2)}) collective-permute-start(bf16[48,896]{1,0:T(8,128)(2,1)S(1)} %get-tuple-element.51), channel_id=1, source_target_pairs={{0,4},{1,8},{2,12},{3,0},{4,5},{5,9},{6,13},{7,1},{8,6},{9,10},{10... | collective-permute-start | bytes 258056 | tf_op jit(solution)/shard_map/scatter_resid/ppermute | solution.py:218
  67.5 8.3 %collective-permute-start.20 = (bf16[48,896]{1,0:T(8,128)(2,1)S(1)}, bf16[48,896]{1,0:T(8,128)(2,1)S(1)}, u32[]{:S(2)}, u32[]{:S(2)}) collective-permute-start(bf16[48,896]{1,0:T(8,128)(2,1)S(1)} %get-tuple-element.61), channel_id=1, source_target_pairs={{0,8},{1,12},{2,0},{3,4},{4,9},{5,13},{6,1},{7,5},{8,10},{9,14},{1... | collective-permute-start | bytes 258056 | tf_op jit(solution)/shard_map/scatter_resid/ppermute | solution.py:218
  72.2 4.2 %collective-permute-start.21 = (bf16[48,896]{1,0:T(8,128)(2,1)S(1)}, bf16[48,896]{1,0:T(8,128)(2,1)S(1)}, u32[]{:S(2)}, u32[]{:S(2)}) collective-permute-start(bf16[48,896]{1,0:T(8,128)(2,1)S(1)} %get-tuple-element.62), channel_id=1, source_target_pairs={{0,12},{1,0},{2,4},{3,8},{4,13},{5,1},{6,5},{7,9},{8,14},{9,2},{10... | collective-permute-start | bytes 258056 | tf_op jit(solution)/shard_map/scatter_resid/ppermute | solution.py:218
  75.8 4.3 %collective-permute-start.15 = (bf16[48,2176]{1,0:T(8,128)(2,1)S(1)}, bf16[48,2176]{1,0:T(8,128)(2,1)S(1)}, u32[]{:S(2)}, u32[]{:S(2)}) collective-permute-start(bf16[48,2176]{1,0:T(8,128)(2,1)S(1)} %get-tuple-element.53), channel_id=1, source_target_pairs={{0,1},{1,0},{2,3},{3,2},{4,5},{5,4},{6,7},{7,6},{8,9},{9,8},{10,11... | collective-permute-start | bytes 626696 | tf_op jit(solution)/shard_map/expand/ppermute | solution.py:214
  77.8 17.4 %copy-start.2 = (bf16[1,1024,896]{2,1,0:T(8,128)(2,1)S(1)}, bf16[1,1024,896]{2,1,0:T(8,128)(2,1)}, u32[]{:S(2)}) copy-start(bf16[1,1024,896]{2,1,0:T(8,128)(2,1)} %param.23) | copy-start | bytes 5505028
  77.8 5.1 %collective-permute-start.22 = (bf16[48,2176]{1,0:T(8,128)(2,1)S(1)}, bf16[48,2176]{1,0:T(8,128)(2,1)S(1)}, u32[]{:S(2)}, u32[]{:S(2)}) collective-permute-start(bf16[48,2176]{1,0:T(8,128)(2,1)S(1)} %get-tuple-element.64), channel_id=1, source_target_pairs={{0,1},{1,0},{2,3},{3,2},{4,5},{5,4},{6,7},{7,6},{8,9},{9,8},{10,11... | collective-permute-start | bytes 626696 | tf_op jit(solution)/shard_map/expand/ppermute | solution.py:214
  80.2 8.7 %collective-permute-start.17 = (bf16[48,2176]{1,0:T(8,128)(2,1)S(1)}, bf16[48,2176]{1,0:T(8,128)(2,1)S(1)}, u32[]{:S(2)}, u32[]{:S(2)}) collective-permute-start(bf16[48,2176]{1,0:T(8,128)(2,1)S(1)} %get-tuple-element.54), channel_id=1, source_target_pairs={{0,2},{1,3},{2,0},{3,1},{4,6},{5,7},{6,4},{7,5},{8,10},{9,11},{10,... | collective-permute-start | bytes 626696 | tf_op jit(solution)/shard_map/expand/ppermute | solution.py:214
  83.0 11.9 %collective-permute-start.23 = (bf16[48,2176]{1,0:T(8,128)(2,1)S(1)}, bf16[48,2176]{1,0:T(8,128)(2,1)S(1)}, u32[]{:S(2)}, u32[]{:S(2)}) collective-permute-start(bf16[48,2176]{1,0:T(8,128)(2,1)S(1)} %get-tuple-element.66), channel_id=1, source_target_pairs={{0,2},{1,3},{2,0},{3,1},{4,6},{5,7},{6,4},{7,5},{8,10},{9,11},{10,... | collective-permute-start | bytes 626696 | tf_op jit(solution)/shard_map/expand/ppermute | solution.py:214
  84.3 0.7 collective-permute-start.16
  89.1 6.1 %collective-permute-start.18 = (bf16[48,1024]{1,0:T(8,128)(2,1)S(1)}, bf16[48,1024]{1,0:T(8,128)(2,1)S(1)}, u32[]{:S(2)}, u32[]{:S(2)}) collective-permute-start(bf16[48,1024]{1,0:T(8,128)(2,1)S(1)} %expand.8.mine_ref), channel_id=1, source_target_pairs={{0,1},{1,0},{2,3},{3,2},{4,5},{5,4},{6,7},{7,6},{8,9},{9,8},{10,11... | collective-permute-start | bytes 294920 | tf_op jit(solution)/shard_map/contract/ppermute | solution.py:214
  95.1 4.7 %collective-permute-start.24 = (bf16[48,1024]{1,0:T(8,128)(2,1)S(1)}, bf16[48,1024]{1,0:T(8,128)(2,1)S(1)}, u32[]{:S(2)}, u32[]{:S(2)}) collective-permute-start(bf16[48,1024]{1,0:T(8,128)(2,1)S(1)} %expand.11.mine_ref), channel_id=1, source_target_pairs={{0,1},{1,0},{2,3},{3,2},{4,5},{5,4},{6,7},{7,6},{8,9},{9,8},{10,11... | collective-permute-start | bytes 294920 | tf_op jit(solution)/shard_map/contract/ppermute | solution.py:214
  96.2 6.5 %collective-permute-start.19 = (bf16[48,896]{1,0:T(8,128)(2,1)S(1)}, bf16[48,896]{1,0:T(8,128)(2,1)S(1)}, u32[]{:S(2)}, u32[]{:S(2)}) collective-permute-start(bf16[48,896]{1,0:T(8,128)(2,1)S(1)} %get-tuple-element.60), channel_id=1, source_target_pairs={{0,12},{4,0},{8,4},{12,8},{1,13},{5,1},{9,5},{13,9},{2,14},{6,2},{... | collective-permute-start | bytes 258056 | tf_op jit(solution)/shard_map/combine/ppermute | solution.py:221
  100.8 7.7 %collective-permute-start.25 = (bf16[48,896]{1,0:T(8,128)(2,1)S(1)}, bf16[48,896]{1,0:T(8,128)(2,1)S(1)}, u32[]{:S(2)}, u32[]{:S(2)}) collective-permute-start(bf16[48,896]{1,0:T(8,128)(2,1)S(1)} %get-tuple-element.67), channel_id=1, source_target_pairs={{0,8},{4,12},{8,0},{12,4},{1,9},{5,13},{9,1},{13,5},{2,10},{6,14},... | collective-permute-start | bytes 258056 | tf_op jit(solution)/shard_map/combine/ppermute | solution.py:221
  100.9 7.6 %collective-permute-start.26 = (bf16[48,896]{1,0:T(8,128)(2,1)S(1)}, bf16[48,896]{1,0:T(8,128)(2,1)S(1)}, u32[]{:S(2)}, u32[]{:S(2)}) collective-permute-start(bf16[48,896]{1,0:T(8,128)(2,1)S(1)} %get-tuple-element.68), channel_id=1, source_target_pairs={{0,4},{4,8},{8,12},{12,0},{1,5},{5,9},{9,13},{13,1},{2,6},{6,10},{... | collective-permute-start | bytes 258056 | tf_op jit(solution)/shard_map/combine/ppermute | solution.py:221

commit v3 on v2

--- a/solution.py
+++ b/solution.py
@@ -11,6 +11,7 @@
 BF16 = jnp.bfloat16
 VMEM = pl.BlockSpec(memory_space=pltpu.VMEM)
 SMEM = pl.BlockSpec(memory_space=pltpu.SMEM)
+HBM = pl.BlockSpec(memory_space=pltpu.HBM)
 
 
 def dot(a, b):
@@ -30,8 +31,8 @@
         in_specs=specs,
         out_specs=[VMEM] * len(outs),
         scratch_shapes=list(scratch),
-        compiler_params=pltpu.CompilerParams(vmem_limit_bytes=32 * 1024 * 1024),
-        cost_estimate=pl.CostEstimate(flops=flops, bytes_accessed=moved, transcendentals=0),
+        compiler_params=pltpu.CompilerParams(vmem_limit_bytes=10 * 1024 * 1024),
+        cost_estimate=pl.CostEstimate(flops=flops + 1000000000, bytes_accessed=moved, transcendentals=0),
     )(*args)
 
 
@@ -63,27 +64,32 @@
     return acc
 
 
-def attend_kernel(scale, group, bits_ref, rel_ref, q_ref, own_ref, *refs):
-    near_ref, far, (vup_ref, out_ref, held) = refs[0], refs[1:-3], refs[-3:]
+def collect_kernel(bits_ref, *refs):
+    parts, held = refs[:-1], refs[-1]
+    half = parts[0].shape[0]
+    for n, part in enumerate(parts):
+        start = pl.multiple_of((bits_ref[0] ^ (n & 1)) * half, 16)
+        held[n // 2, pl.ds(start, half), :] = part[...]
+
+
+def attend_kernel(
+    scale, group, start, stop, rel_ref, q_ref, own_ref, near_ref, far_ref, vup_ref, *refs
+):
+    out_ref = refs[-1]
     rows = own_ref.shape[0]
     latent, vhead = vup_ref.shape[1:]
-    half = far[0].shape[0]
-    start = pl.multiple_of(bits_ref[0] * half, 16)
-    other = pl.multiple_of((1 - bits_ref[0]) * half, 16)
-    caches = [near_ref[...]]
-    for k in range(len(far) // 2):
-        held[k, pl.ds(start, half), :] = far[2 * k][...]
-        held[k, pl.ds(other, half), :] = far[2 * k + 1][...]
-        caches.append(held[k])
+    caches = [near_ref[...]] + [far_ref[k] for k in range(far_ref.shape[0])]
     rel = jnp.concatenate([rel_ref[...]] * group, axis=0)
     own = own_ref[...]
-    for first in range(0, vup_ref.shape[0], group):
+    for first in range(start, stop, group):
         q = q_ref[first * rows : (first + group) * rows, :]
         acc = attend_rows(scale, q, own, caches, range(len(caches)), rel, latent).astype(BF16)
         for h in range(group):
             head = dot(acc[h * rows : (h + 1) * rows], vup_ref[first + h])
             at = (first + h) * vhead
             out_ref[:, at : at + vhead] = head.astype(BF16)
+    if start > 0:
+        out_ref[:, : start * vhead] = refs[0][...]
 
 
 def split_store(flag, value, keep_ref, send_ref):
@@ -100,13 +106,25 @@
         send_ref[...] = value[:half].astype(send_ref.dtype)
 
 
-def project_kernel(bits_ref, h0, h1, h2, h3, w_ref, keep_ref, send_ref, held):
-    rows = h0.shape[0]
-    for i, head in enumerate((h0, h1, h2, h3)):
+def collect_rows(bits_ref, heads, start, held):
+    rows, width = held.shape[0] // len(heads), held.shape[1]
+    for i, head in enumerate(heads):
         shard = bits_ref[2] ^ i
-        position = 2 * (shard % 2) + shard // 2
-        held[pl.ds(pl.multiple_of(position * rows, 16), rows), :] = head[...]
-    split_store(bits_ref[0], dot(held[...], w_ref[...]), keep_ref, send_ref)
+        position = 2 * (shard & 1) + (shard >> 1)
+        at = start if head.shape[1] > width else 0
+        held[pl.ds(pl.multiple_of(position * rows, 16), rows), :] = head[:, at : at + width]
+    return held[...]
+
+
+def project_first_kernel(bits_ref, h0, h1, h2, h3, w_ref, out_ref, held):
+    rows = collect_rows(bits_ref, (h0, h1, h2, h3), 0, held)
+    out_ref[...] = dot(rows, w_ref[: rows.shape[1], :])
+
+
+def project_kernel(bits_ref, first_ref, h0, h1, h2, h3, w_ref, keep_ref, send_ref, held):
+    rows = collect_rows(bits_ref, (h0, h1, h2, h3), held.shape[1], held)
+    total = first_ref[...] + dot(rows, w_ref[rows.shape[1] :, :])
+    split_store(bits_ref[0], total, keep_ref, send_ref)
 
 
 def halve_kernel(bits_ref, kept_ref, got_ref, keep_ref, send_ref):
@@ -129,8 +147,8 @@
     return jnp.where(lane == 0, high, jnp.where(lane == 1, middle, rest))
 
 
-def expand_kernel(bits_ref, a0, a1, gain_ref, gate_ref, up_ref, keep_ref, send_ref):
-    rows = jnp.concatenate([a0[...], a1[...]], axis=0).astype(F32)
+def expand_kernel(bits_ref, a0, a1, a2, a3, gain_ref, gate_ref, up_ref, keep_ref, send_ref):
+    rows = jnp.concatenate([a0[...], a2[...], a1[...], a3[...]], axis=0).astype(F32)
     squares = jnp.sum(rows * rows, axis=1, keepdims=True)
     scaled = (rows * gain_ref[...].astype(F32)).astype(BF16)
     full = jnp.concatenate(
@@ -139,13 +157,16 @@
     split_store(bits_ref[0], full, keep_ref, send_ref)
 
 
-def add_expand_kernel(kept_ref, got_ref, total_ref, send_ref):
+def add_expand_kernel(kept_ref, got_ref, *outs):
     width = kept_ref.shape[1] - 128
     total = kept_ref[...].astype(F32) + got_ref[...].astype(F32)
     squares = jnp.sum(total[:, width:], axis=1, keepdims=True)
     total = jnp.concatenate([total[:, :width], pieces(squares)], axis=1)
-    total_ref[...] = total
-    send_ref[...] = total.astype(BF16)
+    slots = total.shape[0] // 2
+    for n in range(2):
+        part = total[n * slots : (n + 1) * slots]
+        outs[2 * n][...] = part
+        outs[2 * n + 1][...] = part.astype(BF16)
 
 
 def hidden_kernel(features, kept_ref, got_ref, out_ref):
@@ -174,9 +195,64 @@
     out_ref[...] = total.astype(BF16)
 
 
-def ranks(chosen):
-    count = chosen.astype(jnp.int32)
-    return jnp.cumsum(count, axis=-1) - count
+def layout_kernel(q_ref, *refs):
+    many = (len(refs) - 2) // 2
+    given, out_ref, held, sems = refs[:many], refs[many], refs[many + 1 : -1], refs[-1]
+    copies = [
+        pltpu.make_async_copy(given[i], held[i], sems.at[i]) for i in range(many)
+    ]
+    for copy in copies:
+        copy.start()
+    rows, width = q_ref.shape[0], out_ref.shape[1]
+    for h in range(q_ref.shape[1] // width):
+        out_ref[h * rows : (h + 1) * rows, :] = q_ref[:, h * width : (h + 1) * width]
+    for copy in copies:
+        copy.wait()
+
+
+def column(eye, line):
+    high = line.astype(BF16).astype(F32)
+    middle = (line - high).astype(BF16).astype(F32)
+    parts = (high, middle, line - high - middle)
+    return sum(dot_t(eye, part.astype(BF16)) for part in parts)
+
+
+def chosen_slots(ids, first, count, slots, before):
+    named = [ids == lax.rem(first + k, count) for k in range(count)]
+    chosen = [jnp.max(n.astype(F32), axis=0, keepdims=True) for n in named]
+    line = jnp.concatenate(chosen + chosen, axis=0)
+    rank = dot(line.astype(BF16), before)
+    slot = lax.broadcasted_iota(jnp.int32, (slots, ids.shape[1]), 0).astype(F32)
+    one_hot = [
+        jnp.where((slot == rank[k : k + 1]) & (chosen[k] > 0.5), 1.0, 0.0).astype(BF16)
+        for k in range(count)
+    ]
+    return named, one_hot
+
+
+def routing_kernel(
+    bits_ref, ids_ref, there_ref, weight_ref, dest_ref, pick_ref, put_ref, weights_ref, rel_ref
+):
+    count, slots, rows = pick_ref.shape
+    shard = bits_ref[2]
+    tensor = bits_ref[0] + 2 * bits_ref[1]
+    row = lax.broadcasted_iota(jnp.int32, (rows, rows), 0)
+    lane = lax.broadcasted_iota(jnp.int32, (rows, rows), 1)
+    before = jnp.where(row < lane, 1.0, 0.0).astype(BF16)
+    eye = jnp.where(row == lane, 1.0, 0.0).astype(BF16)
+    _, picks = chosen_slots(there_ref[...], tensor, count, slots, before)
+    named, puts = chosen_slots(ids_ref[...], shard, count, slots, before)
+    for k in range(count):
+        pick_ref[k] = picks[k]
+        put_ref[k] = dot_t(eye, puts[k]).astype(BF16)
+    weight = weight_ref[...]
+    lines = [jnp.sum(jnp.where(n, weight, 0.0), axis=0, keepdims=True) for n in named]
+    lines.append(dest_ref[...].astype(F32))
+    lines += [jnp.zeros_like(lines[0])] * (8 - len(lines))
+    columns = column(eye, jnp.concatenate(lines, axis=0))
+    weights_ref[...] = columns[:, :count]
+    dest = columns[:, count : count + 1].astype(jnp.int32)
+    rel_ref[...] = lax.rem(shard - dest + count, count)
 
 
 def square(
@@ -205,7 +281,7 @@
     scale = (vhead + key_width - latent) ** (-0.5)
     shard = lax.axis_index("expert")
     tensor = lax.axis_index("tensor")
-    bits = jnp.stack([tensor % 2, tensor // 2, shard]).astype(jnp.int32)
+    bits = jnp.stack([tensor & 1, tensor >> 1, shard]).astype(jnp.int32)
 
     def across(value, mask):
         return lax.ppermute(value, "expert", [(i, i ^ mask) for i in range(count)])
@@ -223,60 +299,94 @@
     def transposed(value):
         return both(value, lambda e, t: t * count + e)
 
-    def gather(value):
-        second = across(value, 2)
-        return [value, across(value, 1), second, across(second, 1)]
-
     with jax.named_scope("gather_cache"):
         cache = prompt_cache.T
         size = key_width // 2
-        half = lax.dynamic_slice_in_dim(cache, (tensor % 2) * size, size, 0)
-        keys = [cache]
-        for k in range(1, count):
-            got = along(half, k)
-            keys += [got, swap(got, 1)]
+        half = lax.dynamic_slice_in_dim(cache, (tensor & 1) * size, size, 0)
+        far_halves = [along(half, k) for k in range(1, count)]
     with jax.named_scope("query_layout"):
-        q = queries.reshape(rows, heads, key_width).transpose(1, 0, 2)
-        q = q.reshape(heads * rows, key_width)
-    with jax.named_scope("early"):
-        ids, q = lax.optimization_barrier((expert_ids, q))
-        ids = transposed(ids)
+        early = (
+            own_latent, cache, value_up, out_proj, gate_weight[0], up_weight[0], down_weight[0],
+        )
+        q, own, near, vup, proj, gate_w, up_w, down_w = pl.pallas_call(
+            layout_kernel,
+            out_shape=[shape((heads * rows, key_width), BF16)]
+            + [pltpu.VMEM(a.shape, a.dtype) for a in early],
+            in_specs=[VMEM] + [HBM] * len(early),
+            out_specs=[VMEM] * (1 + len(early)),
+            scratch_shapes=[pltpu.SemaphoreType.DMA((len(early),))],
+            compiler_params=pltpu.CompilerParams(vmem_limit_bytes=10 * 1024 * 1024),
+            cost_estimate=pl.CostEstimate(
+                flops=1000000000, bytes_accessed=30000000, transcendentals=0
+            ),
+        )(queries, *[pltpu.with_memory_space_constraint(a, pltpu.HBM) for a in early])
     with jax.named_scope("routing"):
-        step = jnp.arange(count, dtype=jnp.int32)
-        slot = jnp.arange(slots, dtype=jnp.int32)
-        chosen = jnp.any(ids[None] == ((tensor + step) % count)[:, None, None], axis=2)
-        pick = chosen[:, None, :] & (ranks(chosen)[:, None, :] == slot[None, :, None])
-        pick = pick.astype(BF16)
-        named = expert_ids[None] == ((shard + step) % count)[:, None, None]
-        mine = jnp.any(named, axis=2)
-        put = mine[:, :, None] & (ranks(mine)[:, :, None] == slot[None, None, :])
-        put = put.astype(BF16)
-        weights = jnp.sum(jnp.where(named, route_weight[None], 0.0), axis=2).T
-        rel = (shard - row_dest) % count
+        there = transposed(expert_ids.T)
+        pick, put, weights, rel = call(
+            routing_kernel,
+            [
+                shape((count, slots, rows), BF16),
+                shape((count, rows, slots), BF16),
+                shape((rows, count), F32),
+                shape((rows, 1), jnp.int32),
+            ],
+            [SMEM] + [VMEM] * 4,
+            (bits, expert_ids.T, there, route_weight.T, row_dest.T),
+            0,
+        )
+    with jax.named_scope("gather_cache"):
+        far_halves[0], q = lax.optimization_barrier((far_halves[0], q))
+        far_halves[1], pick = lax.optimization_barrier((far_halves[1], pick))
+        keys = []
+        for part in far_halves:
+            keys += [part, swap(part, 1)]
     with jax.named_scope("attend"):
         group = 4
-        q, pick, put, weights = lax.optimization_barrier((q, pick, put, weights))
-        (head_out,) = call(
-            functools.partial(attend_kernel, scale, group),
-            [shape((rows, heads * vhead), BF16)],
-            [SMEM] + [VMEM] * (4 + len(keys)),
-            (bits, rel, q, own_latent, *keys, value_up),
-            2 * heads * rows * count * prompt * (key_width + latent),
-            [pltpu.VMEM((count - 1, key_width, prompt), BF16)],
-        )
+        (far,) = call(
+            collect_kernel,
+            [shape((count - 1, key_width, prompt), BF16)],
+            [SMEM] + [VMEM] * len(keys),
+            (bits, *keys),
+            0,
+        )
+        given, far = lax.optimization_barrier((residual_in, far))
+        given = transposed(given)
+        def attend(start, stop, before):
+            return call(
+                functools.partial(attend_kernel, scale, group, start, stop),
+                [shape((rows, stop * vhead), BF16)],
+                [VMEM] * (6 + len(before)),
+                (rel, q, own, near, far, vup, *before),
+                2 * (stop - start) * rows * count * prompt * (key_width + latent),
+            )
+
+        (half_out,) = attend(0, heads // 2, ())
+        (head_out,) = attend(heads // 2, heads, (half_out,))
     with jax.named_scope("gather_heads"):
-        gathered = gather(head_out)
+        far_first = across(half_out, 2)
+        far_second = across(head_out[:, heads // 2 * vhead :], 2)
+        near_both = across(head_out, 1)
+        far_first, head_out = lax.optimization_barrier((far_first, head_out))
+        last_first = across(far_first, 1)
+        last_second = across(far_second, 1)
+        given, near_both = lax.optimization_barrier((given, near_both))
     with jax.named_scope("project"):
+        (first,) = call(
+            project_first_kernel,
+            [shape((count * rows, width), F32)],
+            [SMEM] + [VMEM] * 5,
+            (bits, half_out, near_both, far_first, last_first, proj),
+            count * rows * heads * vhead * width,
+            [pltpu.VMEM((count * rows, heads // 2 * vhead), BF16)],
+        )
         kept, sent = call(
             project_kernel,
             [shape((2 * rows, width), F32), shape((2 * rows, width), BF16)],
-            [SMEM] + [VMEM] * 5,
-            (bits, *gathered, out_proj),
-            2 * count * rows * heads * vhead * width,
-            [pltpu.VMEM((count * rows, heads * vhead), BF16)],
-        )
-        given, sent = lax.optimization_barrier((residual_in, sent))
-        given = transposed(given)
+            [SMEM] + [VMEM] * 6,
+            (bits, first, head_out, near_both, far_second, last_second, proj),
+            count * rows * heads * vhead * width,
+            [pltpu.VMEM((count * rows, heads // 2 * vhead), BF16)],
+        )
         kept, sent = call(
             halve_kernel,
             [shape((rows, width), F32), shape((rows, width), BF16)],
@@ -291,33 +401,38 @@
             (kept, swap(sent, 2), given, pick),
             2 * count * rows * slots * width,
         )
+    order = (2, 3, 0, 1)
     with jax.named_scope("scatter_resid"):
         arrived = [
-            both(picked[k], lambda e, t, k=k: (t + k) % count * count + e) for k in range(count)
+            both(picked[k], lambda e, t, k=k: (t + k) % count * count + e) for k in order
         ]
     wide = 2 * ff + 128
+    with jax.named_scope("expand"):
+        kept, sent = call(
+            expand_kernel,
+            [shape((2 * slots, wide), BF16), shape((2 * slots, wide), BF16)],
+            [SMEM] + [VMEM] * 7,
+            (bits, *arrived, norm_gain[None, :], gate_w, up_w),
+            4 * count * slots * width * ff,
+        )
+        halves = call(
+            add_expand_kernel,
+            [shape((slots, wide), F32), shape((slots, wide), BF16)] * 2,
+            [VMEM, VMEM],
+            (kept, swap(sent, 1)),
+            2 * slots * wide,
+        )
     outs = []
-    for first in range(0, count, 2):
+    for n in range(2):
+        kept, sent = halves[2 * n : 2 * n + 2]
         with jax.named_scope("expand"):
-            kept, sent = call(
-                expand_kernel,
-                [shape((slots, wide), BF16), shape((slots, wide), BF16)],
-                [SMEM] + [VMEM] * 5,
-                (bits, *arrived[first : first + 2], norm_gain[None, :], gate_weight[0], up_weight[0]),
-                8 * slots * width * ff,
-            )
-            kept, sent = call(
-                add_expand_kernel,
-                [shape((slots, wide), F32), shape((slots, wide), BF16)],
-                [VMEM, VMEM],
-                (kept, swap(sent, 1)),
-                2 * slots * wide,
-            )
             got = swap(sent, 2)
-            if first == 0:
+            if n == 0:
                 resid, _ = lax.optimization_barrier((resid, sent))
                 resid = transposed(resid)
                 resid, got = lax.optimization_barrier((resid, got))
+            else:
+                *outs, got = lax.optimization_barrier((*outs, got))
             (hidden,) = call(
                 functools.partial(hidden_kernel, width * count),
                 [shape((slots, ff), BF16)],
@@ -330,12 +445,12 @@
                 contract_kernel,
                 [shape((slots, width), BF16)] * 2,
                 [SMEM] + [VMEM] * 3,
-                (bits, hidden, swap(hidden, 1), down_weight[0]),
+                (bits, hidden, swap(hidden, 1), down_w),
                 4 * slots * width * ff,
                 [pltpu.VMEM((2 * slots, ff), BF16)],
             )
     with jax.named_scope("combine"):
-        back = [outs[0]] + [along(outs[k], -k) for k in range(1, count)]
+        back = [along(out, -k) if k else out for k, out in sorted(zip(order, outs), key=lambda pair: pair[0])]
         (scored,) = call(
             combine_kernel,
             [shape((rows, width), BF16)],

time: 110 us -> 102 us (0.927)
  waiting for transfers between devices: 44 us -> 33.6 us
  Pallas kernels: 15 us -> 20.1 us
  local copies, waits for them, and re-layouts: 6.39 us -> 2.23 us
  starting transfers between devices: 42.6 us -> 45.2 us
    ppermute x11 -> x10, waiting for transfers between devices: 15.5 us -> 10.9 us  [swap(): return lax.ppermute(value, 'tensor', [(i, i ^ mask) for i in range(count)])]
    pallas_call x0 -> x1, Pallas kernels: none -> 4.48 us  [square(): pl.pallas_call(layout_kernel, out_shape=[shape((heads * rows, key_width),...]
    ppermute x3 -> x5, waiting for transfers between devices: 20.1 us -> 16.2 us  [across(): return lax.ppermute(value, 'expert', [(i, i ^ mask) for i in range(count)])]
    ppermute x6, waiting for transfers between devices: 7.78 us -> 4.12 us  [along(): lax.ppermute(value, 'expert', [(i, (i + k) % count) for i in range(count)])]
    ppermute x7, starting transfers between devices: 11 us -> 7.79 us  [both(): return lax.ppermute(value, ('expert', 'tensor'), pairs)]
    reshape x2 -> x0, local copies, waits for them, and re-layouts: 2.52 us -> none  [square(): q = queries.reshape(rows, heads, key_width).transpose(1, 0, 2)]
    ppermute x3 -> x5, starting transfers between devices: 5.35 us -> 7.78 us  [across(): return lax.ppermute(value, 'expert', [(i, i ^ mask) for i in range(count)])]
    ppermute x6, starting transfers between devices: 11.4 us -> 13.7 us  [along(): lax.ppermute(value, 'expert', [(i, (i + k) % count) for i in range(count)])]
  transfers between devices with their start and end apart: 27 -> 28, of which waited for: 13 -> 18; matrix products, arithmetic and copies ran while one was open for 4% -> 0% of each run, Pallas kernels for 5% -> 11%
where the time goes in v3:
time: 102 us; the launch traced here: 101 us
  starting transfers between devices  45.2 us (44%)
  waiting for transfers between devices  33.6 us (33%)
  Pallas kernels  20.1 us (20%)
  local copies, waits for them, and re-layouts  2.23 us (2%)
    ppermute x5, waiting for transfers between devices, across(): return lax.ppermute(value, 'expert', [(i, i ^ mask) for i in range(count)])  16.2 us
    ppermute x10, starting transfers between devices, swap(): return lax.ppermute(value, 'tensor', [(i, i ^ mask) for i in range(count)])  15.9 us
    pallas_call x15, Pallas kernels, call(): pl.pallas_call(kernel, out_shape=outs, in_specs=specs, out_specs=[VMEM] *...  15.6 us
    ppermute x6, starting transfers between devices, along(): lax.ppermute(value, 'expert', [(i, (i + k) % count) for i in range(count)])  13.7 us
    ppermute x10, waiting for transfers between devices, swap(): return lax.ppermute(value, 'tensor', [(i, i ^ mask) for i in range(count)])  10.9 us
    ppermute x7, starting transfers between devices, both(): return lax.ppermute(value, ('expert', 'tensor'), pairs)  7.79 us
    ppermute x5, starting transfers between devices, across(): return lax.ppermute(value, 'expert', [(i, i ^ mask) for i in range(count)])  7.78 us
    pallas_call x1, Pallas kernels, square(): pl.pallas_call(layout_kernel, out_shape=[shape((heads * rows, key_width),...  4.48 us
  transfers between devices with their start and end apart: 28, of which 18 were waited for; matrix products, arithmetic and copies ran while one was open for 0% of the time, Pallas kernels for 11%

profile of v3, /device:TPU:0, one launch (start us, length us, event | category | flops | bytes accessed | tf_op | source)
XLA Modules:
  0.0 101.5 jit_solution(16852822112464975278)
XLA Ops:
  0.0 0.9 dynamic-slice_bitcast_fusion
  0.9 3.1 %collective-permute-start.1 = (bf16[288,256]{1,0:T(8,128)(2,1)S(1)}, bf16[288,256]{1,0:T(8,128)(2,1)S(1)}, u32[]{:S(2)}, u32[]{:S(2)}) collective-permute-start(bf16[288,256]{1,0:T(8,128)(2,1)S(1)} %dynamic-slice_bitcast_fusion), channel_id=1, source_target_pairs={{0,4},{4,8},{8,12},{12,0},{1,5},{5,9},{9,13},{13,1},{2,6},{6,10},{... | collective-permute-start | bytes 442376 | tf_op jit(solution)/shard_map/gather_cache/ppermute | solution.py:297
  4.0 2.6 %collective-permute-start.3 = (bf16[288,256]{1,0:T(8,128)(2,1)S(1)}, bf16[288,256]{1,0:T(8,128)(2,1)S(1)}, u32[]{:S(2)}, u32[]{:S(2)}) collective-permute-start(bf16[288,256]{1,0:T(8,128)(2,1)S(1)} %dynamic-slice_bitcast_fusion), channel_id=1, source_target_pairs={{0,8},{4,12},{8,0},{12,4},{1,9},{5,13},{9,1},{13,5},{2,10},{6,14},... | collective-permute-start | bytes 442376 | tf_op jit(solution)/shard_map/gather_cache/ppermute | solution.py:297
  6.6 1.3 %collective-permute-start.5 = (bf16[288,256]{1,0:T(8,128)(2,1)S(1)}, bf16[288,256]{1,0:T(8,128)(2,1)S(1)}, u32[]{:S(2)}, u32[]{:S(2)}) collective-permute-start(bf16[288,256]{1,0:T(8,128)(2,1)S(1)} %dynamic-slice_bitcast_fusion), channel_id=1, source_target_pairs={{0,12},{4,0},{8,4},{12,8},{1,13},{5,1},{9,5},{13,9},{2,14},{6,2},{... | collective-permute-start | bytes 442376 | tf_op jit(solution)/shard_map/gather_cache/ppermute | solution.py:297
  7.9 1.3 %collective-permute-start = (s32[2,64]{1,0:T(2,128)}, s32[2,64]{1,0:T(2,128)S(1)}, u32[]{:S(2)}, u32[]{:S(2)}) collective-permute-start(s32[2,64]{1,0:T(2,128)} %bitcast.12), channel_id=1, source_target_pairs={{0,0},{1,4},{2,8},{3,12},{4,1},{5,5},{6,9},{7,13},{8,2},{9,6},{10,... | collective-permute-start | bytes 1544 | tf_op jit(solution)/shard_map/routing/ppermute | solution.py:294
  9.3 1.3 %copy-done = bf16[64,9216]{1,0:T(8,128)(2,1)S(1)} copy-done((bf16[64,9216]{1,0:T(8,128)(2,1)S(1)}, bf16[64,9216]{1,0:T(8,128)(2,1)}, u32[]{:S(2)}) %copy-start) | copy-done | bytes 1179672
  10.6 4.5 %query_layout.1 = (bf16[1024,576]{1,0:T(8,128)(2,1)S(1)}, bf16[64,576]{1,0:T(8,128)(2,1)S(1)}, bf16[576,256]{1,0:T(8,128)(2,1)S(1)}, bf16[16,512,128]{2,1,0:T(8,...) custom-call(bf16[64,9216]{1,0:T(8,128)(2,1)S(1)} %copy-done, ...), custom_call_target="tpu_custom_call" | custom-call | flops 1000000000 | bytes 30000000 | tf_op jit(solution)/shard_map/query_layout/pallas_call | solution.py:311
  15.2 0.9 routing.1
  16.1 1.4 %collective-permute-start.2 = (bf16[288,256]{1,0:T(8,128)(2,1)S(1)}, bf16[288,256]{1,0:T(8,128)(2,1)S(1)}, u32[]{:S(2)}, u32[]{:S(2)}) collective-permute-start(bf16[288,256]{1,0:T(8,128)(2,1)S(1)} %collective-permute-done.1.refs_0_), channel_id=1, source_target_pairs={{0,1},{1,0},{2,3},{3,2},{4,5},{5,4},{6,7},{7,6},{8,9},{9,8},{10,11... | collective-permute-start | bytes 442376 | tf_op jit(solution)/shard_map/gather_cache/ppermute | solution.py:290
  17.6 0.4 collective-permute-start.6
  18.0 0.5 collective-permute-done.2.refs_1_
  19.1 0.6 attend.3.far_ref
  19.7 2.8 %attend.4.refs_0_.h0 = bf16[64,1024]{1,0:T(8,128)(2,1)S(1)} custom-call(s32[64,1]{1,0:T(8,128)S(1)} %get-tuple-element.54.rel_ref, bf16[1024,576]{1,0:T(8,128)(2,1)S(1)} %get-tuple-element.56.q_ref, bf16[64,576]{1,0:T(8,128)(2,1)S(1)} %get-tuple-element.57.own_ref, bf16[576,256]{1,0:T(8,128)(2,1)S(1)} %get-tuple-element.58.near_ref, ...), custom_call_target="tpu_custom_call" | custom-call | flops 2140850688 | bytes 4661504 | tf_op jit(solution)/shard_map/attend/pallas_call | solution.py:28
  22.6 4.4 %collective-permute-start.9 = (bf16[64,1024]{1,0:T(8,128)(2,1)S(1)}, bf16[64,1024]{1,0:T(8,128)(2,1)S(1)}, u32[]{:S(2)}, u32[]{:S(2)}) collective-permute-start(bf16[64,1024]{1,0:T(8,128)(2,1)S(1)} %attend.4.refs_0_.h0), channel_id=1, source_target_pairs={{0,8},{4,12},{8,0},{12,4},{1,9},{5,13},{9,1},{13,5},{2,10},{6,14},... | collective-permute-start | bytes 393224 | tf_op jit(solution)/shard_map/gather_heads/ppermute | solution.py:287
  27.0 2.8 %attend.5.h0 = bf16[64,2048]{1,0:T(8,128)(2,1)S(1)} custom-call(s32[64,1]{1,0:T(8,128)S(1)} %get-tuple-element.54.rel_ref, bf16[1024,576]{1,0:T(8,128)(2,1)S(1)} %get-tuple-element.56.q_ref, bf16[64,576]{1,0:T(8,128)(2,1)S(1)} %get-tuple-element.57.own_ref, bf16[576,256]{1,0:T(8,128)(2,1)S(1)} %get-tuple-element.58.near_ref, ...), custom_call_target="tpu_custom_call" | custom-call | flops 2140850688 | bytes 4923648 | tf_op jit(solution)/shard_map/attend/pallas_call | solution.py:28
  30.2 0.5 collective-permute-start.11
  30.7 3.0 %collective-permute-done.9.h2 = bf16[64,1024]{1,0:T(8,128)(2,1)S(1)} collective-permute-done((bf16[64,1024]{1,0:T(8,128)(2,1)S(1)}, bf16[64,1024]{1,0:T(8,128)(2,1)S(1)}, u32[]{:S(2)}, u32[]{:S(2)}) %collective-permute-start.9) | collective-permute-done | bytes 131104 | tf_op jit(solution)/shard_map/gather_heads/ppermute | solution.py:287
  34.0 0.7 collective-permute-start.7
  34.7 5.0 %collective-permute-done.11.h2 = bf16[64,1024]{1,0:T(8,128)(2,1)S(1)} collective-permute-done((bf16[64,1024]{1,0:T(8,128)(2,1)S(1)}, bf16[64,1024]{1,0:T(8,128)(2,1)S(1)}, u32[]{:S(2)}, u32[]{:S(2)}) %collective-permute-start.11) | collective-permute-done | bytes 131104 | tf_op jit(solution)/shard_map/gather_heads/ppermute | solution.py:287
  39.7 2.1 %collective-permute-start.12 = (bf16[64,1024]{1,0:T(8,128)(2,1)S(1)}, bf16[64,1024]{1,0:T(8,128)(2,1)S(1)}, u32[]{:S(2)}, u32[]{:S(2)}) collective-permute-start(bf16[64,1024]{1,0:T(8,128)(2,1)S(1)} %collective-permute-done.11.h2), channel_id=1, source_target_pairs={{0,4},{4,0},{8,12},{12,8},{1,5},{5,1},{9,13},{13,9},{2,6},{6,2},{1... | collective-permute-start | bytes 393224 | tf_op jit(solution)/shard_map/gather_heads/ppermute | solution.py:287
  42.1 5.2 %collective-permute-done.10.h3 = bf16[64,1024]{1,0:T(8,128)(2,1)S(1)} collective-permute-done((bf16[64,1024]{1,0:T(8,128)(2,1)S(1)}, bf16[64,1024]{1,0:T(8,128)(2,1)S(1)}, u32[]{:S(2)}, u32[]{:S(2)}) %collective-permute-start.10) | collective-permute-done | bytes 131104 | tf_op jit(solution)/shard_map/gather_heads/ppermute | solution.py:287
  47.3 1.3 %project.4.first_ref = f32[256,896]{1,0:T(8,128)S(1)} custom-call(s32[3]{0:T(128)S(1)} %pad_add_fusion.bits_ref, bf16[64,1024]{1,0:T(8,128)(2,1)S(1)} %attend.4.refs_0_.h0, bf16[64,2048]{1,0:T(8,128)(2,1)S(1)} %collective-permute-done.8.h1, bf16[64,1024]{1,0:T(8,128)(2,1)S(1)} %collective-permute-done.9.h2, bf16[64,1024]{1,0:T(8,128)(2,1)S(1)} %collective-permute-done.10.h3, ...), custom_call_target="tpu_custom_call" | custom-call | flops 1469762048 | bytes 5242892 | tf_op jit(solution)/shard_map/project/pallas_call | solution.py:28
  48.5 2.7 %collective-permute-done.12.h3 = bf16[64,1024]{1,0:T(8,128)(2,1)S(1)} collective-permute-done((bf16[64,1024]{1,0:T(8,128)(2,1)S(1)}, bf16[64,1024]{1,0:T(8,128)(2,1)S(1)}, u32[]{:S(2)}, u32[]{:S(2)}) %collective-permute-start.12) | collective-permute-done | bytes 131104 | tf_op jit(solution)/shard_map/gather_heads/ppermute | solution.py:287
  51.3 1.3 %project.5 = (f32[128,896]{1,0:T(8,128)S(1)}, bf16[128,896]{1,0:T(8,128)(2,1)S(1)}) custom-call(s32[3]{0:T(128)S(1)} %pad_add_fusion.bits_ref, f32[256,896]{1,0:T(8,128)S(1)} %project.4.first_ref, bf16[64,2048]{1,0:T(8,128)(2,1)S(1)} %attend.5.h0, bf16[64,2048]{1,0:T(8,128)(2,1)S(1)} %collective-permute-done.8.h1, ...), custom_call_target="tpu_custom_call" | custom-call | flops 1469762048 | bytes 6062092 | tf_op jit(solution)/shard_map/project/pallas_call | solution.py:28
  52.7 1.5 %collective-permute-done.13.got_ref = bf16[128,896]{1,0:T(8,128)(2,1)S(1)} collective-permute-done((bf16[128,896]{1,0:T(8,128)(2,1)S(1)}, bf16[128,896]{1,0:T(8,128)(2,1)S(1)}, u32[]{:S(2)}, u32[]{:S(2)}) %collective-permute-start.13) | collective-permute-done | bytes 229408 | tf_op jit(solution)/shard_map/project/ppermute | solution.py:290
  54.2 0.6 project.6
  54.9 5.2 %collective-permute-done.14.got_ref = bf16[64,896]{1,0:T(8,128)(2,1)S(1)} collective-permute-done((bf16[64,896]{1,0:T(8,128)(2,1)S(1)}, bf16[64,896]{1,0:T(8,128)(2,1)S(1)}, u32[]{:S(2)}, u32[]{:S(2)}) %collective-permute-start.14) | collective-permute-done | bytes 114720 | tf_op jit(solution)/shard_map/project/ppermute | solution.py:290
  60.4 1.6 %collective-permute-start.16 = (bf16[48,896]{1,0:T(8,128)(2,1)S(1)}, bf16[48,896]{1,0:T(8,128)(2,1)S(1)}, u32[]{:S(2)}, u32[]{:S(2)}) collective-permute-start(bf16[48,896]{1,0:T(8,128)(2,1)S(1)} %get-tuple-element.77), channel_id=1, source_target_pairs={{0,12},{1,0},{2,4},{3,8},{4,13},{5,1},{6,5},{7,9},{8,14},{9,2},{10... | collective-permute-start | bytes 258056 | tf_op jit(solution)/shard_map/scatter_resid/ppermute | solution.py:294
  61.9 0.7 collective-permute-start.17
  62.6 2.9 %collective-permute-start.18 = (bf16[48,896]{1,0:T(8,128)(2,1)S(1)}, bf16[48,896]{1,0:T(8,128)(2,1)S(1)}, u32[]{:S(2)}, u32[]{:S(2)}) collective-permute-start(bf16[48,896]{1,0:T(8,128)(2,1)S(1)} %get-tuple-element.79), channel_id=1, source_target_pairs={{0,4},{1,8},{2,12},{3,0},{4,5},{5,9},{6,13},{7,1},{8,6},{9,10},{10... | collective-permute-start | bytes 258056 | tf_op jit(solution)/shard_map/scatter_resid/ppermute | solution.py:294
  65.6 2.3 %collective-permute-done.18.a3 = bf16[48,896]{1,0:T(8,128)(2,1)S(1)} collective-permute-done((bf16[48,896]{1,0:T(8,128)(2,1)S(1)}, bf16[48,896]{1,0:T(8,128)(2,1)S(1)}, u32[]{:S(2)}, u32[]{:S(2)}) %collective-permute-start.18) | collective-permute-done | bytes 86048 | tf_op jit(solution)/shard_map/scatter_resid/ppermute | solution.py:294
  67.9 1.6 %expand.4 = (bf16[96,2176]{1,0:T(8,128)(2,1)S(1)}, bf16[96,2176]{1,0:T(8,128)(2,1)S(1)}) custom-call(s32[3]{0:T(128)S(1)} %pad_add_fusion.bits_ref, bf16[48,896]{1,0:T(8,128)(2,1)S(1)} %collective-permute-done.15.a0, bf16[48,896]{1,0:T(8,128)(2,1)S(1)} %collective-permute-done.16.a1, bf16[48,896]{1,0:T(8,128)(2,1)S(1)} %collective-permute-done.17.a2, ...), custom_call_target="tpu_custom_call" | custom-call | flops 1704643072 | bytes 4851468 | tf_op jit(solution)/shard_map/expand/pallas_call | solution.py:28
  69.5 1.4 %collective-permute-start.19 = (bf16[96,2176]{1,0:T(8,128)(2,1)S(1)}, bf16[96,2176]{1,0:T(8,128)(2,1)S(1)}, u32[]{:S(2)}, u32[]{:S(2)}) collective-permute-start(bf16[96,2176]{1,0:T(8,128)(2,1)S(1)} %get-tuple-element.83), channel_id=1, source_target_pairs={{0,1},{1,0},{2,3},{3,2},{4,5},{5,4},{6,7},{7,6},{8,9},{9,8},{10,11... | collective-permute-start | bytes 1253384 | tf_op jit(solution)/shard_map/expand/ppermute | solution.py:290
  70.9 1.4 %collective-permute-done.19.got_ref = bf16[96,2176]{1,0:T(8,128)(2,1)S(1)} collective-permute-done((bf16[96,2176]{1,0:T(8,128)(2,1)S(1)}, bf16[96,2176]{1,0:T(8,128)(2,1)S(1)}, u32[]{:S(2)}, u32[]{:S(2)}) %collective-permute-start.19) | collective-permute-done | bytes 417824 | tf_op jit(solution)/shard_map/expand/ppermute | solution.py:290
  72.4 3.7 %collective-permute-start.21 = (bf16[48,2176]{1,0:T(8,128)(2,1)S(1)}, bf16[48,2176]{1,0:T(8,128)(2,1)S(1)}, u32[]{:S(2)}, u32[]{:S(2)}) collective-permute-start(bf16[48,2176]{1,0:T(8,128)(2,1)S(1)} %get-tuple-element.84), channel_id=1, source_target_pairs={{0,2},{1,3},{2,0},{3,1},{4,6},{5,7},{6,4},{7,5},{8,10},{9,11},{10,... | collective-permute-start | bytes 626696 | tf_op jit(solution)/shard_map/expand/ppermute | solution.py:290
  76.2 0.7 collective-permute-start.20
  76.8 4.9 %collective-permute-start.23 = (bf16[48,2176]{1,0:T(8,128)(2,1)S(1)}, bf16[48,2176]{1,0:T(8,128)(2,1)S(1)}, u32[]{:S(2)}, u32[]{:S(2)}) collective-permute-start(bf16[48,2176]{1,0:T(8,128)(2,1)S(1)} %get-tuple-element.93), channel_id=1, source_target_pairs={{0,2},{1,3},{2,0},{3,1},{4,6},{5,7},{6,4},{7,5},{8,10},{9,11},{10,... | collective-permute-start | bytes 626696 | tf_op jit(solution)/shard_map/expand/ppermute | solution.py:290
  82.0 3.6 %collective-permute-start.22 = (bf16[48,1024]{1,0:T(8,128)(2,1)S(1)}, bf16[48,1024]{1,0:T(8,128)(2,1)S(1)}, u32[]{:S(2)}, u32[]{:S(2)}) collective-permute-start(bf16[48,1024]{1,0:T(8,128)(2,1)S(1)} %expand.6.mine_ref), channel_id=1, source_target_pairs={{0,1},{1,0},{2,3},{3,2},{4,5},{5,4},{6,7},{7,6},{8,9},{9,8},{10,11... | collective-permute-start | bytes 294920 | tf_op jit(solution)/shard_map/contract/ppermute | solution.py:290
  85.6 0.9 collective-permute-done.22.other_ref
  86.5 1.0 contract.2
  87.5 0.8 collective-permute-done.23.got_ref
  88.7 2.8 %collective-permute-start.26 = (bf16[48,896]{1,0:T(8,128)(2,1)S(1)}, bf16[48,896]{1,0:T(8,128)(2,1)S(1)}, u32[]{:S(2)}, u32[]{:S(2)}) collective-permute-start(bf16[48,896]{1,0:T(8,128)(2,1)S(1)} %get-tuple-element.97), channel_id=1, source_target_pairs={{0,8},{4,12},{8,0},{12,4},{1,9},{5,13},{9,1},{13,5},{2,10},{6,14},... | collective-permute-start | bytes 258056 | tf_op jit(solution)/shard_map/combine/ppermute | solution.py:297
  91.6 2.7 %collective-permute-start.27 = (bf16[48,896]{1,0:T(8,128)(2,1)S(1)}, bf16[48,896]{1,0:T(8,128)(2,1)S(1)}, u32[]{:S(2)}, u32[]{:S(2)}) collective-permute-start(bf16[48,896]{1,0:T(8,128)(2,1)S(1)} %get-tuple-element.98), channel_id=1, source_target_pairs={{0,4},{4,8},{8,12},{12,0},{1,5},{5,9},{9,13},{13,1},{2,6},{6,10},{... | collective-permute-start | bytes 258056 | tf_op jit(solution)/shard_map/combine/ppermute | solution.py:297
  94.3 1.0 contract.3
  95.3 1.2 %collective-permute-start.25 = (bf16[48,896]{1,0:T(8,128)(2,1)S(1)}, bf16[48,896]{1,0:T(8,128)(2,1)S(1)}, u32[]{:S(2)}, u32[]{:S(2)}) collective-permute-start(bf16[48,896]{1,0:T(8,128)(2,1)S(1)} %get-tuple-element.96), channel_id=1, source_target_pairs={{0,12},{4,0},{8,4},{12,8},{1,13},{5,1},{9,5},{13,9},{2,14},{6,2},{... | collective-permute-start | bytes 258056 | tf_op jit(solution)/shard_map/combine/ppermute | solution.py:297
  96.4 2.5 %collective-permute-done.27.r3 = bf16[48,896]{1,0:T(8,128)(2,1)S(1)} collective-permute-done((bf16[48,896]{1,0:T(8,128)(2,1)S(1)}, bf16[48,896]{1,0:T(8,128)(2,1)S(1)}, u32[]{:S(2)}, u32[]{:S(2)}) %collective-permute-start.27) | collective-permute-done | bytes 86048 | tf_op jit(solution)/shard_map/combine/ppermute | solution.py:297
  98.9 1.6 %collective-permute-done.25.r1 = bf16[48,896]{1,0:T(8,128)(2,1)S(1)} collective-permute-done((bf16[48,896]{1,0:T(8,128)(2,1)S(1)}, bf16[48,896]{1,0:T(8,128)(2,1)S(1)}, u32[]{:S(2)}, u32[]{:S(2)}) %collective-permute-start.25) | collective-permute-done | bytes 86048 | tf_op jit(solution)/shard_map/combine/ppermute | solution.py:297
  100.5 0.9 combine.1
  (40 shorter events, 3.1 us)
Async XLA Ops:
  0.9 15.2 %collective-permute-start.1 = (bf16[288,256]{1,0:T(8,128)(2,1)S(1)}, bf16[288,256]{1,0:T(8,128)(2,1)S(1)}, u32[]{:S(2)}, u32[]{:S(2)}) collective-permute-start(bf16[288,256]{1,0:T(8,128)(2,1)S(1)} %dynamic-slice_bitcast_fusion), channel_id=1, source_target_pairs={{0,4},{4,8},{8,12},{12,0},{1,5},{5,9},{9,13},{13,1},{2,6},{6,10},{... | collective-permute-start | bytes 442376 | tf_op jit(solution)/shard_map/gather_cache/ppermute | solution.py:297
  4.0 13.5 %collective-permute-start.3 = (bf16[288,256]{1,0:T(8,128)(2,1)S(1)}, bf16[288,256]{1,0:T(8,128)(2,1)S(1)}, u32[]{:S(2)}, u32[]{:S(2)}) collective-permute-start(bf16[288,256]{1,0:T(8,128)(2,1)S(1)} %dynamic-slice_bitcast_fusion), channel_id=1, source_target_pairs={{0,8},{4,12},{8,0},{12,4},{1,9},{5,13},{9,1},{13,5},{2,10},{6,14},... | collective-permute-start | bytes 442376 | tf_op jit(solution)/shard_map/gather_cache/ppermute | solution.py:297
  6.6 11.0 %collective-permute-start.5 = (bf16[288,256]{1,0:T(8,128)(2,1)S(1)}, bf16[288,256]{1,0:T(8,128)(2,1)S(1)}, u32[]{:S(2)}, u32[]{:S(2)}) collective-permute-start(bf16[288,256]{1,0:T(8,128)(2,1)S(1)} %dynamic-slice_bitcast_fusion), channel_id=1, source_target_pairs={{0,12},{4,0},{8,4},{12,8},{1,13},{5,1},{9,5},{13,9},{2,14},{6,2},{... | collective-permute-start | bytes 442376 | tf_op jit(solution)/shard_map/gather_cache/ppermute | solution.py:297
  7.9 7.2 %collective-permute-start = (s32[2,64]{1,0:T(2,128)}, s32[2,64]{1,0:T(2,128)S(1)}, u32[]{:S(2)}, u32[]{:S(2)}) collective-permute-start(s32[2,64]{1,0:T(2,128)} %bitcast.12), channel_id=1, source_target_pairs={{0,0},{1,4},{2,8},{3,12},{4,1},{5,5},{6,9},{7,13},{8,2},{9,6},{10,... | collective-permute-start | bytes 1544 | tf_op jit(solution)/shard_map/routing/ppermute | solution.py:294
  9.3 1.3 %copy-start = (bf16[64,9216]{1,0:T(8,128)(2,1)S(1)}, bf16[64,9216]{1,0:T(8,128)(2,1)}, u32[]{:S(2)}) copy-start(bf16[64,9216]{1,0:T(8,128)(2,1)} %q_ref.1) | copy-start | bytes 3538948
  10.6 4.5 %copy-start.1 = (s32[64,2]{0,1:T(2,128)S(1)}, s32[64,2]{0,1:T(2,128)}, u32[]{:S(2)}) copy-start(s32[64,2]{0,1:T(2,128)} %param.24) | copy-start | bytes 1540
  10.6 4.5 %copy-start.2 = (f32[64,2]{0,1:T(2,128)S(1)}, f32[64,2]{0,1:T(2,128)}, u32[]{:S(2)}) copy-start(f32[64,2]{0,1:T(2,128)} %param.25) | copy-start | bytes 1540
  10.6 4.5 %copy-start.3 = (s32[64,1]{0,1:T(1,128)S(1)}, s32[64,1]{0,1:T(1,128)}, u32[]{:S(2)}) copy-start(s32[64,1]{0,1:T(1,128)} %param.16) | copy-start | bytes 772
  16.1 2.5 %collective-permute-start.2 = (bf16[288,256]{1,0:T(8,128)(2,1)S(1)}, bf16[288,256]{1,0:T(8,128)(2,1)S(1)}, u32[]{:S(2)}, u32[]{:S(2)}) collective-permute-start(bf16[288,256]{1,0:T(8,128)(2,1)S(1)} %collective-permute-done.1.refs_0_), channel_id=1, source_target_pairs={{0,1},{1,0},{2,3},{3,2},{4,5},{5,4},{6,7},{7,6},{8,9},{9,8},{10,11... | collective-permute-start | bytes 442376 | tf_op jit(solution)/shard_map/gather_cache/ppermute | solution.py:290
  17.5 1.4 %collective-permute-start.4 = (bf16[288,256]{1,0:T(8,128)(2,1)S(1)}, bf16[288,256]{1,0:T(8,128)(2,1)S(1)}, u32[]{:S(2)}, u32[]{:S(2)}) collective-permute-start(bf16[288,256]{1,0:T(8,128)(2,1)S(1)} %collective-permute-done.3.refs_2_), channel_id=1, source_target_pairs={{0,1},{1,0},{2,3},{3,2},{4,5},{5,4},{6,7},{7,6},{8,9},{9,8},{10,11... | collective-permute-start | bytes 442376 | tf_op jit(solution)/shard_map/gather_cache/ppermute | solution.py:290
  17.6 1.5 %collective-permute-start.6 = (bf16[288,256]{1,0:T(8,128)(2,1)S(1)}, bf16[288,256]{1,0:T(8,128)(2,1)S(1)}, u32[]{:S(2)}, u32[]{:S(2)}) collective-permute-start(bf16[288,256]{1,0:T(8,128)(2,1)S(1)} %collective-permute-done.5.refs_4_), channel_id=1, source_target_pairs={{0,1},{1,0},{2,3},{3,2},{4,5},{5,4},{6,7},{7,6},{8,9},{9,8},{10,11... | collective-permute-start | bytes 442376 | tf_op jit(solution)/shard_map/gather_cache/ppermute | solution.py:290
  22.6 11.4 %copy-start.5 = (bf16[64,896]{1,0:T(8,128)(2,1)S(1)}, bf16[64,896]{1,0:T(8,128)(2,1)}, u32[]{:S(2)}) copy-start(bf16[64,896]{1,0:T(8,128)(2,1)} %param.15) | copy-start | bytes 344068
  22.6 11.1 %collective-permute-start.9 = (bf16[64,1024]{1,0:T(8,128)(2,1)S(1)}, bf16[64,1024]{1,0:T(8,128)(2,1)S(1)}, u32[]{:S(2)}, u32[]{:S(2)}) collective-permute-start(bf16[64,1024]{1,0:T(8,128)(2,1)S(1)} %attend.4.refs_0_.h0), channel_id=1, source_target_pairs={{0,8},{4,12},{8,0},{12,4},{1,9},{5,13},{9,1},{13,5},{2,10},{6,14},... | collective-permute-start | bytes 393224 | tf_op jit(solution)/shard_map/gather_heads/ppermute | solution.py:287
  29.8 12.3 %collective-permute-start.8 = (bf16[64,2048]{1,0:T(8,128)(2,1)S(1)}, bf16[64,2048]{1,0:T(8,128)(2,1)S(1)}, u32[]{:S(2)}, u32[]{:S(2)}) collective-permute-start(bf16[64,2048]{1,0:T(8,128)(2,1)S(1)} %attend.5.h0), channel_id=1, source_target_pairs={{0,4},{4,0},{8,12},{12,8},{1,5},{5,1},{9,13},{13,9},{2,6},{6,2},{1... | collective-permute-start | bytes 786440 | tf_op jit(solution)/shard_map/gather_heads/ppermute | solution.py:287
  30.2 9.5 %collective-permute-start.11 = (bf16[64,1024]{1,0:T(8,128)(2,1)S(1)}, bf16[64,1024]{1,0:T(8,128)(2,1)S(1)}, u32[]{:S(2)}, u32[]{:S(2)}) collective-permute-start(bf16[64,1024]{1,0:T(8,128)(2,1)S(1)} %slice.4), channel_id=1, source_target_pairs={{0,8},{4,12},{8,0},{12,4},{1,9},{5,13},{9,1},{13,5},{2,10},{6,14},... | collective-permute-start | bytes 393224 | tf_op jit(solution)/shard_map/gather_heads/ppermute | solution.py:287
  33.7 13.6 %collective-permute-start.10 = (bf16[64,1024]{1,0:T(8,128)(2,1)S(1)}, bf16[64,1024]{1,0:T(8,128)(2,1)S(1)}, u32[]{:S(2)}, u32[]{:S(2)}) collective-permute-start(bf16[64,1024]{1,0:T(8,128)(2,1)S(1)} %collective-permute-done.9.h2), channel_id=1, source_target_pairs={{0,4},{4,0},{8,12},{12,8},{1,5},{5,1},{9,13},{13,9},{2,6},{6,2},{1... | collective-permute-start | bytes 393224 | tf_op jit(solution)/shard_map/gather_heads/ppermute | solution.py:287
  34.0 7.8 %collective-permute-start.7 = (bf16[64,896]{1,0:T(8,128)(2,1)S(1)}, bf16[64,896]{1,0:T(8,128)(2,1)S(1)}, u32[]{:S(2)}, u32[]{:S(2)}) collective-permute-start(bf16[64,896]{1,0:T(8,128)(2,1)S(1)} %copy-done.5), channel_id=1, source_target_pairs={{0,0},{1,4},{2,8},{3,12},{4,1},{5,5},{6,9},{7,13},{8,2},{9,6},{10,... | collective-permute-start | bytes 344072 | tf_op jit(solution)/shard_map/attend/ppermute | solution.py:294
  39.7 11.6 %collective-permute-start.12 = (bf16[64,1024]{1,0:T(8,128)(2,1)S(1)}, bf16[64,1024]{1,0:T(8,128)(2,1)S(1)}, u32[]{:S(2)}, u32[]{:S(2)}) collective-permute-start(bf16[64,1024]{1,0:T(8,128)(2,1)S(1)} %collective-permute-done.11.h2), channel_id=1, source_target_pairs={{0,4},{4,0},{8,12},{12,8},{1,5},{5,1},{9,13},{13,9},{2,6},{6,2},{1... | collective-permute-start | bytes 393224 | tf_op jit(solution)/shard_map/gather_heads/ppermute | solution.py:287
  52.6 1.6 %collective-permute-start.13 = (bf16[128,896]{1,0:T(8,128)(2,1)S(1)}, bf16[128,896]{1,0:T(8,128)(2,1)S(1)}, u32[]{:S(2)}, u32[]{:S(2)}) collective-permute-start(bf16[128,896]{1,0:T(8,128)(2,1)S(1)} %get-tuple-element.70), channel_id=1, source_target_pairs={{0,1},{1,0},{2,3},{3,2},{4,5},{5,4},{6,7},{7,6},{8,9},{9,8},{10,11... | collective-permute-start | bytes 688136 | tf_op jit(solution)/shard_map/project/ppermute | solution.py:290
  54.8 5.3 %collective-permute-start.14 = (bf16[64,896]{1,0:T(8,128)(2,1)S(1)}, bf16[64,896]{1,0:T(8,128)(2,1)S(1)}, u32[]{:S(2)}, u32[]{:S(2)}) collective-permute-start(bf16[64,896]{1,0:T(8,128)(2,1)S(1)} %get-tuple-element.72), channel_id=1, source_target_pairs={{0,2},{1,3},{2,0},{3,1},{4,6},{5,7},{6,4},{7,5},{8,10},{9,11},{10,... | collective-permute-start | bytes 344072 | tf_op jit(solution)/shard_map/project/ppermute | solution.py:290
  60.0 5.5 %copy-start.4 = (bf16[896]{0:T(1024)(128)(2,1)S(1)}, bf16[896]{0:T(1024)(128)(2,1)}, u32[]{:S(2)}) copy-start(bf16[896]{0:T(1024)(128)(2,1)} %param.20) | copy-start | bytes 5380
  60.3 5.3 %collective-permute-start.15 = (bf16[48,896]{1,0:T(8,128)(2,1)S(1)}, bf16[48,896]{1,0:T(8,128)(2,1)S(1)}, u32[]{:S(2)}, u32[]{:S(2)}) collective-permute-start(bf16[48,896]{1,0:T(8,128)(2,1)S(1)} %get-tuple-element.76), channel_id=1, source_target_pairs={{0,8},{1,12},{2,0},{3,4},{4,9},{5,13},{6,1},{7,5},{8,10},{9,14},{1... | collective-permute-start | bytes 258056 | tf_op jit(solution)/shard_map/scatter_resid/ppermute | solution.py:294
  60.4 5.2 %collective-permute-start.16 = (bf16[48,896]{1,0:T(8,128)(2,1)S(1)}, bf16[48,896]{1,0:T(8,128)(2,1)S(1)}, u32[]{:S(2)}, u32[]{:S(2)}) collective-permute-start(bf16[48,896]{1,0:T(8,128)(2,1)S(1)} %get-tuple-element.77), channel_id=1, source_target_pairs={{0,12},{1,0},{2,4},{3,8},{4,13},{5,1},{6,5},{7,9},{8,14},{9,2},{10... | collective-permute-start | bytes 258056 | tf_op jit(solution)/shard_map/scatter_resid/ppermute | solution.py:294
  61.9 3.6 %collective-permute-start.17 = (bf16[48,896]{1,0:T(8,128)(2,1)S(1)}, bf16[48,896]{1,0:T(8,128)(2,1)S(1)}, u32[]{:S(2)}, u32[]{:S(2)}) collective-permute-start(bf16[48,896]{1,0:T(8,128)(2,1)S(1)} %get-tuple-element.78), channel_id=1, source_target_pairs={{0,0},{1,4},{2,8},{3,12},{4,1},{5,5},{6,9},{7,13},{8,2},{9,6},{10,... | collective-permute-start | bytes 258056 | tf_op jit(solution)/shard_map/scatter_resid/ppermute | solution.py:294
  62.6 5.3 %collective-permute-start.18 = (bf16[48,896]{1,0:T(8,128)(2,1)S(1)}, bf16[48,896]{1,0:T(8,128)(2,1)S(1)}, u32[]{:S(2)}, u32[]{:S(2)}) collective-permute-start(bf16[48,896]{1,0:T(8,128)(2,1)S(1)} %get-tuple-element.79), channel_id=1, source_target_pairs={{0,4},{1,8},{2,12},{3,0},{4,5},{5,9},{6,13},{7,1},{8,6},{9,10},{10... | collective-permute-start | bytes 258056 | tf_op jit(solution)/shard_map/scatter_resid/ppermute | solution.py:294
  69.5 2.8 %collective-permute-start.19 = (bf16[96,2176]{1,0:T(8,128)(2,1)S(1)}, bf16[96,2176]{1,0:T(8,128)(2,1)S(1)}, u32[]{:S(2)}, u32[]{:S(2)}) collective-permute-start(bf16[96,2176]{1,0:T(8,128)(2,1)S(1)} %get-tuple-element.83), channel_id=1, source_target_pairs={{0,1},{1,0},{2,3},{3,2},{4,5},{5,4},{6,7},{7,6},{8,9},{9,8},{10,11... | collective-permute-start | bytes 1253384 | tf_op jit(solution)/shard_map/expand/ppermute | solution.py:290
  72.4 9.4 %collective-permute-start.21 = (bf16[48,2176]{1,0:T(8,128)(2,1)S(1)}, bf16[48,2176]{1,0:T(8,128)(2,1)S(1)}, u32[]{:S(2)}, u32[]{:S(2)}) collective-permute-start(bf16[48,2176]{1,0:T(8,128)(2,1)S(1)} %get-tuple-element.84), channel_id=1, source_target_pairs={{0,2},{1,3},{2,0},{3,1},{4,6},{5,7},{6,4},{7,5},{8,10},{9,11},{10,... | collective-permute-start | bytes 626696 | tf_op jit(solution)/shard_map/expand/ppermute | solution.py:290
  76.2 5.6 %collective-permute-start.20 = (bf16[64,896]{1,0:T(8,128)(2,1)S(1)}, bf16[64,896]{1,0:T(8,128)(2,1)S(1)}, u32[]{:S(2)}, u32[]{:S(2)}) collective-permute-start(bf16[64,896]{1,0:T(8,128)(2,1)S(1)} %get-tuple-element.85), channel_id=1, source_target_pairs={{0,0},{1,4},{2,8},{3,12},{4,1},{5,5},{6,9},{7,13},{8,2},{9,6},{10,... | collective-permute-start | bytes 344072 | tf_op jit(solution)/shard_map/expand/ppermute | solution.py:294
  76.8 11.5 %collective-permute-start.23 = (bf16[48,2176]{1,0:T(8,128)(2,1)S(1)}, bf16[48,2176]{1,0:T(8,128)(2,1)S(1)}, u32[]{:S(2)}, u32[]{:S(2)}) collective-permute-start(bf16[48,2176]{1,0:T(8,128)(2,1)S(1)} %get-tuple-element.93), channel_id=1, source_target_pairs={{0,2},{1,3},{2,0},{3,1},{4,6},{5,7},{6,4},{7,5},{8,10},{9,11},{10,... | collective-permute-start | bytes 626696 | tf_op jit(solution)/shard_map/expand/ppermute | solution.py:290
  82.0 4.5 %collective-permute-start.22 = (bf16[48,1024]{1,0:T(8,128)(2,1)S(1)}, bf16[48,1024]{1,0:T(8,128)(2,1)S(1)}, u32[]{:S(2)}, u32[]{:S(2)}) collective-permute-start(bf16[48,1024]{1,0:T(8,128)(2,1)S(1)} %expand.6.mine_ref), channel_id=1, source_target_pairs={{0,1},{1,0},{2,3},{3,2},{4,5},{5,4},{6,7},{7,6},{8,9},{9,8},{10,11... | collective-permute-start | bytes 294920 | tf_op jit(solution)/shard_map/contract/ppermute | solution.py:290
  88.5 5.8 %collective-permute-start.24 = (bf16[48,1024]{1,0:T(8,128)(2,1)S(1)}, bf16[48,1024]{1,0:T(8,128)(2,1)S(1)}, u32[]{:S(2)}, u32[]{:S(2)}) collective-permute-start(bf16[48,1024]{1,0:T(8,128)(2,1)S(1)} %expand.7.mine_ref), channel_id=1, source_target_pairs={{0,1},{1,0},{2,3},{3,2},{4,5},{5,4},{6,7},{7,6},{8,9},{9,8},{10,11... | collective-permute-start | bytes 294920 | tf_op jit(solution)/shard_map/contract/ppermute | solution.py:290
  88.7 7.7 %collective-permute-start.26 = (bf16[48,896]{1,0:T(8,128)(2,1)S(1)}, bf16[48,896]{1,0:T(8,128)(2,1)S(1)}, u32[]{:S(2)}, u32[]{:S(2)}) collective-permute-start(bf16[48,896]{1,0:T(8,128)(2,1)S(1)} %get-tuple-element.97), channel_id=1, source_target_pairs={{0,8},{4,12},{8,0},{12,4},{1,9},{5,13},{9,1},{13,5},{2,10},{6,14},... | collective-permute-start | bytes 258056 | tf_op jit(solution)/shard_map/combine/ppermute | solution.py:297
  91.6 7.4 %collective-permute-start.27 = (bf16[48,896]{1,0:T(8,128)(2,1)S(1)}, bf16[48,896]{1,0:T(8,128)(2,1)S(1)}, u32[]{:S(2)}, u32[]{:S(2)}) collective-permute-start(bf16[48,896]{1,0:T(8,128)(2,1)S(1)} %get-tuple-element.98), channel_id=1, source_target_pairs={{0,4},{4,8},{8,12},{12,0},{1,5},{5,9},{9,13},{13,1},{2,6},{6,10},{... | collective-permute-start | bytes 258056 | tf_op jit(solution)/shard_map/combine/ppermute | solution.py:297
  95.3 5.3 %collective-permute-start.25 = (bf16[48,896]{1,0:T(8,128)(2,1)S(1)}, bf16[48,896]{1,0:T(8,128)(2,1)S(1)}, u32[]{:S(2)}, u32[]{:S(2)}) collective-permute-start(bf16[48,896]{1,0:T(8,128)(2,1)S(1)} %get-tuple-element.96), channel_id=1, source_target_pairs={{0,12},{4,0},{8,4},{12,8},{1,13},{5,1},{9,5},{13,9},{2,14},{6,2},{... | collective-permute-start | bytes 258056 | tf_op jit(solution)/shard_map/combine/ppermute | solution.py:297

commit v4 on v3

--- a/solution.py
+++ b/solution.py
@@ -73,9 +73,8 @@
 
 
 def attend_kernel(
-    scale, group, start, stop, rel_ref, q_ref, own_ref, near_ref, far_ref, vup_ref, *refs
+    scale, group, start, stop, rel_ref, q_ref, own_ref, near_ref, far_ref, vup_ref, out_ref
 ):
-    out_ref = refs[-1]
     rows = own_ref.shape[0]
     latent, vhead = vup_ref.shape[1:]
     caches = [near_ref[...]] + [far_ref[k] for k in range(far_ref.shape[0])]
@@ -86,10 +85,8 @@
         acc = attend_rows(scale, q, own, caches, range(len(caches)), rel, latent).astype(BF16)
         for h in range(group):
             head = dot(acc[h * rows : (h + 1) * rows], vup_ref[first + h])
-            at = (first + h) * vhead
+            at = (first - start + h) * vhead
             out_ref[:, at : at + vhead] = head.astype(BF16)
-    if start > 0:
-        out_ref[:, : start * vhead] = refs[0][...]
 
 
 def split_store(flag, value, keep_ref, send_ref):
@@ -106,23 +103,22 @@
         send_ref[...] = value[:half].astype(send_ref.dtype)
 
 
-def collect_rows(bits_ref, heads, start, held):
-    rows, width = held.shape[0] // len(heads), held.shape[1]
+def collect_rows(bits_ref, heads, held):
+    rows = heads[0].shape[0]
     for i, head in enumerate(heads):
         shard = bits_ref[2] ^ i
         position = 2 * (shard & 1) + (shard >> 1)
-        at = start if head.shape[1] > width else 0
-        held[pl.ds(pl.multiple_of(position * rows, 16), rows), :] = head[:, at : at + width]
+        held[pl.ds(pl.multiple_of(position * rows, 16), rows), :] = head[...]
     return held[...]
 
 
 def project_first_kernel(bits_ref, h0, h1, h2, h3, w_ref, out_ref, held):
-    rows = collect_rows(bits_ref, (h0, h1, h2, h3), 0, held)
+    rows = collect_rows(bits_ref, (h0, h1, h2, h3), held)
     out_ref[...] = dot(rows, w_ref[: rows.shape[1], :])
 
 
 def project_kernel(bits_ref, first_ref, h0, h1, h2, h3, w_ref, keep_ref, send_ref, held):
-    rows = collect_rows(bits_ref, (h0, h1, h2, h3), held.shape[1], held)
+    rows = collect_rows(bits_ref, (h0, h1, h2, h3), held)
     total = first_ref[...] + dot(rows, w_ref[rows.shape[1] :, :])
     split_store(bits_ref[0], total, keep_ref, send_ref)
 
@@ -135,7 +131,7 @@
     resid = kept_ref[...] + got_ref[...].astype(F32) + given_ref[...].astype(F32)
     resid = resid.astype(BF16)
     resid_ref[...] = resid
-    for k, out in enumerate(outs):
+    for k, out in enumerate(outs, 1):
         out[...] = dot(pick_ref[k], resid).astype(BF16)
 
 
@@ -147,8 +143,9 @@
     return jnp.where(lane == 0, high, jnp.where(lane == 1, middle, rest))
 
 
-def expand_kernel(bits_ref, a0, a1, a2, a3, gain_ref, gate_ref, up_ref, keep_ref, send_ref):
-    rows = jnp.concatenate([a0[...], a2[...], a1[...], a3[...]], axis=0).astype(F32)
+def expand_kernel(bits_ref, pick_ref, a0, a1, own_ref, a3, gain_ref, gate_ref, up_ref, keep_ref, send_ref):
+    own = dot(pick_ref[0], own_ref[...]).astype(BF16)
+    rows = jnp.concatenate([a0[...], own, a1[...], a3[...]], axis=0).astype(F32)
     squares = jnp.sum(rows * rows, axis=1, keepdims=True)
     scaled = (rows * gain_ref[...].astype(F32)).astype(BF16)
     full = jnp.concatenate(
@@ -196,17 +193,17 @@
 
 
 def layout_kernel(q_ref, *refs):
-    many = (len(refs) - 2) // 2
-    given, out_ref, held, sems = refs[:many], refs[many], refs[many + 1 : -1], refs[-1]
-    copies = [
-        pltpu.make_async_copy(given[i], held[i], sems.at[i]) for i in range(many)
-    ]
+    many = (len(refs) - 3) // 2
+    given, out_ref, held, (q, sems) = refs[:many], refs[many], refs[many + 1 : -2], refs[-2:]
+    copies = [pltpu.make_async_copy(q_ref, q, sems.at[many])]
+    copies += [pltpu.make_async_copy(given[i], held[i], sems.at[i]) for i in range(many)]
     for copy in copies:
         copy.start()
+    copies[0].wait()
     rows, width = q_ref.shape[0], out_ref.shape[1]
     for h in range(q_ref.shape[1] // width):
-        out_ref[h * rows : (h + 1) * rows, :] = q_ref[:, h * width : (h + 1) * width]
-    for copy in copies:
+        out_ref[h * rows : (h + 1) * rows, :] = q[:, h * width : (h + 1) * width]
+    for copy in copies[1:]:
         copy.wait()
 
 
@@ -243,7 +240,7 @@
     _, picks = chosen_slots(there_ref[...], tensor, count, slots, before)
     named, puts = chosen_slots(ids_ref[...], shard, count, slots, before)
     for k in range(count):
-        pick_ref[k] = picks[k]
+        pick_ref[k] = picks[k] if k else puts[k]
         put_ref[k] = dot_t(eye, puts[k]).astype(BF16)
     weight = weight_ref[...]
     lines = [jnp.sum(jnp.where(n, weight, 0.0), axis=0, keepdims=True) for n in named]
@@ -305,21 +302,21 @@
         half = lax.dynamic_slice_in_dim(cache, (tensor & 1) * size, size, 0)
         far_halves = [along(half, k) for k in range(1, count)]
     with jax.named_scope("query_layout"):
-        early = (
-            own_latent, cache, value_up, out_proj, gate_weight[0], up_weight[0], down_weight[0],
-        )
-        q, own, near, vup, proj, gate_w, up_w, down_w = pl.pallas_call(
+        early = (queries, own_latent, cache, value_up)
+        q, own, near, vup = pl.pallas_call(
             layout_kernel,
             out_shape=[shape((heads * rows, key_width), BF16)]
-            + [pltpu.VMEM(a.shape, a.dtype) for a in early],
-            in_specs=[VMEM] + [HBM] * len(early),
-            out_specs=[VMEM] * (1 + len(early)),
-            scratch_shapes=[pltpu.SemaphoreType.DMA((len(early),))],
+            + [pltpu.VMEM(a.shape, a.dtype) for a in early[1:]],
+            in_specs=[HBM] * len(early),
+            out_specs=[VMEM] * len(early),
+            scratch_shapes=[
+                pltpu.VMEM(queries.shape, BF16), pltpu.SemaphoreType.DMA((len(early),))
+            ],
             compiler_params=pltpu.CompilerParams(vmem_limit_bytes=10 * 1024 * 1024),
             cost_estimate=pl.CostEstimate(
                 flops=1000000000, bytes_accessed=30000000, transcendentals=0
             ),
-        )(queries, *[pltpu.with_memory_space_constraint(a, pltpu.HBM) for a in early])
+        )(*[pltpu.with_memory_space_constraint(a, pltpu.HBM) for a in early])
     with jax.named_scope("routing"):
         there = transposed(expert_ids.T)
         pick, put, weights, rel = call(
@@ -351,31 +348,34 @@
         )
         given, far = lax.optimization_barrier((residual_in, far))
         given = transposed(given)
-        def attend(start, stop, before):
+        def attend(start, stop):
             return call(
                 functools.partial(attend_kernel, scale, group, start, stop),
-                [shape((rows, stop * vhead), BF16)],
-                [VMEM] * (6 + len(before)),
-                (rel, q, own, near, far, vup, *before),
+                [shape((rows, (stop - start) * vhead), BF16)],
+                [VMEM] * 6,
+                (rel, q, own, near, far, vup),
                 2 * (stop - start) * rows * count * prompt * (key_width + latent),
             )
 
-        (half_out,) = attend(0, heads // 2, ())
-        (head_out,) = attend(heads // 2, heads, (half_out,))
+        (half_out,) = attend(0, heads // 2)
+        (half_two,) = attend(heads // 2, heads)
     with jax.named_scope("gather_heads"):
         far_first = across(half_out, 2)
-        far_second = across(head_out[:, heads // 2 * vhead :], 2)
-        near_both = across(head_out, 1)
-        far_first, head_out = lax.optimization_barrier((far_first, head_out))
+        near_first = across(half_out, 1)
+        far_second = across(half_two, 2)
+        far_first, near_first, half_two = lax.optimization_barrier(
+            (far_first, near_first, half_two)
+        )
+        near_second = across(half_two, 1)
         last_first = across(far_first, 1)
         last_second = across(far_second, 1)
-        given, near_both = lax.optimization_barrier((given, near_both))
+        given, near_second = lax.optimization_barrier((given, near_second))
     with jax.named_scope("project"):
         (first,) = call(
             project_first_kernel,
             [shape((count * rows, width), F32)],
             [SMEM] + [VMEM] * 5,
-            (bits, half_out, near_both, far_first, last_first, proj),
+            (bits, half_out, near_first, far_first, last_first, out_proj),
             count * rows * heads * vhead * width,
             [pltpu.VMEM((count * rows, heads // 2 * vhead), BF16)],
         )
@@ -383,7 +383,7 @@
             project_kernel,
             [shape((2 * rows, width), F32), shape((2 * rows, width), BF16)],
             [SMEM] + [VMEM] * 6,
-            (bits, first, head_out, near_both, far_second, last_second, proj),
+            (bits, first, half_two, near_second, far_second, last_second, out_proj),
             count * rows * heads * vhead * width,
             [pltpu.VMEM((count * rows, heads // 2 * vhead), BF16)],
         )
@@ -394,9 +394,9 @@
             (bits, kept, swap(sent, 1)),
             2 * rows * width,
         )
-        resid, *picked = call(
+        picked = call(
             resid_kernel,
-            [shape((rows, width), BF16)] + [shape((slots, width), BF16)] * count,
+            [shape((rows, width), BF16)] + [shape((slots, width), BF16)] * (count - 1),
             [VMEM] * 4,
             (kept, swap(sent, 2), given, pick),
             2 * count * rows * slots * width,
@@ -406,13 +406,14 @@
         arrived = [
             both(picked[k], lambda e, t, k=k: (t + k) % count * count + e) for k in order
         ]
+        resid = arrived[order.index(0)]
     wide = 2 * ff + 128
     with jax.named_scope("expand"):
         kept, sent = call(
             expand_kernel,
             [shape((2 * slots, wide), BF16), shape((2 * slots, wide), BF16)],
-            [SMEM] + [VMEM] * 7,
-            (bits, *arrived, norm_gain[None, :], gate_w, up_w),
+            [SMEM] + [VMEM] * 8,
+            (bits, pick, *arrived, norm_gain[None, :], gate_weight[0], up_weight[0]),
             4 * count * slots * width * ff,
         )
         halves = call(
@@ -427,11 +428,7 @@
         kept, sent = halves[2 * n : 2 * n + 2]
         with jax.named_scope("expand"):
             got = swap(sent, 2)
-            if n == 0:
-                resid, _ = lax.optimization_barrier((resid, sent))
-                resid = transposed(resid)
-                resid, got = lax.optimization_barrier((resid, got))
-            else:
+            if n == 1:
                 *outs, got = lax.optimization_barrier((*outs, got))
             (hidden,) = call(
                 functools.partial(hidden_kernel, width * count),
@@ -445,7 +442,7 @@
                 contract_kernel,
                 [shape((slots, width), BF16)] * 2,
                 [SMEM] + [VMEM] * 3,
-                (bits, hidden, swap(hidden, 1), down_w),
+                (bits, hidden, swap(hidden, 1), down_weight[0]),
                 4 * slots * width * ff,
                 [pltpu.VMEM((2 * slots, ff), BF16)],
             )

time: 102 us -> 100 us (0.980)
  waiting for transfers between devices: 33.6 us -> 42.6 us
  starting transfers between devices: 45.2 us -> 38 us
  Pallas kernels: 20.1 us -> 17.9 us
  local copies, waits for them, and re-layouts: 2.23 us -> 0.96 us
    ppermute x10, starting transfers between devices: 15.9 us -> 7.24 us  [swap(): return lax.ppermute(value, 'tensor', [(i, i ^ mask) for i in range(count)])]
    ppermute x10, waiting for transfers between devices: 10.9 us -> 17.7 us  [swap(): return lax.ppermute(value, 'tensor', [(i, i ^ mask) for i in range(count)])]
    pallas_call x1, Pallas kernels: 4.48 us -> 2.14 us  [square(): pl.pallas_call(layout_kernel, out_shape=[shape((heads * rows, key_width),...]
    ppermute x5 -> x6, starting transfers between devices: 7.78 us -> 9.93 us  [across(): return lax.ppermute(value, 'expert', [(i, i ^ mask) for i in range(count)])]
    ppermute x7 -> x6, waiting for transfers between devices: 2.41 us -> 4.04 us  [both(): return lax.ppermute(value, ('expert', 'tensor'), pairs)]
    ppermute x6, waiting for transfers between devices: 4.12 us -> 5.69 us  [along(): lax.ppermute(value, 'expert', [(i, (i + k) % count) for i in range(count)])]
    unnamed x12 -> x18, local copies, waits for them, and re-layouts: 1.29 us -> 0.04 us
    ppermute x5 -> x6, waiting for transfers between devices: 16.2 us -> 15.2 us  [across(): return lax.ppermute(value, 'expert', [(i, i ^ mask) for i in range(count)])]
  transfers between devices with their start and end apart: 28 -> 28, of which waited for: 18 -> 20; matrix products, arithmetic and copies ran while one was open for 0% -> 0% of each run, Pallas kernels for 11% -> 9%
where the time goes in v4:
time: 100 us; the launch traced here: 99.8 us
  waiting for transfers between devices  42.6 us (43%)
  starting transfers between devices  38 us (38%)
  Pallas kernels  17.9 us (18%)
    ppermute x10, waiting for transfers between devices, swap(): return lax.ppermute(value, 'tensor', [(i, i ^ mask) for i in range(count)])  17.7 us
    pallas_call x15, Pallas kernels, call(): pl.pallas_call(kernel, out_shape=outs, in_specs=specs, out_specs=[VMEM] *...  15.7 us
    ppermute x6, waiting for transfers between devices, across(): return lax.ppermute(value, 'expert', [(i, i ^ mask) for i in range(count)])  15.2 us
    ppermute x6, starting transfers between devices, along(): lax.ppermute(value, 'expert', [(i, (i + k) % count) for i in range(count)])  13 us
    ppermute x6, starting transfers between devices, across(): return lax.ppermute(value, 'expert', [(i, i ^ mask) for i in range(count)])  9.93 us
    ppermute x6, starting transfers between devices, both(): return lax.ppermute(value, ('expert', 'tensor'), pairs)  7.92 us
    ppermute x10, starting transfers between devices, swap(): return lax.ppermute(value, 'tensor', [(i, i ^ mask) for i in range(count)])  7.24 us
    ppermute x6, waiting for transfers between devices, along(): lax.ppermute(value, 'expert', [(i, (i + k) % count) for i in range(count)])  5.69 us
  transfers between devices with their start and end apart: 28, of which 20 were waited for; matrix products, arithmetic and copies ran while one was open for 0% of the time, Pallas kernels for 9%

profile of v4, /device:TPU:0, one launch (start us, length us, event | category | flops | bytes accessed | tf_op | source)
XLA Modules:
  0.0 99.8 jit_solution(12486216909054519085)
XLA Ops:
  0.0 0.9 dynamic-slice_bitcast_fusion
  0.9 3.1 %collective-permute-start.1 = (bf16[288,256]{1,0:T(8,128)(2,1)S(1)}, bf16[288,256]{1,0:T(8,128)(2,1)S(1)}, u32[]{:S(2)}, u32[]{:S(2)}) collective-permute-start(bf16[288,256]{1,0:T(8,128)(2,1)S(1)} %dynamic-slice_bitcast_fusion), channel_id=1, source_target_pairs={{0,4},{4,8},{8,12},{12,0},{1,5},{5,9},{9,13},{13,1},{2,6},{6,10},{... | collective-permute-start | bytes 442376 | tf_op jit(solution)/shard_map/gather_cache/ppermute | solution.py:294
  4.0 2.6 %collective-permute-start.3 = (bf16[288,256]{1,0:T(8,128)(2,1)S(1)}, bf16[288,256]{1,0:T(8,128)(2,1)S(1)}, u32[]{:S(2)}, u32[]{:S(2)}) collective-permute-start(bf16[288,256]{1,0:T(8,128)(2,1)S(1)} %dynamic-slice_bitcast_fusion), channel_id=1, source_target_pairs={{0,8},{4,12},{8,0},{12,4},{1,9},{5,13},{9,1},{13,5},{2,10},{6,14},... | collective-permute-start | bytes 442376 | tf_op jit(solution)/shard_map/gather_cache/ppermute | solution.py:294
  6.6 1.3 %collective-permute-start.5 = (bf16[288,256]{1,0:T(8,128)(2,1)S(1)}, bf16[288,256]{1,0:T(8,128)(2,1)S(1)}, u32[]{:S(2)}, u32[]{:S(2)}) collective-permute-start(bf16[288,256]{1,0:T(8,128)(2,1)S(1)} %dynamic-slice_bitcast_fusion), channel_id=1, source_target_pairs={{0,12},{4,0},{8,4},{12,8},{1,13},{5,1},{9,5},{13,9},{2,14},{6,2},{... | collective-permute-start | bytes 442376 | tf_op jit(solution)/shard_map/gather_cache/ppermute | solution.py:294
  7.9 1.3 %collective-permute-start = (s32[2,64]{1,0:T(2,128)}, s32[2,64]{1,0:T(2,128)S(1)}, u32[]{:S(2)}, u32[]{:S(2)}) collective-permute-start(s32[2,64]{1,0:T(2,128)} %bitcast.16), channel_id=1, source_target_pairs={{0,0},{1,4},{2,8},{3,12},{4,1},{5,5},{6,9},{7,13},{8,2},{9,6},{10,... | collective-permute-start | bytes 1544 | tf_op jit(solution)/shard_map/routing/ppermute | solution.py:291
  9.3 2.1 %query_layout.1 = (bf16[1024,576]{1,0:T(8,128)(2,1)S(1)}, bf16[64,576]{1,0:T(8,128)(2,1)S(1)}, bf16[576,256]{1,0:T(8,128)(2,1)S(1)}, bf16[16,512,128]{2,1,0:T(8,128)(2,1)S(1)}) custom-call(bf16[64,9216]{1,0:T(8,128)(2,1)} %q_ref.1, bf16[64,576]{1,0:T(8,128)(2,1)} %refs_0_.1, bf16[576,256]{1,0:T(8,128)(2,1)} %bitcast.20, bf16[16,512,128]{2,1,0:T(8,128)(2,1)} %refs_2_.1), custom_call_target="tpu_custom_call" | custom-call | flops 1000000000 | bytes 30000000 | tf_op jit(solution)/shard_map/query_layout/pallas_call | solution.py:306
  11.5 0.9 routing.1
  12.5 2.6 %collective-permute-start.2 = (bf16[288,256]{1,0:T(8,128)(2,1)S(1)}, bf16[288,256]{1,0:T(8,128)(2,1)S(1)}, u32[]{:S(2)}, u32[]{:S(2)}) collective-permute-start(bf16[288,256]{1,0:T(8,128)(2,1)S(1)} %collective-permute-done.1.refs_0_), channel_id=1, source_target_pairs={{0,1},{1,0},{2,3},{3,2},{4,5},{5,4},{6,7},{7,6},{8,9},{9,8},{10,11... | collective-permute-start | bytes 442376 | tf_op jit(solution)/shard_map/gather_cache/ppermute | solution.py:287
  15.0 1.3 %collective-permute-done.3.refs_2_ = bf16[288,256]{1,0:T(8,128)(2,1)S(1)} collective-permute-done((bf16[288,256]{1,0:T(8,128)(2,1)S(1)}, bf16[288,256]{1,0:T(8,128)(2,1)S(1)}, u32[]{:S(2)}, u32[]{:S(2)}) %collective-permute-start.3) | collective-permute-done | bytes 147488 | tf_op jit(solution)/shard_map/gather_cache/ppermute | solution.py:294
  16.8 0.9 collective-permute-done.4.refs_3_
  17.9 0.6 attend.3.far_ref
  18.5 2.8 %attend.4.h0 = bf16[64,1024]{1,0:T(8,128)(2,1)S(1)} custom-call(s32[64,1]{1,0:T(8,128)S(1)} %get-tuple-element.47.rel_ref, bf16[1024,576]{1,0:T(8,128)(2,1)S(1)} %get-tuple-element.49.q_ref, bf16[64,576]{1,0:T(8,128)(2,1)S(1)} %get-tuple-element.50.own_ref, bf16[576,256]{1,0:T(8,128)(2,1)S(1)} %get-tuple-element.51.near_ref, ...), custom_call_target="tpu_custom_call" | custom-call | flops 2140850688 | bytes 4661504 | tf_op jit(solution)/shard_map/attend/pallas_call | solution.py:28
  21.3 5.6 %collective-permute-start.7 = (bf16[64,1024]{1,0:T(8,128)(2,1)S(1)}, bf16[64,1024]{1,0:T(8,128)(2,1)S(1)}, u32[]{:S(2)}, u32[]{:S(2)}) collective-permute-start(bf16[64,1024]{1,0:T(8,128)(2,1)S(1)} %attend.4.h0), channel_id=1, source_target_pairs={{0,8},{4,12},{8,0},{12,4},{1,9},{5,13},{9,1},{13,5},{2,10},{6,14},... | collective-permute-start | bytes 393224 | tf_op jit(solution)/shard_map/gather_heads/ppermute | solution.py:284
  27.3 2.8 %attend.5.h0 = bf16[64,1024]{1,0:T(8,128)(2,1)S(1)} custom-call(s32[64,1]{1,0:T(8,128)S(1)} %get-tuple-element.47.rel_ref, bf16[1024,576]{1,0:T(8,128)(2,1)S(1)} %get-tuple-element.49.q_ref, bf16[64,576]{1,0:T(8,128)(2,1)S(1)} %get-tuple-element.50.own_ref, bf16[576,256]{1,0:T(8,128)(2,1)S(1)} %get-tuple-element.51.near_ref, ...), custom_call_target="tpu_custom_call" | custom-call | flops 2140850688 | bytes 4661504 | tf_op jit(solution)/shard_map/attend/pallas_call | solution.py:28
  30.6 3.0 %collective-permute-done.7.h2 = bf16[64,1024]{1,0:T(8,128)(2,1)S(1)} collective-permute-done((bf16[64,1024]{1,0:T(8,128)(2,1)S(1)}, bf16[64,1024]{1,0:T(8,128)(2,1)S(1)}, u32[]{:S(2)}, u32[]{:S(2)}) %collective-permute-start.7) | collective-permute-done | bytes 131104 | tf_op jit(solution)/shard_map/gather_heads/ppermute | solution.py:284
  33.7 2.6 %collective-permute-done.8.h1 = bf16[64,1024]{1,0:T(8,128)(2,1)S(1)} collective-permute-done((bf16[64,1024]{1,0:T(8,128)(2,1)S(1)}, bf16[64,1024]{1,0:T(8,128)(2,1)S(1)}, u32[]{:S(2)}, u32[]{:S(2)}) %collective-permute-start.8) | collective-permute-done | bytes 131104 | tf_op jit(solution)/shard_map/gather_heads/ppermute | solution.py:284
  36.2 2.0 %collective-permute-start.9 = (bf16[64,1024]{1,0:T(8,128)(2,1)S(1)}, bf16[64,1024]{1,0:T(8,128)(2,1)S(1)}, u32[]{:S(2)}, u32[]{:S(2)}) collective-permute-start(bf16[64,1024]{1,0:T(8,128)(2,1)S(1)} %collective-permute-done.7.h2), channel_id=1, source_target_pairs={{0,4},{4,0},{8,12},{12,8},{1,5},{5,1},{9,13},{13,9},{2,6},{6,2},{1... | collective-permute-start | bytes 393224 | tf_op jit(solution)/shard_map/gather_heads/ppermute | solution.py:284
  38.3 0.7 collective-permute-start.10
  39.3 1.4 %collective-permute-start.13 = (bf16[64,1024]{1,0:T(8,128)(2,1)S(1)}, bf16[64,1024]{1,0:T(8,128)(2,1)S(1)}, u32[]{:S(2)}, u32[]{:S(2)}) collective-permute-start(bf16[64,1024]{1,0:T(8,128)(2,1)S(1)} %collective-permute-done.12.h2), channel_id=1, source_target_pairs={{0,4},{4,0},{8,12},{12,8},{1,5},{5,1},{9,13},{13,9},{2,6},{6,2},{1... | collective-permute-start | bytes 393224 | tf_op jit(solution)/shard_map/gather_heads/ppermute | solution.py:284
  40.7 1.9 %collective-permute-done.11.h1 = bf16[64,1024]{1,0:T(8,128)(2,1)S(1)} collective-permute-done((bf16[64,1024]{1,0:T(8,128)(2,1)S(1)}, bf16[64,1024]{1,0:T(8,128)(2,1)S(1)}, u32[]{:S(2)}, u32[]{:S(2)}) %collective-permute-start.11) | collective-permute-done | bytes 131104 | tf_op jit(solution)/shard_map/gather_heads/ppermute | solution.py:284
  42.7 4.0 %collective-permute-done.9.h3 = bf16[64,1024]{1,0:T(8,128)(2,1)S(1)} collective-permute-done((bf16[64,1024]{1,0:T(8,128)(2,1)S(1)}, bf16[64,1024]{1,0:T(8,128)(2,1)S(1)}, u32[]{:S(2)}, u32[]{:S(2)}) %collective-permute-start.9) | collective-permute-done | bytes 131104 | tf_op jit(solution)/shard_map/gather_heads/ppermute | solution.py:284
  46.7 1.3 %project.4.first_ref = f32[256,896]{1,0:T(8,128)S(1)} custom-call(s32[3]{0:T(128)S(1)} %pad_add_fusion.bits_ref, bf16[64,1024]{1,0:T(8,128)(2,1)S(1)} %attend.4.h0, bf16[64,1024]{1,0:T(8,128)(2,1)S(1)} %collective-permute-done.8.h1, bf16[64,1024]{1,0:T(8,128)(2,1)S(1)} %collective-permute-done.7.h2, bf16[64,1024]{1,0:T(8,128)(2,1)S(1)} %collective-permute-done.9.h3, ...), custom_call_target="tpu_custom_call" | custom-call | flops 1469762048 | bytes 5111820 | tf_op jit(solution)/shard_map/project/pallas_call | solution.py:28
  48.0 3.2 %collective-permute-done.13.h3 = bf16[64,1024]{1,0:T(8,128)(2,1)S(1)} collective-permute-done((bf16[64,1024]{1,0:T(8,128)(2,1)S(1)}, bf16[64,1024]{1,0:T(8,128)(2,1)S(1)}, u32[]{:S(2)}, u32[]{:S(2)}) %collective-permute-start.13) | collective-permute-done | bytes 131104 | tf_op jit(solution)/shard_map/gather_heads/ppermute | solution.py:284
  51.2 1.3 %project.5 = (f32[128,896]{1,0:T(8,128)S(1)}, bf16[128,896]{1,0:T(8,128)(2,1)S(1)}) custom-call(s32[3]{0:T(128)S(1)} %pad_add_fusion.bits_ref, f32[256,896]{1,0:T(8,128)S(1)} %project.4.first_ref, bf16[64,1024]{1,0:T(8,128)(2,1)S(1)} %attend.5.h0, bf16[64,1024]{1,0:T(8,128)(2,1)S(1)} %collective-permute-done.11.h1, ...), custom_call_target="tpu_custom_call" | custom-call | flops 1469762048 | bytes 5799948 | tf_op jit(solution)/shard_map/project/pallas_call | solution.py:28
  52.6 1.5 %collective-permute-done.14.got_ref = bf16[128,896]{1,0:T(8,128)(2,1)S(1)} collective-permute-done((bf16[128,896]{1,0:T(8,128)(2,1)S(1)}, bf16[128,896]{1,0:T(8,128)(2,1)S(1)}, u32[]{:S(2)}, u32[]{:S(2)}) %collective-permute-start.14) | collective-permute-done | bytes 229408 | tf_op jit(solution)/shard_map/project/ppermute | solution.py:287
  54.1 0.6 project.6
  54.8 5.2 %collective-permute-done.15.got_ref = bf16[64,896]{1,0:T(8,128)(2,1)S(1)} collective-permute-done((bf16[64,896]{1,0:T(8,128)(2,1)S(1)}, bf16[64,896]{1,0:T(8,128)(2,1)S(1)}, u32[]{:S(2)}, u32[]{:S(2)}) %collective-permute-start.15) | collective-permute-done | bytes 114720 | tf_op jit(solution)/shard_map/project/ppermute | solution.py:287
  60.3 0.8 collective-permute-start.16
  61.1 4.1 %collective-permute-start.17 = (bf16[48,896]{1,0:T(8,128)(2,1)S(1)}, bf16[48,896]{1,0:T(8,128)(2,1)S(1)}, u32[]{:S(2)}, u32[]{:S(2)}) collective-permute-start(bf16[48,896]{1,0:T(8,128)(2,1)S(1)} %get-tuple-element.69), channel_id=1, source_target_pairs={{0,8},{1,12},{2,0},{3,4},{4,9},{5,13},{6,1},{7,5},{8,10},{9,14},{1... | collective-permute-start | bytes 258056 | tf_op jit(solution)/shard_map/scatter_resid/ppermute | solution.py:291
  65.1 1.1 %collective-permute-start.18 = (bf16[48,896]{1,0:T(8,128)(2,1)S(1)}, bf16[48,896]{1,0:T(8,128)(2,1)S(1)}, u32[]{:S(2)}, u32[]{:S(2)}) collective-permute-start(bf16[48,896]{1,0:T(8,128)(2,1)S(1)} %get-tuple-element.70), channel_id=1, source_target_pairs={{0,12},{1,0},{2,4},{3,8},{4,13},{5,1},{6,5},{7,9},{8,14},{9,2},{10... | collective-permute-start | bytes 258056 | tf_op jit(solution)/shard_map/scatter_resid/ppermute | solution.py:291
  66.2 1.4 %collective-permute-done.17.a0 = bf16[48,896]{1,0:T(8,128)(2,1)S(1)} collective-permute-done((bf16[48,896]{1,0:T(8,128)(2,1)S(1)}, bf16[48,896]{1,0:T(8,128)(2,1)S(1)}, u32[]{:S(2)}, u32[]{:S(2)}) %collective-permute-start.17) | collective-permute-done | bytes 86048 | tf_op jit(solution)/shard_map/scatter_resid/ppermute | solution.py:291
  67.6 1.0 collective-permute-done.18.a1
  68.6 1.7 %collective-permute-done.19.a3 = bf16[48,896]{1,0:T(8,128)(2,1)S(1)} collective-permute-done((bf16[48,896]{1,0:T(8,128)(2,1)S(1)}, bf16[48,896]{1,0:T(8,128)(2,1)S(1)}, u32[]{:S(2)}, u32[]{:S(2)}) %collective-permute-start.19) | collective-permute-done | bytes 86048 | tf_op jit(solution)/shard_map/scatter_resid/ppermute | solution.py:291
  70.3 1.7 %expand.4 = (bf16[96,2176]{1,0:T(8,128)(2,1)S(1)}, bf16[96,2176]{1,0:T(8,128)(2,1)S(1)}) custom-call(s32[3]{0:T(128)S(1)} %pad_add_fusion.bits_ref, bf16[4,48,64]{2,1,0:T(8,128)(2,1)S(1)} %get-tuple-element.67.pick_ref, bf16[48,896]{1,0:T(8,128)(2,1)S(1)} %collective-permute-done.17.a0, bf16[48,896]{1,0:T(8,128)(2,1)S(1)} %collective-permute-done.18.a1, ...), custom_call_target="tpu_custom_call" | custom-call | flops 1704643072 | bytes 4904716 | tf_op jit(solution)/shard_map/expand/pallas_call | solution.py:28
  72.0 1.2 %collective-permute-start.20 = (bf16[96,2176]{1,0:T(8,128)(2,1)S(1)}, bf16[96,2176]{1,0:T(8,128)(2,1)S(1)}, u32[]{:S(2)}, u32[]{:S(2)}) collective-permute-start(bf16[96,2176]{1,0:T(8,128)(2,1)S(1)} %get-tuple-element.73), channel_id=1, source_target_pairs={{0,1},{1,0},{2,3},{3,2},{4,5},{5,4},{6,7},{7,6},{8,9},{9,8},{10,11... | collective-permute-start | bytes 1253384 | tf_op jit(solution)/shard_map/expand/ppermute | solution.py:287
  73.2 1.4 %collective-permute-done.20.got_ref = bf16[96,2176]{1,0:T(8,128)(2,1)S(1)} collective-permute-done((bf16[96,2176]{1,0:T(8,128)(2,1)S(1)}, bf16[96,2176]{1,0:T(8,128)(2,1)S(1)}, u32[]{:S(2)}, u32[]{:S(2)}) %collective-permute-start.20) | collective-permute-done | bytes 417824 | tf_op jit(solution)/shard_map/expand/ppermute | solution.py:287
  74.7 2.6 %collective-permute-start.21 = (bf16[48,2176]{1,0:T(8,128)(2,1)S(1)}, bf16[48,2176]{1,0:T(8,128)(2,1)S(1)}, u32[]{:S(2)}, u32[]{:S(2)}) collective-permute-start(bf16[48,2176]{1,0:T(8,128)(2,1)S(1)} %get-tuple-element.76), channel_id=1, source_target_pairs={{0,2},{1,3},{2,0},{3,1},{4,6},{5,7},{6,4},{7,5},{8,10},{9,11},{10,... | collective-permute-start | bytes 626696 | tf_op jit(solution)/shard_map/expand/ppermute | solution.py:287
  77.4 5.9 %collective-permute-done.21.got_ref = bf16[48,2176]{1,0:T(8,128)(2,1)S(1)} collective-permute-done((bf16[48,2176]{1,0:T(8,128)(2,1)S(1)}, bf16[48,2176]{1,0:T(8,128)(2,1)S(1)}, u32[]{:S(2)}, u32[]{:S(2)}) %collective-permute-start.21) | collective-permute-done | bytes 208928 | tf_op jit(solution)/shard_map/expand/ppermute | solution.py:287
  83.5 1.3 %collective-permute-done.22.other_ref = bf16[48,1024]{1,0:T(8,128)(2,1)S(1)} collective-permute-done((bf16[48,1024]{1,0:T(8,128)(2,1)S(1)}, bf16[48,1024]{1,0:T(8,128)(2,1)S(1)}, u32[]{:S(2)}, u32[]{:S(2)}) %collective-permute-start.22) | collective-permute-done | bytes 98336 | tf_op jit(solution)/shard_map/contract/ppermute | solution.py:287
  84.8 1.0 %contract.2 = (bf16[48,896]{1,0:T(8,128)(2,1)S(1)}, bf16[48,896]{1,0:T(8,128)(2,1)S(1)}) custom-call(s32[3]{0:T(128)S(1)} %pad_add_fusion.bits_ref, bf16[48,1024]{1,0:T(8,128)(2,1)S(1)} %expand.6.mine_ref, bf16[48,1024]{1,0:T(8,128)(2,1)S(1)} %collective-permute-done.22.other_ref, bf16[1024,896]{1,0:T(8,128)(2,1)S(1)} %bitcast.14), custom_call_target="tpu_custom_call" | custom-call | flops 1176160768 | bytes 2203660 | tf_op jit(solution)/shard_map/contract/pallas_call | solution.py:28
  85.8 1.4 %collective-permute-done.23.got_ref = bf16[48,2176]{1,0:T(8,128)(2,1)S(1)} collective-permute-done((bf16[48,2176]{1,0:T(8,128)(2,1)S(1)}, bf16[48,2176]{1,0:T(8,128)(2,1)S(1)}, u32[]{:S(2)}, u32[]{:S(2)}) %collective-permute-start.23) | collective-permute-done | bytes 208928 | tf_op jit(solution)/shard_map/expand/ppermute | solution.py:287
  87.5 2.1 %collective-permute-start.26 = (bf16[48,896]{1,0:T(8,128)(2,1)S(1)}, bf16[48,896]{1,0:T(8,128)(2,1)S(1)}, u32[]{:S(2)}, u32[]{:S(2)}) collective-permute-start(bf16[48,896]{1,0:T(8,128)(2,1)S(1)} %get-tuple-element.83), channel_id=1, source_target_pairs={{0,8},{4,12},{8,0},{12,4},{1,9},{5,13},{9,1},{13,5},{2,10},{6,14},... | collective-permute-start | bytes 258056 | tf_op jit(solution)/shard_map/combine/ppermute | solution.py:294
  89.6 1.2 %collective-permute-start.27 = (bf16[48,896]{1,0:T(8,128)(2,1)S(1)}, bf16[48,896]{1,0:T(8,128)(2,1)S(1)}, u32[]{:S(2)}, u32[]{:S(2)}) collective-permute-start(bf16[48,896]{1,0:T(8,128)(2,1)S(1)} %get-tuple-element.84), channel_id=1, source_target_pairs={{0,4},{4,8},{8,12},{12,0},{1,5},{5,9},{9,13},{13,1},{2,6},{6,10},{... | collective-permute-start | bytes 258056 | tf_op jit(solution)/shard_map/combine/ppermute | solution.py:294
  90.7 1.0 contract.3
  91.8 2.7 %collective-permute-start.25 = (bf16[48,896]{1,0:T(8,128)(2,1)S(1)}, bf16[48,896]{1,0:T(8,128)(2,1)S(1)}, u32[]{:S(2)}, u32[]{:S(2)}) collective-permute-start(bf16[48,896]{1,0:T(8,128)(2,1)S(1)} %get-tuple-element.82), channel_id=1, source_target_pairs={{0,12},{4,0},{8,4},{12,8},{1,13},{5,1},{9,5},{13,9},{2,14},{6,2},{... | collective-permute-start | bytes 258056 | tf_op jit(solution)/shard_map/combine/ppermute | solution.py:294
  94.5 3.1 %collective-permute-done.26.r2 = bf16[48,896]{1,0:T(8,128)(2,1)S(1)} collective-permute-done((bf16[48,896]{1,0:T(8,128)(2,1)S(1)}, bf16[48,896]{1,0:T(8,128)(2,1)S(1)}, u32[]{:S(2)}, u32[]{:S(2)}) %collective-permute-start.26) | collective-permute-done | bytes 86048 | tf_op jit(solution)/shard_map/combine/ppermute | solution.py:294
  97.5 1.3 %collective-permute-done.25.r1 = bf16[48,896]{1,0:T(8,128)(2,1)S(1)} collective-permute-done((bf16[48,896]{1,0:T(8,128)(2,1)S(1)}, bf16[48,896]{1,0:T(8,128)(2,1)S(1)}, u32[]{:S(2)}, u32[]{:S(2)}) %collective-permute-start.25) | collective-permute-done | bytes 86048 | tf_op jit(solution)/shard_map/combine/ppermute | solution.py:294
  98.9 0.9 combine.1
  (45 shorter events, 3.2 us)
Async XLA Ops:
  0.9 11.5 %collective-permute-start.1 = (bf16[288,256]{1,0:T(8,128)(2,1)S(1)}, bf16[288,256]{1,0:T(8,128)(2,1)S(1)}, u32[]{:S(2)}, u32[]{:S(2)}) collective-permute-start(bf16[288,256]{1,0:T(8,128)(2,1)S(1)} %dynamic-slice_bitcast_fusion), channel_id=1, source_target_pairs={{0,4},{4,8},{8,12},{12,0},{1,5},{5,9},{9,13},{13,1},{2,6},{6,10},{... | collective-permute-start | bytes 442376 | tf_op jit(solution)/shard_map/gather_cache/ppermute | solution.py:294
  4.0 12.3 %collective-permute-start.3 = (bf16[288,256]{1,0:T(8,128)(2,1)S(1)}, bf16[288,256]{1,0:T(8,128)(2,1)S(1)}, u32[]{:S(2)}, u32[]{:S(2)}) collective-permute-start(bf16[288,256]{1,0:T(8,128)(2,1)S(1)} %dynamic-slice_bitcast_fusion), channel_id=1, source_target_pairs={{0,8},{4,12},{8,0},{12,4},{1,9},{5,13},{9,1},{13,5},{2,10},{6,14},... | collective-permute-start | bytes 442376 | tf_op jit(solution)/shard_map/gather_cache/ppermute | solution.py:294
  6.6 9.7 %collective-permute-start.5 = (bf16[288,256]{1,0:T(8,128)(2,1)S(1)}, bf16[288,256]{1,0:T(8,128)(2,1)S(1)}, u32[]{:S(2)}, u32[]{:S(2)}) collective-permute-start(bf16[288,256]{1,0:T(8,128)(2,1)S(1)} %dynamic-slice_bitcast_fusion), channel_id=1, source_target_pairs={{0,12},{4,0},{8,4},{12,8},{1,13},{5,1},{9,5},{13,9},{2,14},{6,2},{... | collective-permute-start | bytes 442376 | tf_op jit(solution)/shard_map/gather_cache/ppermute | solution.py:294
  7.9 3.6 %collective-permute-start = (s32[2,64]{1,0:T(2,128)}, s32[2,64]{1,0:T(2,128)S(1)}, u32[]{:S(2)}, u32[]{:S(2)}) collective-permute-start(s32[2,64]{1,0:T(2,128)} %bitcast.16), channel_id=1, source_target_pairs={{0,0},{1,4},{2,8},{3,12},{4,1},{5,5},{6,9},{7,13},{8,2},{9,6},{10,... | collective-permute-start | bytes 1544 | tf_op jit(solution)/shard_map/routing/ppermute | solution.py:291
  9.3 2.2 %copy-start.4 = (s32[64,2]{0,1:T(2,128)S(1)}, s32[64,2]{0,1:T(2,128)}, u32[]{:S(2)}) copy-start(s32[64,2]{0,1:T(2,128)} %param.24) | copy-start | bytes 1540
  9.3 2.2 %copy-start.5 = (f32[64,2]{0,1:T(2,128)S(1)}, f32[64,2]{0,1:T(2,128)}, u32[]{:S(2)}) copy-start(f32[64,2]{0,1:T(2,128)} %param.25) | copy-start | bytes 1540
  9.3 2.2 %copy-start.6 = (s32[64,1]{0,1:T(1,128)S(1)}, s32[64,1]{0,1:T(1,128)}, u32[]{:S(2)}) copy-start(s32[64,1]{0,1:T(1,128)} %param.16) | copy-start | bytes 772
  12.5 4.4 %collective-permute-start.2 = (bf16[288,256]{1,0:T(8,128)(2,1)S(1)}, bf16[288,256]{1,0:T(8,128)(2,1)S(1)}, u32[]{:S(2)}, u32[]{:S(2)}) collective-permute-start(bf16[288,256]{1,0:T(8,128)(2,1)S(1)} %collective-permute-done.1.refs_0_), channel_id=1, source_target_pairs={{0,1},{1,0},{2,3},{3,2},{4,5},{5,4},{6,7},{7,6},{8,9},{9,8},{10,11... | collective-permute-start | bytes 442376 | tf_op jit(solution)/shard_map/gather_cache/ppermute | solution.py:287
  16.3 1.4 %collective-permute-start.4 = (bf16[288,256]{1,0:T(8,128)(2,1)S(1)}, bf16[288,256]{1,0:T(8,128)(2,1)S(1)}, u32[]{:S(2)}, u32[]{:S(2)}) collective-permute-start(bf16[288,256]{1,0:T(8,128)(2,1)S(1)} %collective-permute-done.3.refs_2_), channel_id=1, source_target_pairs={{0,1},{1,0},{2,3},{3,2},{4,5},{5,4},{6,7},{7,6},{8,9},{9,8},{10,11... | collective-permute-start | bytes 442376 | tf_op jit(solution)/shard_map/gather_cache/ppermute | solution.py:287
  16.3 1.6 %collective-permute-start.6 = (bf16[288,256]{1,0:T(8,128)(2,1)S(1)}, bf16[288,256]{1,0:T(8,128)(2,1)S(1)}, u32[]{:S(2)}, u32[]{:S(2)}) collective-permute-start(bf16[288,256]{1,0:T(8,128)(2,1)S(1)} %collective-permute-done.5.refs_4_), channel_id=1, source_target_pairs={{0,1},{1,0},{2,3},{3,2},{4,5},{5,4},{6,7},{7,6},{8,9},{9,8},{10,11... | collective-permute-start | bytes 442376 | tf_op jit(solution)/shard_map/gather_cache/ppermute | solution.py:287
  21.3 16.9 %copy-start.8 = (bf16[64,896]{1,0:T(8,128)(2,1)S(1)}, bf16[64,896]{1,0:T(8,128)(2,1)}, u32[]{:S(2)}) copy-start(bf16[64,896]{1,0:T(8,128)(2,1)} %param.15) | copy-start | bytes 344068
  21.3 25.4 %copy-start = (bf16[2048,896]{1,0:T(8,128)(2,1)S(1)}, bf16[2048,896]{1,0:T(8,128)(2,1)}, u32[]{:S(2)}) copy-start(bf16[2048,896]{1,0:T(8,128)(2,1)} %w_ref.3) | copy-start | bytes 11010052
  21.3 12.3 %collective-permute-start.7 = (bf16[64,1024]{1,0:T(8,128)(2,1)S(1)}, bf16[64,1024]{1,0:T(8,128)(2,1)S(1)}, u32[]{:S(2)}, u32[]{:S(2)}) collective-permute-start(bf16[64,1024]{1,0:T(8,128)(2,1)S(1)} %attend.4.h0), channel_id=1, source_target_pairs={{0,8},{4,12},{8,0},{12,4},{1,9},{5,13},{9,1},{13,5},{2,10},{6,14},... | collective-permute-start | bytes 393224 | tf_op jit(solution)/shard_map/gather_heads/ppermute | solution.py:284
  27.0 9.3 %collective-permute-start.8 = (bf16[64,1024]{1,0:T(8,128)(2,1)S(1)}, bf16[64,1024]{1,0:T(8,128)(2,1)S(1)}, u32[]{:S(2)}, u32[]{:S(2)}) collective-permute-start(bf16[64,1024]{1,0:T(8,128)(2,1)S(1)} %attend.4.h0), channel_id=1, source_target_pairs={{0,4},{4,0},{8,12},{12,8},{1,5},{5,1},{9,13},{13,9},{2,6},{6,2},{1... | collective-permute-start | bytes 393224 | tf_op jit(solution)/shard_map/gather_heads/ppermute | solution.py:284
  30.1 9.2 %collective-permute-start.12 = (bf16[64,1024]{1,0:T(8,128)(2,1)S(1)}, bf16[64,1024]{1,0:T(8,128)(2,1)S(1)}, u32[]{:S(2)}, u32[]{:S(2)}) collective-permute-start(bf16[64,1024]{1,0:T(8,128)(2,1)S(1)} %attend.5.h0), channel_id=1, source_target_pairs={{0,8},{4,12},{8,0},{12,4},{1,9},{5,13},{9,1},{13,5},{2,10},{6,14},... | collective-permute-start | bytes 393224 | tf_op jit(solution)/shard_map/gather_heads/ppermute | solution.py:284
  36.2 6.4 %collective-permute-start.11 = (bf16[64,1024]{1,0:T(8,128)(2,1)S(1)}, bf16[64,1024]{1,0:T(8,128)(2,1)S(1)}, u32[]{:S(2)}, u32[]{:S(2)}) collective-permute-start(bf16[64,1024]{1,0:T(8,128)(2,1)S(1)} %attend.5.h0), channel_id=1, source_target_pairs={{0,4},{4,0},{8,12},{12,8},{1,5},{5,1},{9,13},{13,9},{2,6},{6,2},{1... | collective-permute-start | bytes 393224 | tf_op jit(solution)/shard_map/gather_heads/ppermute | solution.py:284
  36.2 10.5 %collective-permute-start.9 = (bf16[64,1024]{1,0:T(8,128)(2,1)S(1)}, bf16[64,1024]{1,0:T(8,128)(2,1)S(1)}, u32[]{:S(2)}, u32[]{:S(2)}) collective-permute-start(bf16[64,1024]{1,0:T(8,128)(2,1)S(1)} %collective-permute-done.7.h2), channel_id=1, source_target_pairs={{0,4},{4,0},{8,12},{12,8},{1,5},{5,1},{9,13},{13,9},{2,6},{6,2},{1... | collective-permute-start | bytes 393224 | tf_op jit(solution)/shard_map/gather_heads/ppermute | solution.py:284
  38.3 2.5 %collective-permute-start.10 = (bf16[64,896]{1,0:T(8,128)(2,1)S(1)}, bf16[64,896]{1,0:T(8,128)(2,1)S(1)}, u32[]{:S(2)}, u32[]{:S(2)}) collective-permute-start(bf16[64,896]{1,0:T(8,128)(2,1)S(1)} %copy-done.8), channel_id=1, source_target_pairs={{0,0},{1,4},{2,8},{3,12},{4,1},{5,5},{6,9},{7,13},{8,2},{9,6},{10,... | collective-permute-start | bytes 344072 | tf_op jit(solution)/shard_map/attend/ppermute | solution.py:291
  39.3 11.9 %collective-permute-start.13 = (bf16[64,1024]{1,0:T(8,128)(2,1)S(1)}, bf16[64,1024]{1,0:T(8,128)(2,1)S(1)}, u32[]{:S(2)}, u32[]{:S(2)}) collective-permute-start(bf16[64,1024]{1,0:T(8,128)(2,1)S(1)} %collective-permute-done.12.h2), channel_id=1, source_target_pairs={{0,4},{4,0},{8,12},{12,8},{1,5},{5,1},{9,13},{13,9},{2,6},{6,2},{1... | collective-permute-start | bytes 393224 | tf_op jit(solution)/shard_map/gather_heads/ppermute | solution.py:284
  52.6 1.6 %collective-permute-start.14 = (bf16[128,896]{1,0:T(8,128)(2,1)S(1)}, bf16[128,896]{1,0:T(8,128)(2,1)S(1)}, u32[]{:S(2)}, u32[]{:S(2)}) collective-permute-start(bf16[128,896]{1,0:T(8,128)(2,1)S(1)} %get-tuple-element.63), channel_id=1, source_target_pairs={{0,1},{1,0},{2,3},{3,2},{4,5},{5,4},{6,7},{7,6},{8,9},{9,8},{10,11... | collective-permute-start | bytes 688136 | tf_op jit(solution)/shard_map/project/ppermute | solution.py:287
  54.7 5.3 %collective-permute-start.15 = (bf16[64,896]{1,0:T(8,128)(2,1)S(1)}, bf16[64,896]{1,0:T(8,128)(2,1)S(1)}, u32[]{:S(2)}, u32[]{:S(2)}) collective-permute-start(bf16[64,896]{1,0:T(8,128)(2,1)S(1)} %get-tuple-element.65), channel_id=1, source_target_pairs={{0,2},{1,3},{2,0},{3,1},{4,6},{5,7},{6,4},{7,5},{8,10},{9,11},{10,... | collective-permute-start | bytes 344072 | tf_op jit(solution)/shard_map/project/ppermute | solution.py:287
  60.0 6.2 %copy-start.7 = (bf16[896]{0:T(1024)(128)(2,1)S(1)}, bf16[896]{0:T(1024)(128)(2,1)}, u32[]{:S(2)}) copy-start(bf16[896]{0:T(1024)(128)(2,1)} %param.20) | copy-start | bytes 5380
  60.0 10.3 %copy-start.1 = (bf16[1,896,1024]{2,1,0:T(8,128)(2,1)S(1)}, bf16[1,896,1024]{2,1,0:T(8,128)(2,1)}, u32[]{:S(2)}) copy-start(bf16[1,896,1024]{2,1,0:T(8,128)(2,1)} %param.21) | copy-start | bytes 5505028
  60.0 10.3 %copy-start.2 = (bf16[1,896,1024]{2,1,0:T(8,128)(2,1)S(1)}, bf16[1,896,1024]{2,1,0:T(8,128)(2,1)}, u32[]{:S(2)}) copy-start(bf16[1,896,1024]{2,1,0:T(8,128)(2,1)} %param.22) | copy-start | bytes 5505028
  60.3 10.0 %collective-permute-start.16 = (bf16[64,896]{1,0:T(8,128)(2,1)S(1)}, bf16[64,896]{1,0:T(8,128)(2,1)S(1)}, u32[]{:S(2)}, u32[]{:S(2)}) collective-permute-start(bf16[64,896]{1,0:T(8,128)(2,1)S(1)} %get-tuple-element.68), channel_id=1, source_target_pairs={{0,0},{1,4},{2,8},{3,12},{4,1},{5,5},{6,9},{7,13},{8,2},{9,6},{10,... | collective-permute-start | bytes 344072 | tf_op jit(solution)/shard_map/scatter_resid/ppermute | solution.py:291
  61.1 6.6 %collective-permute-start.17 = (bf16[48,896]{1,0:T(8,128)(2,1)S(1)}, bf16[48,896]{1,0:T(8,128)(2,1)S(1)}, u32[]{:S(2)}, u32[]{:S(2)}) collective-permute-start(bf16[48,896]{1,0:T(8,128)(2,1)S(1)} %get-tuple-element.69), channel_id=1, source_target_pairs={{0,8},{1,12},{2,0},{3,4},{4,9},{5,13},{6,1},{7,5},{8,10},{9,14},{1... | collective-permute-start | bytes 258056 | tf_op jit(solution)/shard_map/scatter_resid/ppermute | solution.py:291
  65.1 3.4 %collective-permute-start.18 = (bf16[48,896]{1,0:T(8,128)(2,1)S(1)}, bf16[48,896]{1,0:T(8,128)(2,1)S(1)}, u32[]{:S(2)}, u32[]{:S(2)}) collective-permute-start(bf16[48,896]{1,0:T(8,128)(2,1)S(1)} %get-tuple-element.70), channel_id=1, source_target_pairs={{0,12},{1,0},{2,4},{3,8},{4,13},{5,1},{6,5},{7,9},{8,14},{9,2},{10... | collective-permute-start | bytes 258056 | tf_op jit(solution)/shard_map/scatter_resid/ppermute | solution.py:291
  66.2 4.0 %collective-permute-start.19 = (bf16[48,896]{1,0:T(8,128)(2,1)S(1)}, bf16[48,896]{1,0:T(8,128)(2,1)S(1)}, u32[]{:S(2)}, u32[]{:S(2)}) collective-permute-start(bf16[48,896]{1,0:T(8,128)(2,1)S(1)} %get-tuple-element.71), channel_id=1, source_target_pairs={{0,4},{1,8},{2,12},{3,0},{4,5},{5,9},{6,13},{7,1},{8,6},{9,10},{10... | collective-permute-start | bytes 258056 | tf_op jit(solution)/shard_map/scatter_resid/ppermute | solution.py:291
  72.0 2.6 %collective-permute-start.20 = (bf16[96,2176]{1,0:T(8,128)(2,1)S(1)}, bf16[96,2176]{1,0:T(8,128)(2,1)S(1)}, u32[]{:S(2)}, u32[]{:S(2)}) collective-permute-start(bf16[96,2176]{1,0:T(8,128)(2,1)S(1)} %get-tuple-element.73), channel_id=1, source_target_pairs={{0,1},{1,0},{2,3},{3,2},{4,5},{5,4},{6,7},{7,6},{8,9},{9,8},{10,11... | collective-permute-start | bytes 1253384 | tf_op jit(solution)/shard_map/expand/ppermute | solution.py:287
  74.7 8.5 %collective-permute-start.21 = (bf16[48,2176]{1,0:T(8,128)(2,1)S(1)}, bf16[48,2176]{1,0:T(8,128)(2,1)S(1)}, u32[]{:S(2)}, u32[]{:S(2)}) collective-permute-start(bf16[48,2176]{1,0:T(8,128)(2,1)S(1)} %get-tuple-element.76), channel_id=1, source_target_pairs={{0,2},{1,3},{2,0},{3,1},{4,6},{5,7},{6,4},{7,5},{8,10},{9,11},{10,... | collective-permute-start | bytes 626696 | tf_op jit(solution)/shard_map/expand/ppermute | solution.py:287
  77.3 9.9 %collective-permute-start.23 = (bf16[48,2176]{1,0:T(8,128)(2,1)S(1)}, bf16[48,2176]{1,0:T(8,128)(2,1)S(1)}, u32[]{:S(2)}, u32[]{:S(2)}) collective-permute-start(bf16[48,2176]{1,0:T(8,128)(2,1)S(1)} %get-tuple-element.79), channel_id=1, source_target_pairs={{0,2},{1,3},{2,0},{3,1},{4,6},{5,7},{6,4},{7,5},{8,10},{9,11},{10,... | collective-permute-start | bytes 626696 | tf_op jit(solution)/shard_map/expand/ppermute | solution.py:287
  83.3 1.5 %copy-start.3 = (bf16[1,1024,896]{2,1,0:T(8,128)(2,1)S(1)}, bf16[1,1024,896]{2,1,0:T(8,128)(2,1)}, u32[]{:S(2)}) copy-start(bf16[1,1024,896]{2,1,0:T(8,128)(2,1)} %param.23) | copy-start | bytes 5505028
  83.4 1.4 %collective-permute-start.22 = (bf16[48,1024]{1,0:T(8,128)(2,1)S(1)}, bf16[48,1024]{1,0:T(8,128)(2,1)S(1)}, u32[]{:S(2)}, u32[]{:S(2)}) collective-permute-start(bf16[48,1024]{1,0:T(8,128)(2,1)S(1)} %expand.6.mine_ref), channel_id=1, source_target_pairs={{0,1},{1,0},{2,3},{3,2},{4,5},{5,4},{6,7},{7,6},{8,9},{9,8},{10,11... | collective-permute-start | bytes 294920 | tf_op jit(solution)/shard_map/contract/ppermute | solution.py:287
  87.4 3.3 %collective-permute-start.24 = (bf16[48,1024]{1,0:T(8,128)(2,1)S(1)}, bf16[48,1024]{1,0:T(8,128)(2,1)S(1)}, u32[]{:S(2)}, u32[]{:S(2)}) collective-permute-start(bf16[48,1024]{1,0:T(8,128)(2,1)S(1)} %expand.7.mine_ref), channel_id=1, source_target_pairs={{0,1},{1,0},{2,3},{3,2},{4,5},{5,4},{6,7},{7,6},{8,9},{9,8},{10,11... | collective-permute-start | bytes 294920 | tf_op jit(solution)/shard_map/contract/ppermute | solution.py:287
  87.5 10.0 %collective-permute-start.26 = (bf16[48,896]{1,0:T(8,128)(2,1)S(1)}, bf16[48,896]{1,0:T(8,128)(2,1)S(1)}, u32[]{:S(2)}, u32[]{:S(2)}) collective-permute-start(bf16[48,896]{1,0:T(8,128)(2,1)S(1)} %get-tuple-element.83), channel_id=1, source_target_pairs={{0,8},{4,12},{8,0},{12,4},{1,9},{5,13},{9,1},{13,5},{2,10},{6,14},... | collective-permute-start | bytes 258056 | tf_op jit(solution)/shard_map/combine/ppermute | solution.py:294
  89.6 8.0 %collective-permute-start.27 = (bf16[48,896]{1,0:T(8,128)(2,1)S(1)}, bf16[48,896]{1,0:T(8,128)(2,1)S(1)}, u32[]{:S(2)}, u32[]{:S(2)}) collective-permute-start(bf16[48,896]{1,0:T(8,128)(2,1)S(1)} %get-tuple-element.84), channel_id=1, source_target_pairs={{0,4},{4,8},{8,12},{12,0},{1,5},{5,9},{9,13},{13,1},{2,6},{6,10},{... | collective-permute-start | bytes 258056 | tf_op jit(solution)/shard_map/combine/ppermute | solution.py:294
  91.8 7.1 %collective-permute-start.25 = (bf16[48,896]{1,0:T(8,128)(2,1)S(1)}, bf16[48,896]{1,0:T(8,128)(2,1)S(1)}, u32[]{:S(2)}, u32[]{:S(2)}) collective-permute-start(bf16[48,896]{1,0:T(8,128)(2,1)S(1)} %get-tuple-element.82), channel_id=1, source_target_pairs={{0,12},{4,0},{8,4},{12,8},{1,13},{5,1},{9,5},{13,9},{2,14},{6,2},{... | collective-permute-start | bytes 258056 | tf_op jit(solution)/shard_map/combine/ppermute | solution.py:294

commit v5 on v4

--- a/solution.py
+++ b/solution.py
@@ -185,10 +185,15 @@
     second_ref[...] = result[slots:]
 
 
-def combine_kernel(put_ref, weight_ref, resid_ref, r0, r1, r2, r3, out_ref):
+def combine_early_kernel(put_ref, weight_ref, resid_ref, r0, r2, r3, out_ref):
     total = resid_ref[...].astype(F32)
-    for k, got in enumerate((r0, r1, r2, r3)):
+    for k, got in ((0, r0), (2, r2), (3, r3)):
         total = total + weight_ref[:, k : k + 1] * dot(put_ref[k], got[...])
+    out_ref[...] = total
+
+
+def combine_kernel(put_ref, weight_ref, early_ref, r1, out_ref):
+    total = early_ref[...] + weight_ref[:, 1:2] * dot(put_ref[1], r1[...])
     out_ref[...] = total.astype(BF16)
 
 
@@ -448,12 +453,19 @@
             )
     with jax.named_scope("combine"):
         back = [along(out, -k) if k else out for k, out in sorted(zip(order, outs), key=lambda pair: pair[0])]
+        (early,) = call(
+            combine_early_kernel,
+            [shape((rows, width), F32)],
+            [VMEM] * 6,
+            (put, weights, resid, back[0], back[2], back[3]),
+            6 * rows * slots * width,
+        )
         (scored,) = call(
             combine_kernel,
             [shape((rows, width), BF16)],
-            [VMEM] * 7,
-            (put, weights, resid, *back),
-            2 * count * rows * slots * width,
+            [VMEM] * 4,
+            (put, weights, early, back[1]),
+            2 * rows * slots * width,
         )
     return scored
 

time: 100 us -> 99.9 us (level)
    pallas_call x15 -> x16, Pallas kernels: 15.7 us -> 15.9 us  [call(): pl.pallas_call(kernel, out_shape=outs, in_specs=specs, out_specs=[VMEM] *...]
  transfers between devices with their start and end apart: 28 -> 28, of which waited for: 20 -> 20; matrix products, arithmetic and copies ran while one was open for 0% -> 0% of each run, Pallas kernels for 9% -> 10%
where the time goes in v5:
time: 99.9 us; the launch traced here: 99.7 us
  waiting for transfers between devices  42.4 us (42%)
  starting transfers between devices  38 us (38%)
  Pallas kernels  18 us (18%)
    ppermute x10, waiting for transfers between devices, swap(): return lax.ppermute(value, 'tensor', [(i, i ^ mask) for i in range(count)])  17.7 us
    pallas_call x16, Pallas kernels, call(): pl.pallas_call(kernel, out_shape=outs, in_specs=specs, out_specs=[VMEM] *...  15.9 us
    ppermute x6, waiting for transfers between devices, across(): return lax.ppermute(value, 'expert', [(i, i ^ mask) for i in range(count)])  15.2 us
    ppermute x6, starting transfers between devices, along(): lax.ppermute(value, 'expert', [(i, (i + k) % count) for i in range(count)])  13 us
    ppermute x6, starting transfers between devices, across(): return lax.ppermute(value, 'expert', [(i, i ^ mask) for i in range(count)])  9.93 us
    ppermute x6, starting transfers between devices, both(): return lax.ppermute(value, ('expert', 'tensor'), pairs)  7.92 us
    ppermute x10, starting transfers between devices, swap(): return lax.ppermute(value, 'tensor', [(i, i ^ mask) for i in range(count)])  7.24 us
    ppermute x6, waiting for transfers between devices, along(): lax.ppermute(value, 'expert', [(i, (i + k) % count) for i in range(count)])  5.45 us
  transfers between devices with their start and end apart: 28, of which 20 were waited for; matrix products, arithmetic and copies ran while one was open for 0% of the time, Pallas kernels for 10%

profile of v5, /device:TPU:0, one launch (start us, length us, event | category | flops | bytes accessed | tf_op | source)
XLA Modules:
  0.0 99.7 jit_solution(15043618872653592965)
XLA Ops:
  0.0 0.9 dynamic-slice_bitcast_fusion
  0.9 3.1 %collective-permute-start.1 = (bf16[288,256]{1,0:T(8,128)(2,1)S(1)}, bf16[288,256]{1,0:T(8,128)(2,1)S(1)}, u32[]{:S(2)}, u32[]{:S(2)}) collective-permute-start(bf16[288,256]{1,0:T(8,128)(2,1)S(1)} %dynamic-slice_bitcast_fusion), channel_id=1, source_target_pairs={{0,4},{4,8},{8,12},{12,0},{1,5},{5,9},{9,13},{13,1},{2,6},{6,10},{... | collective-permute-start | bytes 442376 | tf_op jit(solution)/shard_map/gather_cache/ppermute | solution.py:299
  4.0 2.6 %collective-permute-start.3 = (bf16[288,256]{1,0:T(8,128)(2,1)S(1)}, bf16[288,256]{1,0:T(8,128)(2,1)S(1)}, u32[]{:S(2)}, u32[]{:S(2)}) collective-permute-start(bf16[288,256]{1,0:T(8,128)(2,1)S(1)} %dynamic-slice_bitcast_fusion), channel_id=1, source_target_pairs={{0,8},{4,12},{8,0},{12,4},{1,9},{5,13},{9,1},{13,5},{2,10},{6,14},... | collective-permute-start | bytes 442376 | tf_op jit(solution)/shard_map/gather_cache/ppermute | solution.py:299
  6.6 1.3 %collective-permute-start.5 = (bf16[288,256]{1,0:T(8,128)(2,1)S(1)}, bf16[288,256]{1,0:T(8,128)(2,1)S(1)}, u32[]{:S(2)}, u32[]{:S(2)}) collective-permute-start(bf16[288,256]{1,0:T(8,128)(2,1)S(1)} %dynamic-slice_bitcast_fusion), channel_id=1, source_target_pairs={{0,12},{4,0},{8,4},{12,8},{1,13},{5,1},{9,5},{13,9},{2,14},{6,2},{... | collective-permute-start | bytes 442376 | tf_op jit(solution)/shard_map/gather_cache/ppermute | solution.py:299
  7.9 1.3 %collective-permute-start = (s32[2,64]{1,0:T(2,128)}, s32[2,64]{1,0:T(2,128)S(1)}, u32[]{:S(2)}, u32[]{:S(2)}) collective-permute-start(s32[2,64]{1,0:T(2,128)} %bitcast.16), channel_id=1, source_target_pairs={{0,0},{1,4},{2,8},{3,12},{4,1},{5,5},{6,9},{7,13},{8,2},{9,6},{10,... | collective-permute-start | bytes 1544 | tf_op jit(solution)/shard_map/routing/ppermute | solution.py:296
  9.3 2.1 %query_layout.1 = (bf16[1024,576]{1,0:T(8,128)(2,1)S(1)}, bf16[64,576]{1,0:T(8,128)(2,1)S(1)}, bf16[576,256]{1,0:T(8,128)(2,1)S(1)}, bf16[16,512,128]{2,1,0:T(8,128)(2,1)S(1)}) custom-call(bf16[64,9216]{1,0:T(8,128)(2,1)} %q_ref.1, bf16[64,576]{1,0:T(8,128)(2,1)} %refs_0_.1, bf16[576,256]{1,0:T(8,128)(2,1)} %bitcast.20, bf16[16,512,128]{2,1,0:T(8,128)(2,1)} %refs_2_.1), custom_call_target="tpu_custom_call" | custom-call | flops 1000000000 | bytes 30000000 | tf_op jit(solution)/shard_map/query_layout/pallas_call | solution.py:311
  11.5 0.9 routing.1
  12.5 2.6 %collective-permute-start.2 = (bf16[288,256]{1,0:T(8,128)(2,1)S(1)}, bf16[288,256]{1,0:T(8,128)(2,1)S(1)}, u32[]{:S(2)}, u32[]{:S(2)}) collective-permute-start(bf16[288,256]{1,0:T(8,128)(2,1)S(1)} %collective-permute-done.1.refs_0_), channel_id=1, source_target_pairs={{0,1},{1,0},{2,3},{3,2},{4,5},{5,4},{6,7},{7,6},{8,9},{9,8},{10,11... | collective-permute-start | bytes 442376 | tf_op jit(solution)/shard_map/gather_cache/ppermute | solution.py:292
  15.0 1.3 %collective-permute-done.3.refs_2_ = bf16[288,256]{1,0:T(8,128)(2,1)S(1)} collective-permute-done((bf16[288,256]{1,0:T(8,128)(2,1)S(1)}, bf16[288,256]{1,0:T(8,128)(2,1)S(1)}, u32[]{:S(2)}, u32[]{:S(2)}) %collective-permute-start.3) | collective-permute-done | bytes 147488 | tf_op jit(solution)/shard_map/gather_cache/ppermute | solution.py:299
  16.8 0.9 collective-permute-done.4.refs_3_
  17.9 0.6 attend.3.far_ref
  18.5 2.8 %attend.4.h0 = bf16[64,1024]{1,0:T(8,128)(2,1)S(1)} custom-call(s32[64,1]{1,0:T(8,128)S(1)} %get-tuple-element.47.rel_ref, bf16[1024,576]{1,0:T(8,128)(2,1)S(1)} %get-tuple-element.49.q_ref, bf16[64,576]{1,0:T(8,128)(2,1)S(1)} %get-tuple-element.50.own_ref, bf16[576,256]{1,0:T(8,128)(2,1)S(1)} %get-tuple-element.51.near_ref, ...), custom_call_target="tpu_custom_call" | custom-call | flops 2140850688 | bytes 4661504 | tf_op jit(solution)/shard_map/attend/pallas_call | solution.py:28
  21.3 5.6 %collective-permute-start.7 = (bf16[64,1024]{1,0:T(8,128)(2,1)S(1)}, bf16[64,1024]{1,0:T(8,128)(2,1)S(1)}, u32[]{:S(2)}, u32[]{:S(2)}) collective-permute-start(bf16[64,1024]{1,0:T(8,128)(2,1)S(1)} %attend.4.h0), channel_id=1, source_target_pairs={{0,8},{4,12},{8,0},{12,4},{1,9},{5,13},{9,1},{13,5},{2,10},{6,14},... | collective-permute-start | bytes 393224 | tf_op jit(solution)/shard_map/gather_heads/ppermute | solution.py:289
  27.3 2.8 %attend.5.h0 = bf16[64,1024]{1,0:T(8,128)(2,1)S(1)} custom-call(s32[64,1]{1,0:T(8,128)S(1)} %get-tuple-element.47.rel_ref, bf16[1024,576]{1,0:T(8,128)(2,1)S(1)} %get-tuple-element.49.q_ref, bf16[64,576]{1,0:T(8,128)(2,1)S(1)} %get-tuple-element.50.own_ref, bf16[576,256]{1,0:T(8,128)(2,1)S(1)} %get-tuple-element.51.near_ref, ...), custom_call_target="tpu_custom_call" | custom-call | flops 2140850688 | bytes 4661504 | tf_op jit(solution)/shard_map/attend/pallas_call | solution.py:28
  30.6 3.0 %collective-permute-done.7.h2 = bf16[64,1024]{1,0:T(8,128)(2,1)S(1)} collective-permute-done((bf16[64,1024]{1,0:T(8,128)(2,1)S(1)}, bf16[64,1024]{1,0:T(8,128)(2,1)S(1)}, u32[]{:S(2)}, u32[]{:S(2)}) %collective-permute-start.7) | collective-permute-done | bytes 131104 | tf_op jit(solution)/shard_map/gather_heads/ppermute | solution.py:289
  33.7 2.6 %collective-permute-done.8.h1 = bf16[64,1024]{1,0:T(8,128)(2,1)S(1)} collective-permute-done((bf16[64,1024]{1,0:T(8,128)(2,1)S(1)}, bf16[64,1024]{1,0:T(8,128)(2,1)S(1)}, u32[]{:S(2)}, u32[]{:S(2)}) %collective-permute-start.8) | collective-permute-done | bytes 131104 | tf_op jit(solution)/shard_map/gather_heads/ppermute | solution.py:289
  36.2 2.0 %collective-permute-start.9 = (bf16[64,1024]{1,0:T(8,128)(2,1)S(1)}, bf16[64,1024]{1,0:T(8,128)(2,1)S(1)}, u32[]{:S(2)}, u32[]{:S(2)}) collective-permute-start(bf16[64,1024]{1,0:T(8,128)(2,1)S(1)} %collective-permute-done.7.h2), channel_id=1, source_target_pairs={{0,4},{4,0},{8,12},{12,8},{1,5},{5,1},{9,13},{13,9},{2,6},{6,2},{1... | collective-permute-start | bytes 393224 | tf_op jit(solution)/shard_map/gather_heads/ppermute | solution.py:289
  38.3 0.7 collective-permute-start.10
  39.3 1.4 %collective-permute-start.13 = (bf16[64,1024]{1,0:T(8,128)(2,1)S(1)}, bf16[64,1024]{1,0:T(8,128)(2,1)S(1)}, u32[]{:S(2)}, u32[]{:S(2)}) collective-permute-start(bf16[64,1024]{1,0:T(8,128)(2,1)S(1)} %collective-permute-done.12.h2), channel_id=1, source_target_pairs={{0,4},{4,0},{8,12},{12,8},{1,5},{5,1},{9,13},{13,9},{2,6},{6,2},{1... | collective-permute-start | bytes 393224 | tf_op jit(solution)/shard_map/gather_heads/ppermute | solution.py:289
  40.7 1.9 %collective-permute-done.11.h1 = bf16[64,1024]{1,0:T(8,128)(2,1)S(1)} collective-permute-done((bf16[64,1024]{1,0:T(8,128)(2,1)S(1)}, bf16[64,1024]{1,0:T(8,128)(2,1)S(1)}, u32[]{:S(2)}, u32[]{:S(2)}) %collective-permute-start.11) | collective-permute-done | bytes 131104 | tf_op jit(solution)/shard_map/gather_heads/ppermute | solution.py:289
  42.7 4.0 %collective-permute-done.9.h3 = bf16[64,1024]{1,0:T(8,128)(2,1)S(1)} collective-permute-done((bf16[64,1024]{1,0:T(8,128)(2,1)S(1)}, bf16[64,1024]{1,0:T(8,128)(2,1)S(1)}, u32[]{:S(2)}, u32[]{:S(2)}) %collective-permute-start.9) | collective-permute-done | bytes 131104 | tf_op jit(solution)/shard_map/gather_heads/ppermute | solution.py:289
  46.7 1.3 %project.4.first_ref = f32[256,896]{1,0:T(8,128)S(1)} custom-call(s32[3]{0:T(128)S(1)} %pad_add_fusion.bits_ref, bf16[64,1024]{1,0:T(8,128)(2,1)S(1)} %attend.4.h0, bf16[64,1024]{1,0:T(8,128)(2,1)S(1)} %collective-permute-done.8.h1, bf16[64,1024]{1,0:T(8,128)(2,1)S(1)} %collective-permute-done.7.h2, bf16[64,1024]{1,0:T(8,128)(2,1)S(1)} %collective-permute-done.9.h3, ...), custom_call_target="tpu_custom_call" | custom-call | flops 1469762048 | bytes 5111820 | tf_op jit(solution)/shard_map/project/pallas_call | solution.py:28
  48.0 3.2 %collective-permute-done.13.h3 = bf16[64,1024]{1,0:T(8,128)(2,1)S(1)} collective-permute-done((bf16[64,1024]{1,0:T(8,128)(2,1)S(1)}, bf16[64,1024]{1,0:T(8,128)(2,1)S(1)}, u32[]{:S(2)}, u32[]{:S(2)}) %collective-permute-start.13) | collective-permute-done | bytes 131104 | tf_op jit(solution)/shard_map/gather_heads/ppermute | solution.py:289
  51.2 1.3 %project.5 = (f32[128,896]{1,0:T(8,128)S(1)}, bf16[128,896]{1,0:T(8,128)(2,1)S(1)}) custom-call(s32[3]{0:T(128)S(1)} %pad_add_fusion.bits_ref, f32[256,896]{1,0:T(8,128)S(1)} %project.4.first_ref, bf16[64,1024]{1,0:T(8,128)(2,1)S(1)} %attend.5.h0, bf16[64,1024]{1,0:T(8,128)(2,1)S(1)} %collective-permute-done.11.h1, ...), custom_call_target="tpu_custom_call" | custom-call | flops 1469762048 | bytes 5799948 | tf_op jit(solution)/shard_map/project/pallas_call | solution.py:28
  52.6 1.5 %collective-permute-done.14.got_ref = bf16[128,896]{1,0:T(8,128)(2,1)S(1)} collective-permute-done((bf16[128,896]{1,0:T(8,128)(2,1)S(1)}, bf16[128,896]{1,0:T(8,128)(2,1)S(1)}, u32[]{:S(2)}, u32[]{:S(2)}) %collective-permute-start.14) | collective-permute-done | bytes 229408 | tf_op jit(solution)/shard_map/project/ppermute | solution.py:292
  54.1 0.6 project.6
  54.8 5.2 %collective-permute-done.15.got_ref = bf16[64,896]{1,0:T(8,128)(2,1)S(1)} collective-permute-done((bf16[64,896]{1,0:T(8,128)(2,1)S(1)}, bf16[64,896]{1,0:T(8,128)(2,1)S(1)}, u32[]{:S(2)}, u32[]{:S(2)}) %collective-permute-start.15) | collective-permute-done | bytes 114720 | tf_op jit(solution)/shard_map/project/ppermute | solution.py:292
  60.3 0.8 collective-permute-start.16
  61.1 4.1 %collective-permute-start.17 = (bf16[48,896]{1,0:T(8,128)(2,1)S(1)}, bf16[48,896]{1,0:T(8,128)(2,1)S(1)}, u32[]{:S(2)}, u32[]{:S(2)}) collective-permute-start(bf16[48,896]{1,0:T(8,128)(2,1)S(1)} %get-tuple-element.69), channel_id=1, source_target_pairs={{0,8},{1,12},{2,0},{3,4},{4,9},{5,13},{6,1},{7,5},{8,10},{9,14},{1... | collective-permute-start | bytes 258056 | tf_op jit(solution)/shard_map/scatter_resid/ppermute | solution.py:296
  65.1 1.1 %collective-permute-start.18 = (bf16[48,896]{1,0:T(8,128)(2,1)S(1)}, bf16[48,896]{1,0:T(8,128)(2,1)S(1)}, u32[]{:S(2)}, u32[]{:S(2)}) collective-permute-start(bf16[48,896]{1,0:T(8,128)(2,1)S(1)} %get-tuple-element.70), channel_id=1, source_target_pairs={{0,12},{1,0},{2,4},{3,8},{4,13},{5,1},{6,5},{7,9},{8,14},{9,2},{10... | collective-permute-start | bytes 258056 | tf_op jit(solution)/shard_map/scatter_resid/ppermute | solution.py:296
  66.2 1.4 %collective-permute-done.17.a0 = bf16[48,896]{1,0:T(8,128)(2,1)S(1)} collective-permute-done((bf16[48,896]{1,0:T(8,128)(2,1)S(1)}, bf16[48,896]{1,0:T(8,128)(2,1)S(1)}, u32[]{:S(2)}, u32[]{:S(2)}) %collective-permute-start.17) | collective-permute-done | bytes 86048 | tf_op jit(solution)/shard_map/scatter_resid/ppermute | solution.py:296
  67.6 1.0 collective-permute-done.18.a1
  68.6 1.7 %collective-permute-done.19.a3 = bf16[48,896]{1,0:T(8,128)(2,1)S(1)} collective-permute-done((bf16[48,896]{1,0:T(8,128)(2,1)S(1)}, bf16[48,896]{1,0:T(8,128)(2,1)S(1)}, u32[]{:S(2)}, u32[]{:S(2)}) %collective-permute-start.19) | collective-permute-done | bytes 86048 | tf_op jit(solution)/shard_map/scatter_resid/ppermute | solution.py:296
  70.3 1.7 %expand.4 = (bf16[96,2176]{1,0:T(8,128)(2,1)S(1)}, bf16[96,2176]{1,0:T(8,128)(2,1)S(1)}) custom-call(s32[3]{0:T(128)S(1)} %pad_add_fusion.bits_ref, bf16[4,48,64]{2,1,0:T(8,128)(2,1)S(1)} %get-tuple-element.67.pick_ref, bf16[48,896]{1,0:T(8,128)(2,1)S(1)} %collective-permute-done.17.a0, bf16[48,896]{1,0:T(8,128)(2,1)S(1)} %collective-permute-done.18.a1, ...), custom_call_target="tpu_custom_call" | custom-call | flops 1704643072 | bytes 4904716 | tf_op jit(solution)/shard_map/expand/pallas_call | solution.py:28
  72.0 1.2 %collective-permute-start.20 = (bf16[96,2176]{1,0:T(8,128)(2,1)S(1)}, bf16[96,2176]{1,0:T(8,128)(2,1)S(1)}, u32[]{:S(2)}, u32[]{:S(2)}) collective-permute-start(bf16[96,2176]{1,0:T(8,128)(2,1)S(1)} %get-tuple-element.73), channel_id=1, source_target_pairs={{0,1},{1,0},{2,3},{3,2},{4,5},{5,4},{6,7},{7,6},{8,9},{9,8},{10,11... | collective-permute-start | bytes 1253384 | tf_op jit(solution)/shard_map/expand/ppermute | solution.py:292
  73.2 1.4 %collective-permute-done.20.got_ref = bf16[96,2176]{1,0:T(8,128)(2,1)S(1)} collective-permute-done((bf16[96,2176]{1,0:T(8,128)(2,1)S(1)}, bf16[96,2176]{1,0:T(8,128)(2,1)S(1)}, u32[]{:S(2)}, u32[]{:S(2)}) %collective-permute-start.20) | collective-permute-done | bytes 417824 | tf_op jit(solution)/shard_map/expand/ppermute | solution.py:292
  74.7 2.6 %collective-permute-start.21 = (bf16[48,2176]{1,0:T(8,128)(2,1)S(1)}, bf16[48,2176]{1,0:T(8,128)(2,1)S(1)}, u32[]{:S(2)}, u32[]{:S(2)}) collective-permute-start(bf16[48,2176]{1,0:T(8,128)(2,1)S(1)} %get-tuple-element.76), channel_id=1, source_target_pairs={{0,2},{1,3},{2,0},{3,1},{4,6},{5,7},{6,4},{7,5},{8,10},{9,11},{10,... | collective-permute-start | bytes 626696 | tf_op jit(solution)/shard_map/expand/ppermute | solution.py:292
  77.4 5.9 %collective-permute-done.21.got_ref = bf16[48,2176]{1,0:T(8,128)(2,1)S(1)} collective-permute-done((bf16[48,2176]{1,0:T(8,128)(2,1)S(1)}, bf16[48,2176]{1,0:T(8,128)(2,1)S(1)}, u32[]{:S(2)}, u32[]{:S(2)}) %collective-permute-start.21) | collective-permute-done | bytes 208928 | tf_op jit(solution)/shard_map/expand/ppermute | solution.py:292
  83.5 1.3 %collective-permute-done.22.other_ref = bf16[48,1024]{1,0:T(8,128)(2,1)S(1)} collective-permute-done((bf16[48,1024]{1,0:T(8,128)(2,1)S(1)}, bf16[48,1024]{1,0:T(8,128)(2,1)S(1)}, u32[]{:S(2)}, u32[]{:S(2)}) %collective-permute-start.22) | collective-permute-done | bytes 98336 | tf_op jit(solution)/shard_map/contract/ppermute | solution.py:292
  84.8 1.0 %contract.2 = (bf16[48,896]{1,0:T(8,128)(2,1)S(1)}, bf16[48,896]{1,0:T(8,128)(2,1)S(1)}) custom-call(s32[3]{0:T(128)S(1)} %pad_add_fusion.bits_ref, bf16[48,1024]{1,0:T(8,128)(2,1)S(1)} %expand.6.mine_ref, bf16[48,1024]{1,0:T(8,128)(2,1)S(1)} %collective-permute-done.22.other_ref, bf16[1024,896]{1,0:T(8,128)(2,1)S(1)} %bitcast.14), custom_call_target="tpu_custom_call" | custom-call | flops 1176160768 | bytes 2203660 | tf_op jit(solution)/shard_map/contract/pallas_call | solution.py:28
  85.8 1.4 %collective-permute-done.23.got_ref = bf16[48,2176]{1,0:T(8,128)(2,1)S(1)} collective-permute-done((bf16[48,2176]{1,0:T(8,128)(2,1)S(1)}, bf16[48,2176]{1,0:T(8,128)(2,1)S(1)}, u32[]{:S(2)}, u32[]{:S(2)}) %collective-permute-start.23) | collective-permute-done | bytes 208928 | tf_op jit(solution)/shard_map/expand/ppermute | solution.py:292
  87.5 2.1 %collective-permute-start.25 = (bf16[48,896]{1,0:T(8,128)(2,1)S(1)}, bf16[48,896]{1,0:T(8,128)(2,1)S(1)}, u32[]{:S(2)}, u32[]{:S(2)}) collective-permute-start(bf16[48,896]{1,0:T(8,128)(2,1)S(1)} %get-tuple-element.82), channel_id=1, source_target_pairs={{0,8},{4,12},{8,0},{12,4},{1,9},{5,13},{9,1},{13,5},{2,10},{6,14},... | collective-permute-start | bytes 258056 | tf_op jit(solution)/shard_map/combine/ppermute | solution.py:299
  89.6 1.2 %collective-permute-start.26 = (bf16[48,896]{1,0:T(8,128)(2,1)S(1)}, bf16[48,896]{1,0:T(8,128)(2,1)S(1)}, u32[]{:S(2)}, u32[]{:S(2)}) collective-permute-start(bf16[48,896]{1,0:T(8,128)(2,1)S(1)} %get-tuple-element.83), channel_id=1, source_target_pairs={{0,4},{4,8},{8,12},{12,0},{1,5},{5,9},{9,13},{13,1},{2,6},{6,10},{... | collective-permute-start | bytes 258056 | tf_op jit(solution)/shard_map/combine/ppermute | solution.py:299
  90.7 1.0 contract.3
  91.8 2.7 %collective-permute-start.27 = (bf16[48,896]{1,0:T(8,128)(2,1)S(1)}, bf16[48,896]{1,0:T(8,128)(2,1)S(1)}, u32[]{:S(2)}, u32[]{:S(2)}) collective-permute-start(bf16[48,896]{1,0:T(8,128)(2,1)S(1)} %get-tuple-element.84), channel_id=1, source_target_pairs={{0,12},{4,0},{8,4},{12,8},{1,13},{5,1},{9,5},{13,9},{2,14},{6,2},{... | collective-permute-start | bytes 258056 | tf_op jit(solution)/shard_map/combine/ppermute | solution.py:299
  94.5 3.1 %collective-permute-done.25.r2 = bf16[48,896]{1,0:T(8,128)(2,1)S(1)} collective-permute-done((bf16[48,896]{1,0:T(8,128)(2,1)S(1)}, bf16[48,896]{1,0:T(8,128)(2,1)S(1)}, u32[]{:S(2)}, u32[]{:S(2)}) %collective-permute-start.25) | collective-permute-done | bytes 86048 | tf_op jit(solution)/shard_map/combine/ppermute | solution.py:299
  97.8 1.1 %collective-permute-done.27.r1 = bf16[48,896]{1,0:T(8,128)(2,1)S(1)} collective-permute-done((bf16[48,896]{1,0:T(8,128)(2,1)S(1)}, bf16[48,896]{1,0:T(8,128)(2,1)S(1)}, u32[]{:S(2)}, u32[]{:S(2)}) %collective-permute-start.27) | collective-permute-done | bytes 86048 | tf_op jit(solution)/shard_map/combine/ppermute | solution.py:299
  98.9 0.8 combine.3
  (46 shorter events, 3.4 us)
Async XLA Ops:
  0.9 11.5 %collective-permute-start.1 = (bf16[288,256]{1,0:T(8,128)(2,1)S(1)}, bf16[288,256]{1,0:T(8,128)(2,1)S(1)}, u32[]{:S(2)}, u32[]{:S(2)}) collective-permute-start(bf16[288,256]{1,0:T(8,128)(2,1)S(1)} %dynamic-slice_bitcast_fusion), channel_id=1, source_target_pairs={{0,4},{4,8},{8,12},{12,0},{1,5},{5,9},{9,13},{13,1},{2,6},{6,10},{... | collective-permute-start | bytes 442376 | tf_op jit(solution)/shard_map/gather_cache/ppermute | solution.py:299
  4.0 12.3 %collective-permute-start.3 = (bf16[288,256]{1,0:T(8,128)(2,1)S(1)}, bf16[288,256]{1,0:T(8,128)(2,1)S(1)}, u32[]{:S(2)}, u32[]{:S(2)}) collective-permute-start(bf16[288,256]{1,0:T(8,128)(2,1)S(1)} %dynamic-slice_bitcast_fusion), channel_id=1, source_target_pairs={{0,8},{4,12},{8,0},{12,4},{1,9},{5,13},{9,1},{13,5},{2,10},{6,14},... | collective-permute-start | bytes 442376 | tf_op jit(solution)/shard_map/gather_cache/ppermute | solution.py:299
  6.6 9.7 %collective-permute-start.5 = (bf16[288,256]{1,0:T(8,128)(2,1)S(1)}, bf16[288,256]{1,0:T(8,128)(2,1)S(1)}, u32[]{:S(2)}, u32[]{:S(2)}) collective-permute-start(bf16[288,256]{1,0:T(8,128)(2,1)S(1)} %dynamic-slice_bitcast_fusion), channel_id=1, source_target_pairs={{0,12},{4,0},{8,4},{12,8},{1,13},{5,1},{9,5},{13,9},{2,14},{6,2},{... | collective-permute-start | bytes 442376 | tf_op jit(solution)/shard_map/gather_cache/ppermute | solution.py:299
  7.9 3.6 %collective-permute-start = (s32[2,64]{1,0:T(2,128)}, s32[2,64]{1,0:T(2,128)S(1)}, u32[]{:S(2)}, u32[]{:S(2)}) collective-permute-start(s32[2,64]{1,0:T(2,128)} %bitcast.16), channel_id=1, source_target_pairs={{0,0},{1,4},{2,8},{3,12},{4,1},{5,5},{6,9},{7,13},{8,2},{9,6},{10,... | collective-permute-start | bytes 1544 | tf_op jit(solution)/shard_map/routing/ppermute | solution.py:296
  9.3 2.2 %copy-start.4 = (s32[64,2]{0,1:T(2,128)S(1)}, s32[64,2]{0,1:T(2,128)}, u32[]{:S(2)}) copy-start(s32[64,2]{0,1:T(2,128)} %param.24) | copy-start | bytes 1540
  9.3 2.2 %copy-start.5 = (f32[64,2]{0,1:T(2,128)S(1)}, f32[64,2]{0,1:T(2,128)}, u32[]{:S(2)}) copy-start(f32[64,2]{0,1:T(2,128)} %param.25) | copy-start | bytes 1540
  9.3 2.2 %copy-start.6 = (s32[64,1]{0,1:T(1,128)S(1)}, s32[64,1]{0,1:T(1,128)}, u32[]{:S(2)}) copy-start(s32[64,1]{0,1:T(1,128)} %param.16) | copy-start | bytes 772
  12.5 4.4 %collective-permute-start.2 = (bf16[288,256]{1,0:T(8,128)(2,1)S(1)}, bf16[288,256]{1,0:T(8,128)(2,1)S(1)}, u32[]{:S(2)}, u32[]{:S(2)}) collective-permute-start(bf16[288,256]{1,0:T(8,128)(2,1)S(1)} %collective-permute-done.1.refs_0_), channel_id=1, source_target_pairs={{0,1},{1,0},{2,3},{3,2},{4,5},{5,4},{6,7},{7,6},{8,9},{9,8},{10,11... | collective-permute-start | bytes 442376 | tf_op jit(solution)/shard_map/gather_cache/ppermute | solution.py:292
  16.3 1.4 %collective-permute-start.4 = (bf16[288,256]{1,0:T(8,128)(2,1)S(1)}, bf16[288,256]{1,0:T(8,128)(2,1)S(1)}, u32[]{:S(2)}, u32[]{:S(2)}) collective-permute-start(bf16[288,256]{1,0:T(8,128)(2,1)S(1)} %collective-permute-done.3.refs_2_), channel_id=1, source_target_pairs={{0,1},{1,0},{2,3},{3,2},{4,5},{5,4},{6,7},{7,6},{8,9},{9,8},{10,11... | collective-permute-start | bytes 442376 | tf_op jit(solution)/shard_map/gather_cache/ppermute | solution.py:292
  16.3 1.6 %collective-permute-start.6 = (bf16[288,256]{1,0:T(8,128)(2,1)S(1)}, bf16[288,256]{1,0:T(8,128)(2,1)S(1)}, u32[]{:S(2)}, u32[]{:S(2)}) collective-permute-start(bf16[288,256]{1,0:T(8,128)(2,1)S(1)} %collective-permute-done.5.refs_4_), channel_id=1, source_target_pairs={{0,1},{1,0},{2,3},{3,2},{4,5},{5,4},{6,7},{7,6},{8,9},{9,8},{10,11... | collective-permute-start | bytes 442376 | tf_op jit(solution)/shard_map/gather_cache/ppermute | solution.py:292
  21.3 16.9 %copy-start.8 = (bf16[64,896]{1,0:T(8,128)(2,1)S(1)}, bf16[64,896]{1,0:T(8,128)(2,1)}, u32[]{:S(2)}) copy-start(bf16[64,896]{1,0:T(8,128)(2,1)} %param.15) | copy-start | bytes 344068
  21.3 25.4 %copy-start = (bf16[2048,896]{1,0:T(8,128)(2,1)S(1)}, bf16[2048,896]{1,0:T(8,128)(2,1)}, u32[]{:S(2)}) copy-start(bf16[2048,896]{1,0:T(8,128)(2,1)} %w_ref.3) | copy-start | bytes 11010052
  21.3 12.3 %collective-permute-start.7 = (bf16[64,1024]{1,0:T(8,128)(2,1)S(1)}, bf16[64,1024]{1,0:T(8,128)(2,1)S(1)}, u32[]{:S(2)}, u32[]{:S(2)}) collective-permute-start(bf16[64,1024]{1,0:T(8,128)(2,1)S(1)} %attend.4.h0), channel_id=1, source_target_pairs={{0,8},{4,12},{8,0},{12,4},{1,9},{5,13},{9,1},{13,5},{2,10},{6,14},... | collective-permute-start | bytes 393224 | tf_op jit(solution)/shard_map/gather_heads/ppermute | solution.py:289
  27.0 9.3 %collective-permute-start.8 = (bf16[64,1024]{1,0:T(8,128)(2,1)S(1)}, bf16[64,1024]{1,0:T(8,128)(2,1)S(1)}, u32[]{:S(2)}, u32[]{:S(2)}) collective-permute-start(bf16[64,1024]{1,0:T(8,128)(2,1)S(1)} %attend.4.h0), channel_id=1, source_target_pairs={{0,4},{4,0},{8,12},{12,8},{1,5},{5,1},{9,13},{13,9},{2,6},{6,2},{1... | collective-permute-start | bytes 393224 | tf_op jit(solution)/shard_map/gather_heads/ppermute | solution.py:289
  30.1 9.2 %collective-permute-start.12 = (bf16[64,1024]{1,0:T(8,128)(2,1)S(1)}, bf16[64,1024]{1,0:T(8,128)(2,1)S(1)}, u32[]{:S(2)}, u32[]{:S(2)}) collective-permute-start(bf16[64,1024]{1,0:T(8,128)(2,1)S(1)} %attend.5.h0), channel_id=1, source_target_pairs={{0,8},{4,12},{8,0},{12,4},{1,9},{5,13},{9,1},{13,5},{2,10},{6,14},... | collective-permute-start | bytes 393224 | tf_op jit(solution)/shard_map/gather_heads/ppermute | solution.py:289
  36.2 6.4 %collective-permute-start.11 = (bf16[64,1024]{1,0:T(8,128)(2,1)S(1)}, bf16[64,1024]{1,0:T(8,128)(2,1)S(1)}, u32[]{:S(2)}, u32[]{:S(2)}) collective-permute-start(bf16[64,1024]{1,0:T(8,128)(2,1)S(1)} %attend.5.h0), channel_id=1, source_target_pairs={{0,4},{4,0},{8,12},{12,8},{1,5},{5,1},{9,13},{13,9},{2,6},{6,2},{1... | collective-permute-start | bytes 393224 | tf_op jit(solution)/shard_map/gather_heads/ppermute | solution.py:289
  36.2 10.5 %collective-permute-start.9 = (bf16[64,1024]{1,0:T(8,128)(2,1)S(1)}, bf16[64,1024]{1,0:T(8,128)(2,1)S(1)}, u32[]{:S(2)}, u32[]{:S(2)}) collective-permute-start(bf16[64,1024]{1,0:T(8,128)(2,1)S(1)} %collective-permute-done.7.h2), channel_id=1, source_target_pairs={{0,4},{4,0},{8,12},{12,8},{1,5},{5,1},{9,13},{13,9},{2,6},{6,2},{1... | collective-permute-start | bytes 393224 | tf_op jit(solution)/shard_map/gather_heads/ppermute | solution.py:289
  38.3 2.5 %collective-permute-start.10 = (bf16[64,896]{1,0:T(8,128)(2,1)S(1)}, bf16[64,896]{1,0:T(8,128)(2,1)S(1)}, u32[]{:S(2)}, u32[]{:S(2)}) collective-permute-start(bf16[64,896]{1,0:T(8,128)(2,1)S(1)} %copy-done.8), channel_id=1, source_target_pairs={{0,0},{1,4},{2,8},{3,12},{4,1},{5,5},{6,9},{7,13},{8,2},{9,6},{10,... | collective-permute-start | bytes 344072 | tf_op jit(solution)/shard_map/attend/ppermute | solution.py:296
  39.3 11.9 %collective-permute-start.13 = (bf16[64,1024]{1,0:T(8,128)(2,1)S(1)}, bf16[64,1024]{1,0:T(8,128)(2,1)S(1)}, u32[]{:S(2)}, u32[]{:S(2)}) collective-permute-start(bf16[64,1024]{1,0:T(8,128)(2,1)S(1)} %collective-permute-done.12.h2), channel_id=1, source_target_pairs={{0,4},{4,0},{8,12},{12,8},{1,5},{5,1},{9,13},{13,9},{2,6},{6,2},{1... | collective-permute-start | bytes 393224 | tf_op jit(solution)/shard_map/gather_heads/ppermute | solution.py:289
  52.6 1.6 %collective-permute-start.14 = (bf16[128,896]{1,0:T(8,128)(2,1)S(1)}, bf16[128,896]{1,0:T(8,128)(2,1)S(1)}, u32[]{:S(2)}, u32[]{:S(2)}) collective-permute-start(bf16[128,896]{1,0:T(8,128)(2,1)S(1)} %get-tuple-element.63), channel_id=1, source_target_pairs={{0,1},{1,0},{2,3},{3,2},{4,5},{5,4},{6,7},{7,6},{8,9},{9,8},{10,11... | collective-permute-start | bytes 688136 | tf_op jit(solution)/shard_map/project/ppermute | solution.py:292
  54.7 5.3 %collective-permute-start.15 = (bf16[64,896]{1,0:T(8,128)(2,1)S(1)}, bf16[64,896]{1,0:T(8,128)(2,1)S(1)}, u32[]{:S(2)}, u32[]{:S(2)}) collective-permute-start(bf16[64,896]{1,0:T(8,128)(2,1)S(1)} %get-tuple-element.65), channel_id=1, source_target_pairs={{0,2},{1,3},{2,0},{3,1},{4,6},{5,7},{6,4},{7,5},{8,10},{9,11},{10,... | collective-permute-start | bytes 344072 | tf_op jit(solution)/shard_map/project/ppermute | solution.py:292
  60.0 6.2 %copy-start.7 = (bf16[896]{0:T(1024)(128)(2,1)S(1)}, bf16[896]{0:T(1024)(128)(2,1)}, u32[]{:S(2)}) copy-start(bf16[896]{0:T(1024)(128)(2,1)} %param.20) | copy-start | bytes 5380
  60.0 10.3 %copy-start.1 = (bf16[1,896,1024]{2,1,0:T(8,128)(2,1)S(1)}, bf16[1,896,1024]{2,1,0:T(8,128)(2,1)}, u32[]{:S(2)}) copy-start(bf16[1,896,1024]{2,1,0:T(8,128)(2,1)} %param.21) | copy-start | bytes 5505028
  60.0 10.3 %copy-start.2 = (bf16[1,896,1024]{2,1,0:T(8,128)(2,1)S(1)}, bf16[1,896,1024]{2,1,0:T(8,128)(2,1)}, u32[]{:S(2)}) copy-start(bf16[1,896,1024]{2,1,0:T(8,128)(2,1)} %param.22) | copy-start | bytes 5505028
  60.3 10.0 %collective-permute-start.16 = (bf16[64,896]{1,0:T(8,128)(2,1)S(1)}, bf16[64,896]{1,0:T(8,128)(2,1)S(1)}, u32[]{:S(2)}, u32[]{:S(2)}) collective-permute-start(bf16[64,896]{1,0:T(8,128)(2,1)S(1)} %get-tuple-element.68), channel_id=1, source_target_pairs={{0,0},{1,4},{2,8},{3,12},{4,1},{5,5},{6,9},{7,13},{8,2},{9,6},{10,... | collective-permute-start | bytes 344072 | tf_op jit(solution)/shard_map/scatter_resid/ppermute | solution.py:296
  61.1 6.6 %collective-permute-start.17 = (bf16[48,896]{1,0:T(8,128)(2,1)S(1)}, bf16[48,896]{1,0:T(8,128)(2,1)S(1)}, u32[]{:S(2)}, u32[]{:S(2)}) collective-permute-start(bf16[48,896]{1,0:T(8,128)(2,1)S(1)} %get-tuple-element.69), channel_id=1, source_target_pairs={{0,8},{1,12},{2,0},{3,4},{4,9},{5,13},{6,1},{7,5},{8,10},{9,14},{1... | collective-permute-start | bytes 258056 | tf_op jit(solution)/shard_map/scatter_resid/ppermute | solution.py:296
  65.1 3.4 %collective-permute-start.18 = (bf16[48,896]{1,0:T(8,128)(2,1)S(1)}, bf16[48,896]{1,0:T(8,128)(2,1)S(1)}, u32[]{:S(2)}, u32[]{:S(2)}) collective-permute-start(bf16[48,896]{1,0:T(8,128)(2,1)S(1)} %get-tuple-element.70), channel_id=1, source_target_pairs={{0,12},{1,0},{2,4},{3,8},{4,13},{5,1},{6,5},{7,9},{8,14},{9,2},{10... | collective-permute-start | bytes 258056 | tf_op jit(solution)/shard_map/scatter_resid/ppermute | solution.py:296
  66.2 4.0 %collective-permute-start.19 = (bf16[48,896]{1,0:T(8,128)(2,1)S(1)}, bf16[48,896]{1,0:T(8,128)(2,1)S(1)}, u32[]{:S(2)}, u32[]{:S(2)}) collective-permute-start(bf16[48,896]{1,0:T(8,128)(2,1)S(1)} %get-tuple-element.71), channel_id=1, source_target_pairs={{0,4},{1,8},{2,12},{3,0},{4,5},{5,9},{6,13},{7,1},{8,6},{9,10},{10... | collective-permute-start | bytes 258056 | tf_op jit(solution)/shard_map/scatter_resid/ppermute | solution.py:296
  72.0 2.6 %collective-permute-start.20 = (bf16[96,2176]{1,0:T(8,128)(2,1)S(1)}, bf16[96,2176]{1,0:T(8,128)(2,1)S(1)}, u32[]{:S(2)}, u32[]{:S(2)}) collective-permute-start(bf16[96,2176]{1,0:T(8,128)(2,1)S(1)} %get-tuple-element.73), channel_id=1, source_target_pairs={{0,1},{1,0},{2,3},{3,2},{4,5},{5,4},{6,7},{7,6},{8,9},{9,8},{10,11... | collective-permute-start | bytes 1253384 | tf_op jit(solution)/shard_map/expand/ppermute | solution.py:292
  74.7 8.5 %collective-permute-start.21 = (bf16[48,2176]{1,0:T(8,128)(2,1)S(1)}, bf16[48,2176]{1,0:T(8,128)(2,1)S(1)}, u32[]{:S(2)}, u32[]{:S(2)}) collective-permute-start(bf16[48,2176]{1,0:T(8,128)(2,1)S(1)} %get-tuple-element.76), channel_id=1, source_target_pairs={{0,2},{1,3},{2,0},{3,1},{4,6},{5,7},{6,4},{7,5},{8,10},{9,11},{10,... | collective-permute-start | bytes 626696 | tf_op jit(solution)/shard_map/expand/ppermute | solution.py:292
  77.3 9.9 %collective-permute-start.23 = (bf16[48,2176]{1,0:T(8,128)(2,1)S(1)}, bf16[48,2176]{1,0:T(8,128)(2,1)S(1)}, u32[]{:S(2)}, u32[]{:S(2)}) collective-permute-start(bf16[48,2176]{1,0:T(8,128)(2,1)S(1)} %get-tuple-element.79), channel_id=1, source_target_pairs={{0,2},{1,3},{2,0},{3,1},{4,6},{5,7},{6,4},{7,5},{8,10},{9,11},{10,... | collective-permute-start | bytes 626696 | tf_op jit(solution)/shard_map/expand/ppermute | solution.py:292
  83.3 1.5 %copy-start.3 = (bf16[1,1024,896]{2,1,0:T(8,128)(2,1)S(1)}, bf16[1,1024,896]{2,1,0:T(8,128)(2,1)}, u32[]{:S(2)}) copy-start(bf16[1,1024,896]{2,1,0:T(8,128)(2,1)} %param.23) | copy-start | bytes 5505028
  83.4 1.4 %collective-permute-start.22 = (bf16[48,1024]{1,0:T(8,128)(2,1)S(1)}, bf16[48,1024]{1,0:T(8,128)(2,1)S(1)}, u32[]{:S(2)}, u32[]{:S(2)}) collective-permute-start(bf16[48,1024]{1,0:T(8,128)(2,1)S(1)} %expand.6.mine_ref), channel_id=1, source_target_pairs={{0,1},{1,0},{2,3},{3,2},{4,5},{5,4},{6,7},{7,6},{8,9},{9,8},{10,11... | collective-permute-start | bytes 294920 | tf_op jit(solution)/shard_map/contract/ppermute | solution.py:292
  87.4 3.3 %collective-permute-start.24 = (bf16[48,1024]{1,0:T(8,128)(2,1)S(1)}, bf16[48,1024]{1,0:T(8,128)(2,1)S(1)}, u32[]{:S(2)}, u32[]{:S(2)}) collective-permute-start(bf16[48,1024]{1,0:T(8,128)(2,1)S(1)} %expand.7.mine_ref), channel_id=1, source_target_pairs={{0,1},{1,0},{2,3},{3,2},{4,5},{5,4},{6,7},{7,6},{8,9},{9,8},{10,11... | collective-permute-start | bytes 294920 | tf_op jit(solution)/shard_map/contract/ppermute | solution.py:292
  87.5 10.0 %collective-permute-start.25 = (bf16[48,896]{1,0:T(8,128)(2,1)S(1)}, bf16[48,896]{1,0:T(8,128)(2,1)S(1)}, u32[]{:S(2)}, u32[]{:S(2)}) collective-permute-start(bf16[48,896]{1,0:T(8,128)(2,1)S(1)} %get-tuple-element.82), channel_id=1, source_target_pairs={{0,8},{4,12},{8,0},{12,4},{1,9},{5,13},{9,1},{13,5},{2,10},{6,14},... | collective-permute-start | bytes 258056 | tf_op jit(solution)/shard_map/combine/ppermute | solution.py:299
  89.6 8.0 %collective-permute-start.26 = (bf16[48,896]{1,0:T(8,128)(2,1)S(1)}, bf16[48,896]{1,0:T(8,128)(2,1)S(1)}, u32[]{:S(2)}, u32[]{:S(2)}) collective-permute-start(bf16[48,896]{1,0:T(8,128)(2,1)S(1)} %get-tuple-element.83), channel_id=1, source_target_pairs={{0,4},{4,8},{8,12},{12,0},{1,5},{5,9},{9,13},{13,1},{2,6},{6,10},{... | collective-permute-start | bytes 258056 | tf_op jit(solution)/shard_map/combine/ppermute | solution.py:299
  91.8 7.1 %collective-permute-start.27 = (bf16[48,896]{1,0:T(8,128)(2,1)S(1)}, bf16[48,896]{1,0:T(8,128)(2,1)S(1)}, u32[]{:S(2)}, u32[]{:S(2)}) collective-permute-start(bf16[48,896]{1,0:T(8,128)(2,1)S(1)} %get-tuple-element.84), channel_id=1, source_target_pairs={{0,12},{4,0},{8,4},{12,8},{1,13},{5,1},{9,5},{13,9},{2,14},{6,2},{... | collective-permute-start | bytes 258056 | tf_op jit(solution)/shard_map/combine/ppermute | solution.py:299
